TPU v7x, 512 devices: a whole 4x8x8 slice. The times are simulated.
512 devices in a mesh: lon: 32 (over z, x_hi, core), lat: 16 (over y, x_lo).
Axes of the slice: x: 4 (x_hi: 2, x_lo: 2; x = x_hi * 2 + x_lo), y: 8, z: 8, core: 2. Of those that a mesh axis runs over, the one named last changes fastest.
Arguments:
- tokens: bfloat16 [2, 192, 384, 192], P(None, 'lat', 'lon'), may hold values from -6 to 6
- cotangent: bfloat16 [2, 192, 384, 192], P(None, 'lat', 'lon'), may hold values from -6 to 6
- qkv_codes: int32 [192, 576], replicated, may hold values from -128 to 127
- proj_codes: int32 [192, 192], replicated, may hold values from -128 to 127
- up_codes: int32 [192, 768], replicated, may hold values from -128 to 127
- down_codes: int32 [768, 192], replicated, may hold values from -128 to 127
- bit_widths: int32 [4], replicated, may hold values from 6 to 8
- quant_scales: int32 [4], replicated, may hold values from 300 to 599
- bias_table: bfloat16 [32, 1, 6, 3312], P('lat'), may hold values from -4 to 302
- bias_index: int32 [20736], replicated, may hold values from 0 to 3311
- merge_weight: bfloat16 [768, 384], replicated, may hold values from -0.21875 to 0.21875
Outputs:
- merged: bfloat16 [2, 96, 192, 384], P(None, 'lat', 'lon')
- grad_tokens: bfloat16 [2, 192, 384, 192], P(None, 'lat', 'lon')
- grad_qkv: bfloat16 [192, 576], replicated
- grad_proj: bfloat16 [192, 192], replicated
- grad_up: bfloat16 [192, 768], replicated
- grad_down: bfloat16 [768, 192], replicated
All inputs are finite; a program needn't handle non-finite values.
Results may differ from a plain program's by a relative error of at most 0.024.
The roundings to bfloat16 on the way count: a program that leaves them out, or rounds other values in their place, can miss the bound.
Values may be sent and summed in bfloat16 or wider, within the bound.
No kernel may reach another device: no remote copies, remote signals or barrier semaphores. Data moves between devices by JAX's collectives and lax.ppermute only.
A program may use at most 128 MiB of HBM per device.

v0:
```python
import math

import jax
import jax.numpy as jnp
from jax import lax
from jax.sharding import PartitionSpec as P

C = 192
HEADS = 6
FF = 768
HEAD_DIM = 32
WLEV = 2
WLAT = 6
WLON = 12
LAT_PAD = 11
WTOK = 144


EPSILON = 1e-05
MASKED = -1000000000.0


def from_behind(x, axis, by):
    count = lax.axis_size(axis)
    pairs = [(i, i + by) for i in range(count) if 0 <= i + by < count]
    return lax.ppermute(x, axis, pairs)


def passed_along(block, axis, distance):
    devices = range(lax.axis_size(axis))
    route = [((i - distance) % len(devices), i) for i in devices]
    return lax.ppermute(block, axis, route)


def product(left, right):
    return jnp.dot(left, right, preferred_element_type=jnp.float32)


def crossed(left, right):
    return jnp.dot(left.T, right, preferred_element_type=jnp.float32)


def dequant(int_codes, bit_count, quant_scale, fan_in):
    largest = jnp.left_shift(jnp.ones((), jnp.int32), bit_count - 1) - 1
    clipped = jnp.clip(int_codes, -largest, largest).astype(jnp.float32)
    factor = math.sqrt(C / fan_in) / quant_scale.astype(jnp.float32)
    return (clipped * factor).astype(jnp.bfloat16)


def normalize(values):
    center = values - jnp.mean(values, axis=-1, keepdims=True)
    spread = jnp.mean(center * center, axis=-1, keepdims=True)
    return center * lax.rsqrt(spread + EPSILON)


def norm_back(source, upstream):
    pullback = jax.vjp(normalize, source.astype(jnp.float32))[1]
    return pullback(upstream.astype(jnp.float32))[0]


def gelu_back(pre_act, upstream):
    pullback = jax.vjp(jax.nn.gelu, pre_act)[1]
    return pullback(upstream.astype(jnp.float32))[0]


def allowed_table(lat_start, lat_limit, level_count, row_windows):
    position = jnp.arange(WTOK, dtype=jnp.int32)
    level_in = position // (WLAT * WLON)
    row_in = position // WLON % WLAT
    window_level = WLEV * jnp.arange(level_count // WLEV, dtype=jnp.int32)
    levels = (window_level[:, None] + level_in[None, :] + 1) % level_count
    group = (levels + 1) // 2
    same = group[:, :, None] == group[:, None, :]
    lat_rows = (
        lat_start + WLAT * jnp.arange(row_windows, dtype=jnp.int32)[:, None] + row_in[None, :]
    )
    key_ok = (lat_rows >= 0) & (lat_rows < lat_limit)
    allowed = same[:, None, :, :] & key_ok[None, :, None, :]
    return allowed.reshape(-1, WTOK, WTOK)


def window_terms(table_rows, bias_index, lat_start, lat_limit, level_count):
    row_windows = table_rows.shape[0]
    level_windows = level_count // WLEV
    gathered = table_rows[:, :, :, bias_index].astype(jnp.float32)
    gathered = gathered.reshape(row_windows, level_windows, HEADS, WTOK, WTOK).transpose(
        1, 0, 2, 3, 4
    )
    gathered = gathered.reshape(level_windows * row_windows, HEADS, WTOK, WTOK)
    return (gathered, allowed_table(lat_start, lat_limit, level_count, row_windows))


def to_windows(window_frame):
    level_count, row_count, col_count, feat_count = window_frame.shape
    rolled = jnp.roll(window_frame, -1, axis=0)
    pieces = rolled.reshape(
        level_count // WLEV, WLEV, row_count // WLAT, WLAT, col_count // WLON, WLON, feat_count
    )
    return pieces.transpose(0, 2, 4, 1, 3, 5, 6).reshape(-1, WTOK, feat_count)


def from_windows(windows, level_count, row_count, col_count):
    feat_count = windows.shape[-1]
    pieces = windows.reshape(
        level_count // WLEV, row_count // WLAT, col_count // WLON, WLEV, WLAT, WLON, feat_count
    )
    pieces = pieces.transpose(0, 3, 1, 4, 2, 5, 6).reshape(
        level_count, row_count, col_count, feat_count
    )
    return jnp.roll(pieces, 1, axis=0)


def attend(windows, bias_terms, allowed):
    window_count = windows.shape[0]
    group_count = bias_terms.shape[0]
    query_part, key_part, value_part = jnp.split(windows.astype(jnp.float32), 3, axis=-1)
    query_part = query_part.reshape(window_count, WTOK, HEADS, HEAD_DIM)
    key_part = key_part.reshape(window_count, WTOK, HEADS, HEAD_DIM)
    value_part = value_part.reshape(window_count, WTOK, HEADS, HEAD_DIM)
    scores = jnp.einsum("wqhd,wkhd->whqk", query_part, key_part) * HEAD_DIM ** (-0.5)
    scores = (
        scores.reshape(group_count, window_count // group_count, HEADS, WTOK, WTOK)
        + bias_terms[:, None]
    )
    scores = jnp.where(allowed[:, None, None], scores, MASKED)
    top_score = jnp.max(scores, axis=-1, keepdims=True)
    weights = jnp.exp(scores - top_score)
    weights = (weights / jnp.sum(weights, axis=-1, keepdims=True)).astype(jnp.bfloat16)
    weights = weights.reshape(window_count, HEADS, WTOK, WTOK)
    mixed = jnp.einsum("whqk,wkhd->wqhd", weights.astype(jnp.float32), value_part)
    return mixed.reshape(window_count, WTOK, C)


def merge_patches(final, merge_weight):
    level_count, row_count, col_count, feat_count = final.shape
    grouped = final.reshape(level_count, row_count // 2, 2, col_count // 2, 2, feat_count)
    grouped = grouped.transpose(0, 1, 3, 2, 4, 5).reshape(-1, 4 * feat_count)
    normed = normalize(grouped.astype(jnp.float32)).astype(jnp.bfloat16)
    merged = product(normed, merge_weight).astype(jnp.bfloat16)
    return merged.reshape(level_count, row_count // 2, col_count // 2, 2 * feat_count)


def pull_rim(source):
    lat_part = from_behind(source[:, -(WLAT // 2) :], "lat", 1)
    upper = jnp.concatenate([lat_part, source[:, : -(WLAT // 2)]], axis=1)
    lon_part = passed_along(upper[:, :, -(WLON // 2) :], "lon", 1)
    return jnp.concatenate([lon_part, upper[:, :, : -(WLON // 2)]], axis=2)


def push_rim(window_frame):
    lon_part = passed_along(window_frame[:, :, : WLON // 2], "lon", -1)
    upper = jnp.concatenate([window_frame[:, :, WLON // 2 :], lon_part], axis=2)
    lat_part = from_behind(upper[:, : WLAT // 2], "lat", -1)
    return jnp.concatenate([upper[:, WLAT // 2 :], lat_part], axis=1)


def after_attention(start_flat, heads_flat, d_out, w_proj, w_up, w_down):
    resid = (start_flat.astype(jnp.float32) + product(heads_flat, w_proj)).astype(jnp.bfloat16)
    normed_two = normalize(resid.astype(jnp.float32)).astype(jnp.bfloat16)
    pre_act = product(normed_two, w_up)
    hidden = jax.nn.gelu(pre_act).astype(jnp.bfloat16)
    final = resid.astype(jnp.float32) + product(hidden, w_down)
    down_total = crossed(hidden, d_out)
    d_hidden = product(d_out, w_down.T).astype(jnp.bfloat16)
    d_pre = gelu_back(pre_act, d_hidden).astype(jnp.bfloat16)
    up_total = crossed(normed_two, d_pre)
    d_normed_two = product(d_pre, w_up.T).astype(jnp.bfloat16)
    d_resid = (d_out.astype(jnp.float32) + norm_back(resid, d_normed_two)).astype(jnp.bfloat16)
    proj_total = crossed(heads_flat, d_resid)
    d_heads = product(d_resid, w_proj.T).astype(jnp.bfloat16)
    return (final, d_resid, d_heads, proj_total, up_total, down_total)


def per_device(
    tokens,
    cotangent,
    qkv_codes,
    proj_codes,
    up_codes,
    down_codes,
    bit_widths,
    quant_scales,
    bias_table,
    bias_index,
    merge_weight,
):
    level_count, row_count, col_count, feat_count = tokens.shape
    token_count = level_count * row_count * col_count
    grid_shape = (level_count, row_count, col_count)
    lat_limit = lax.axis_size("lat") * row_count - LAT_PAD
    lat_index = lax.axis_index("lat")
    lat_start = lat_index * row_count - WLAT // 2
    w_qkv = dequant(qkv_codes, bit_widths[0], quant_scales[0], C)
    w_proj = dequant(proj_codes, bit_widths[1], quant_scales[1], C)
    w_up = dequant(up_codes, bit_widths[2], quant_scales[2], C)
    w_down = dequant(down_codes, bit_widths[3], quant_scales[3], FF)
    bias_terms, allowed = window_terms(bias_table, bias_index, lat_start, lat_limit, level_count)

    def local_attend(windows):
        return attend(windows, bias_terms, allowed)

    row_ids = lat_index * row_count + jnp.arange(row_count, dtype=jnp.int32)
    row_mask = (row_ids < lat_limit)[None, :, None, None]
    start = jnp.where(row_mask, tokens, jnp.zeros_like(tokens))
    start_flat = start.reshape(token_count, feat_count)
    normed = normalize(start.astype(jnp.float32)).astype(jnp.bfloat16)
    own_qkv = (
        product(normed.reshape(token_count, feat_count), w_qkv)
        .astype(jnp.bfloat16)
        .reshape(grid_shape + (3 * feat_count,))
    )
    frame_qkv = pull_rim(own_qkv)
    heads_windows, pullback = jax.vjp(local_attend, to_windows(frame_qkv))
    heads_out = push_rim(
        from_windows(heads_windows.astype(jnp.bfloat16), level_count, row_count, col_count)
    )
    heads_flat = heads_out.reshape(token_count, feat_count)
    d_out = jnp.where(row_mask, cotangent, jnp.zeros_like(cotangent)).reshape(
        token_count, feat_count
    )
    final, d_resid, d_heads, proj_total, up_total, down_total = after_attention(
        start_flat, heads_flat, d_out, w_proj, w_up, w_down
    )
    frame_grad = pull_rim(d_heads.reshape(grid_shape + (feat_count,)))
    d_frame = from_windows(
        pullback(to_windows(frame_grad).astype(jnp.float32))[0], level_count, row_count, col_count
    )
    d_qkv = push_rim(d_frame).reshape(token_count, 3 * feat_count)
    qkv_total = crossed(normed.reshape(token_count, feat_count), d_qkv)
    d_normed = product(d_qkv, w_qkv.T).astype(jnp.bfloat16)
    grad_flat = d_resid.astype(jnp.float32) + norm_back(start_flat, d_normed)
    grad_tokens = jnp.where(row_mask, grad_flat.reshape(grid_shape + (feat_count,)), 0.0).astype(
        jnp.bfloat16
    )
    final_owned = jnp.where(row_mask, final.reshape(grid_shape + (feat_count,)), 0.0).astype(
        jnp.bfloat16
    )
    merged = merge_patches(final_owned, merge_weight)
    summed = lax.psum((qkv_total, proj_total, up_total, down_total), ("lon", "lat"))
    return (
        merged,
        grad_tokens,
        summed[0].astype(jnp.bfloat16),
        summed[1].astype(jnp.bfloat16),
        summed[2].astype(jnp.bfloat16),
        summed[3].astype(jnp.bfloat16),
    )


def solution(mesh):
    placed = (
        P(None, "lat", "lon", None),
        P(None, "lat", "lon", None),
        P(),
        P(),
        P(),
        P(),
        P(),
        P(),
        P("lat", None, None, None),
        P(),
        P(),
    )
    return jax.shard_map(
        per_device,
        mesh=mesh,
        in_specs=placed,
        out_specs=(P(None, "lat", "lon", None), P(None, "lat", "lon", None), P(), P(), P(), P()),
        check_vma=False,
    )
```

profile of v0, /device:TPU:1, one launch (start us, length us, event | category | flops | bytes accessed | tf_op | source)
XLA Modules:
  0.0 347.0 jit_solution(9052688700906485169)
XLA Ops:
  0.7 1.2 convert_reduce_fusion.1
  1.9 1.2 multiply_reduce_fusion
  3.2 1.1 multiply_convert_fusion.4
  4.4 1.4 fusion.69
  6.4 1.4 fusion.70
  8.5 1.4 convolution_convert_fusion.2
  10.0 4.0 %collective-permute-start = (bf16[2,3,12,576]{3,2,1,0:T(8,128)(2,1)S(1)}, bf16[2,3,12,576]{3,2,1,0:T(8,128)(2,1)S(1)}, u32[]{:S(2)}, u32[]{:S(2)}) collective-permute-start(bf16[2,3,12,576]{3,2,1,0:T(8,128)(2,1)S(1)} %slice.154), channel_id=1, source_target_pairs={{0,1},{1,2},{2,3},{3,4},{4,5},{5,6},{6,7},{7,8},{8,9},{9,10},{10,1... | collective-permute-start | bytes 248840 | tf_op jit(solution)/shard_map/ppermute | solution.py:26
  16.6 5.9 %collective-permute-start.1 = (bf16[2,12,6,576]{3,2,1,0:T(8,128)(2,1)}, bf16[2,12,6,576]{3,2,1,0:T(8,128)(2,1)}, u32[]{:S(2)}, u32[]{:S(2)}) collective-permute-start(bf16[2,12,6,576]{3,2,1,0:T(8,128)(2,1)} %fusion.33), channel_id=1, source_target_pairs={{496,0},{0,16},{16,32},{32,48},{48,64},{64,80},{80,96},{96,112},{1... | collective-permute-start | bytes 497672 | tf_op jit(solution)/shard_map/ppermute | solution.py:32
  23.9 3.6 %copy.35 = bf16[2,1,6,3312]{2,0,3,1:T(2,128)(2,1)S(1)} copy(bf16[2,1,6,3312]{3,0,2,1:T(2,128)(2,1)} %param.19) | data formatting | bytes 158976 | tf_op args[8]
  27.5 51.2 %gather_fusion = bf16[20736,2,6]{2,1,0:T(2,128)(2,1)} fusion(bf16[2,6,3312]{1,0,2:T(2,128)(2,1)S(1)} %bitcast.85, s32[21504]{0:T(1024)S(1)} %copy-done.24), kind=kCustom, calls=%fused_computation | custom fusion | bytes 1078272 | tf_op jit(solution)/shard_map/gather | solution.py:85
  78.8 11.4 %convert_element_type.254 = f32[20736,2,6]{2,1,0:T(2,128)} convert(bf16[20736,2,6]{2,1,0:T(2,128)(2,1)} %gather_fusion) | non-fusion elementwise | flops 248832 | bytes 1492992 | tf_op jit(solution)/shard_map/convert_element_type | solution.py:85
  90.2 31.1 %copy.37 = f32[2,6,144,144]{2,3,1,0:T(8,128)} copy(f32[2,6,144,144]{1,0,3,2:T(2,128)} %bitcast.84) | data formatting | bytes 1990656 | tf_op jit(solution)/shard_map/convert_element_type | solution.py:85
  127.1 1.1 fusion.29
  130.1 2.1 fusion.71
  133.2 2.0 convert_reduce_fusion
  135.2 1.7 copy.32
  136.9 1.9 fusion.9
  138.8 2.2 copy.39
  141.0 2.2 convert_element_type.208
  144.3 2.7 collective-permute-start.2
  147.0 1.3 multiply_divide_fusion
  148.3 3.4 collective-permute-done.2
  151.8 1.5 collective-permute-start.3
  153.3 3.4 collective-permute-done.3
  157.5 1.6 reshape.592
  159.1 1.4 fusion.72
  160.7 1.4 fusion.43
  163.0 1.4 fusion.55
  167.1 1.3 fusion.57
  168.4 1.2 convolution_add_fusion
  169.6 1.6 reshape.596
  171.2 1.4 slice.166
  172.7 5.6 %collective-permute-start.4 = (bf16[2,3,12,192]{3,2,1,0:T(8,128)(2,1)}, bf16[2,3,12,192]{3,2,1,0:T(8,128)(2,1)}, u32[]{:S(2)}, u32[]{:S(2)}) collective-permute-start(bf16[2,3,12,192]{3,2,1,0:T(8,128)(2,1)} %slice.166), channel_id=1, source_target_pairs={{0,1},{1,2},{2,3},{3,4},{4,5},{5,6},{6,7},{7,8},{8,9},{9,10},{10,1... | collective-permute-start | bytes 82952 | tf_op jit(solution)/shard_map/ppermute | solution.py:26
  178.3 1.7 reshape.593
  179.9 1.3 fusion.38
  184.1 1.5 fusion.41
  185.6 3.3 collective-permute-start.5
  189.6 1.4 div.157
  190.9 1.4 rsqrt.43
  192.3 1.9 reshape.603
  196.2 2.1 reshape.598
  198.3 2.1 copy.45
  200.4 1.7 fusion.3
  209.2 8.4 %collective-permute-start.6 = (bf16[2,12,6,576]{3,2,1,0:T(8,128)(2,1)S(1)}, bf16[2,12,6,576]{3,2,1,0:T(8,128)(2,1)S(1)}, u32[]{:S(2)}, u32[]{:S(2)}) collective-permute-start(bf16[2,12,6,576]{3,2,1,0:T(8,128)(2,1)S(1)} %get-tuple-element.34), channel_id=1, source_target_pairs={{16,0},{32,16},{48,32},{64,48},{80,64},{96,80},{112,96},{128,112},... | collective-permute-start | bytes 497672 | tf_op jit(solution)/shard_map/ppermute | solution.py:32
  218.8 1.3 collective-permute-start.7
  220.2 4.2 %collective-permute-done.7 = bf16[2,3,12,576]{3,2,1,0:T(8,128)(2,1)S(1)} collective-permute-done((bf16[2,3,12,576]{3,2,1,0:T(8,128)(2,1)S(1)}, bf16[2,3,12,576]{3,2,1,0:T(8,128)(2,1)S(1)}, u32[]{:S(2)}, u32[]{:S(2)}) %collective-permute-start.7) | collective-permute-done | bytes 82976 | tf_op jit(solution)/shard_map/ppermute | solution.py:26
  224.4 1.3 convolution_bitcast_fusion
  228.7 118.3 %all-reduce.2 = (bf16[192,576]{1,0:T(8,128)(2,1)}, bf16[192,192]{1,0:T(8,128)(2,1)}, bf16[192,768]{1,0:T(8,128)(2,1)}, bf16[768,192]{0,1:T(8,128)(2,1)}) all-reduce(f32[192,576]{1,0:T(8,128)S(1)} %copy-done.20, f32[192,192]{1,0:T(8,128)S(1)} %copy-done.16, ...), channel_id=1, replica_groups=mesh['lon'=32,'lat'=16] {'lon','lat'}, use_global_device_ids=true, to_apply=%region_15.16 | all-reduce | flops 442368 | bytes 2654208 | tf_op jit(solution)/shard_map/psum | solution.py:239
  (181 shorter events, 31.0 us)
Async XLA Ops:
  0.6 217.0 %copy-start = (bf16[768,384]{1,0:T(8,128)(2,1)S(1)}, bf16[768,384]{1,0:T(8,128)(2,1)}, u32[]{:S(2)}) copy-start(bf16[768,384]{1,0:T(8,128)(2,1)} %param.21) | copy-start | bytes 1769476
  0.6 13.5 %copy-start.32 = (s32[20736]{0:T(1024)S(1)}, s32[20736]{0:T(1024)}, u32[]{:S(2)}) copy-start(s32[20736]{0:T(1024)} %param.20) | copy-start | bytes 248836
  0.7 14.1 %copy-start.38 = (pred[12]{0:T(512)(128)(4,1)}, pred[12]{0:T(512)(128)(4,1)S(1)}, u32[]{:S(2)}) copy-start(pred[12]{0:T(512)(128)(4,1)S(1)} %add_compare_fusion.1) | copy-start | bytes 40
  1.9 12.9 %copy-start.3 = (bf16[2,12,12,192]{3,0,2,1:T(2,128)(2,1)S(1)}, bf16[2,12,12,192]{3,0,2,1:T(2,128)(2,1)}, u32[]{:S(2)}) copy-start(bf16[2,12,12,192]{3,0,2,1:T(2,128)(2,1)} %param.11) | copy-start | bytes 331780
  1.9 12.9 %copy-start.31 = (bf16[2,12,12,192]{3,0,2,1:T(2,128)(2,1)S(1)}, bf16[2,12,12,192]{3,0,2,1:T(2,128)(2,1)}, u32[]{:S(2)}) copy-start(bf16[2,12,12,192]{3,0,2,1:T(2,128)(2,1)} %param.12) | copy-start | bytes 331780
  1.9 21.4 %copy-start.29 = (f32[2,12,12]{2,1,0:T(8,128)}, f32[2,12,12]{2,1,0:T(8,128)S(1)}, u32[]{:S(2)}) copy-start(f32[2,12,12]{2,1,0:T(8,128)S(1)} %broadcast_multiply_fusion) | copy-start | bytes 3460
  3.2 10.8 %copy-start.35 = (f32[2,12,12]{2,1,0:T(8,128)}, f32[2,12,12]{2,1,0:T(8,128)S(1)}, u32[]{:S(2)}) copy-start(f32[2,12,12]{2,1,0:T(8,128)S(1)} %get-tuple-element.49) | copy-start | bytes 3460
  10.0 5.8 %collective-permute-start = (bf16[2,3,12,576]{3,2,1,0:T(8,128)(2,1)S(1)}, bf16[2,3,12,576]{3,2,1,0:T(8,128)(2,1)S(1)}, u32[]{:S(2)}, u32[]{:S(2)}) collective-permute-start(bf16[2,3,12,576]{3,2,1,0:T(8,128)(2,1)S(1)} %slice.154), channel_id=1, source_target_pairs={{0,1},{1,2},{2,3},{3,4},{4,5},{5,6},{6,7},{7,8},{8,9},{9,10},{10,1... | collective-permute-start | bytes 248840 | tf_op jit(solution)/shard_map/ppermute | solution.py:26
  14.9 12.6 %copy-start.24 = (s32[21504]{0:T(1024)S(1)}, s32[21504]{0:T(1024)}, u32[]{:S(2)}) copy-start(s32[21504]{0:T(1024)} %pad_clamp_fusion) | copy-start | bytes 258052
  15.8 63.0 %copy-start.21 = (bf16[2,3,12,576]{3,2,1,0:T(8,128)(2,1)}, bf16[2,3,12,576]{3,2,1,0:T(8,128)(2,1)S(1)}, u32[]{:S(2)}) copy-start(bf16[2,3,12,576]{3,2,1,0:T(8,128)(2,1)S(1)} %collective-permute-done) | copy-start | bytes 248836
  16.6 110.5 %collective-permute-start.1 = (bf16[2,12,6,576]{3,2,1,0:T(8,128)(2,1)}, bf16[2,12,6,576]{3,2,1,0:T(8,128)(2,1)}, u32[]{:S(2)}, u32[]{:S(2)}) collective-permute-start(bf16[2,12,6,576]{3,2,1,0:T(8,128)(2,1)} %fusion.33), channel_id=1, source_target_pairs={{496,0},{0,16},{16,32},{32,48},{48,64},{64,80},{80,96},{96,112},{1... | collective-permute-start | bytes 497672 | tf_op jit(solution)/shard_map/ppermute | solution.py:32
  90.2 36.9 %copy-start.22 = (bf16[2,3,12,576]{3,2,1,0:T(8,128)(2,1)S(1)}, bf16[2,3,12,576]{3,2,1,0:T(8,128)(2,1)}, u32[]{:S(2)}) copy-start(bf16[2,3,12,576]{3,2,1,0:T(8,128)(2,1)} %copy-done.21) | copy-start | bytes 248836
  128.3 1.8 copy-start.25
  129.9 2.3 copy-start.12
  130.1 2.2 copy-start.14
  144.3 7.4 %collective-permute-start.2 = (bf16[2,12,6,192]{3,2,1,0:T(8,128)(2,1)S(1)}, bf16[2,12,6,192]{3,2,1,0:T(8,128)(2,1)S(1)}, u32[]{:S(2)}, u32[]{:S(2)}) collective-permute-start(bf16[2,12,6,192]{3,2,1,0:T(8,128)(2,1)S(1)} %get-tuple-element.45), channel_id=1, source_target_pairs={{16,0},{32,16},{48,32},{64,48},{80,64},{96,80},{112,96},{128,112},... | collective-permute-start | bytes 165896 | tf_op jit(solution)/shard_map/ppermute | solution.py:32
  151.8 5.0 %collective-permute-start.3 = (bf16[2,3,12,192]{3,2,1,0:T(8,128)(2,1)S(1)}, bf16[2,3,12,192]{3,2,1,0:T(8,128)(2,1)S(1)}, u32[]{:S(2)}, u32[]{:S(2)}) collective-permute-start(bf16[2,3,12,192]{3,2,1,0:T(8,128)(2,1)S(1)} %pad_maximum_fusion.9), channel_id=1, source_target_pairs={{1,0},{2,1},{3,2},{4,3},{5,4},{6,5},{7,6},{8,7},{9,8},{10,9},{11,1... | collective-permute-start | bytes 82952 | tf_op jit(solution)/shard_map/ppermute | solution.py:26
  159.1 3.1 copy-start.19
  159.1 3.1 copy-start.43
  162.2 2.2 copy-start.1
  164.4 1.9 copy-start.17
  165.3 0.9 copy-start.5
  172.7 10.8 %collective-permute-start.4 = (bf16[2,3,12,192]{3,2,1,0:T(8,128)(2,1)}, bf16[2,3,12,192]{3,2,1,0:T(8,128)(2,1)}, u32[]{:S(2)}, u32[]{:S(2)}) collective-permute-start(bf16[2,3,12,192]{3,2,1,0:T(8,128)(2,1)} %slice.166), channel_id=1, source_target_pairs={{0,1},{1,2},{2,3},{3,4},{4,5},{5,6},{6,7},{7,8},{8,9},{9,10},{10,1... | collective-permute-start | bytes 82952 | tf_op jit(solution)/shard_map/ppermute | solution.py:26
  181.3 4.4 %copy-start.33 = (f32[2,6,6]{2,1,0:T(8,128)}, f32[2,6,6]{2,1,0:T(8,128)S(1)}, u32[]{:S(2)}) copy-start(f32[2,6,6]{2,1,0:T(8,128)S(1)} %broadcast_multiply_fusion.1) | copy-start | bytes 868
  185.6 8.6 %collective-permute-start.5 = (bf16[2,12,6,192]{3,2,1,0:T(8,128)(2,1)}, bf16[2,12,6,192]{3,2,1,0:T(8,128)(2,1)}, u32[]{:S(2)}, u32[]{:S(2)}) collective-permute-start(bf16[2,12,6,192]{3,2,1,0:T(8,128)(2,1)} %fusion.41), channel_id=1, source_target_pairs={{496,0},{0,16},{16,32},{32,48},{48,64},{64,80},{80,96},{96,112},{1... | collective-permute-start | bytes 165896 | tf_op jit(solution)/shard_map/ppermute | solution.py:32
  200.4 1.7 copy-start.28
  202.1 0.9 copy-start.15
  202.1 1.1 copy-start.23
  202.1 1.1 copy-start.26
  203.2 0.9 copy-start.13
  204.1 0.9 copy-start.8
  208.1 9.5 %copy-start.11 = (f32[72,768]{1,0:T(8,128)S(1)}, f32[72,768]{1,0:T(8,128)}, u32[]{:S(2)}) copy-start(f32[72,768]{1,0:T(8,128)} %reshape.603) | copy-start | bytes 663556
  208.1 9.5 %copy-start.41 = (f32[72]{0:T(128)S(1)}, f32[72]{0:T(128)}, u32[]{:S(2)}) copy-start(f32[72]{0:T(128)} %div.157) | copy-start | bytes 868
  208.1 9.5 %copy-start.42 = (f32[72]{0:T(128)S(1)}, f32[72]{0:T(128)}, u32[]{:S(2)}) copy-start(f32[72]{0:T(128)} %rsqrt.43) | copy-start | bytes 868
  209.0 15.4 %copy-start.4 = (bf16[2,12,12,192]{3,0,2,1:T(2,128)(2,1)S(1)}, bf16[2,12,12,192]{3,0,2,1:T(2,128)(2,1)}, u32[]{:S(2)}) copy-start(bf16[2,12,12,192]{3,0,2,1:T(2,128)(2,1)} %param.11) | copy-start | bytes 331780
  209.0 15.3 %copy-start.30 = (f32[2,12,12]{2,1,0:T(8,128)S(1)}, f32[2,12,12]{2,1,0:T(8,128)}, u32[]{:S(2)}) copy-start(f32[2,12,12]{2,1,0:T(8,128)} %copy-done.29) | copy-start | bytes 3460
  209.1 15.3 %copy-start.36 = (f32[2,12,12]{2,1,0:T(8,128)S(1)}, f32[2,12,12]{2,1,0:T(8,128)}, u32[]{:S(2)}) copy-start(f32[2,12,12]{2,1,0:T(8,128)} %copy-done.35) | copy-start | bytes 3460
  209.1 15.3 %copy-start.39 = (pred[12]{0:T(512)(128)(4,1)S(1)}, pred[12]{0:T(512)(128)(4,1)}, u32[]{:S(2)}) copy-start(pred[12]{0:T(512)(128)(4,1)} %copy-done.38) | copy-start | bytes 40
  209.2 9.5 %collective-permute-start.6 = (bf16[2,12,6,576]{3,2,1,0:T(8,128)(2,1)S(1)}, bf16[2,12,6,576]{3,2,1,0:T(8,128)(2,1)S(1)}, u32[]{:S(2)}, u32[]{:S(2)}) collective-permute-start(bf16[2,12,6,576]{3,2,1,0:T(8,128)(2,1)S(1)} %get-tuple-element.34), channel_id=1, source_target_pairs={{16,0},{32,16},{48,32},{64,48},{80,64},{96,80},{112,96},{128,112},... | collective-permute-start | bytes 497672 | tf_op jit(solution)/shard_map/ppermute | solution.py:32
  218.8 5.6 %collective-permute-start.7 = (bf16[2,3,12,576]{3,2,1,0:T(8,128)(2,1)S(1)}, bf16[2,3,12,576]{3,2,1,0:T(8,128)(2,1)S(1)}, u32[]{:S(2)}, u32[]{:S(2)}) collective-permute-start(bf16[2,3,12,576]{3,2,1,0:T(8,128)(2,1)S(1)} %pad_maximum_fusion.7), channel_id=1, source_target_pairs={{1,0},{2,1},{3,2},{4,3},{5,4},{6,5},{7,6},{8,7},{9,8},{10,9},{11,1... | collective-permute-start | bytes 248840 | tf_op jit(solution)/shard_map/ppermute | solution.py:26
  225.7 1.0 copy-start.7
  225.7 1.0 copy-start.37
  225.7 1.5 copy-start.40
  225.8 1.7 copy-start.6
  226.8 1.9 copy-start.2
  226.8 1.9 copy-start.16
  226.8 1.9 copy-start.18
  227.2 1.4 copy-start.20
  (4 other events, 2.9 us)
where the time goes:
time: 349 us; the launch traced here: 347 us
  local copies, waits for them, and re-layouts  125 us (36%)
  blocking collectives  118 us (34%)
  starting transfers between devices  32.7 us (9%)
  other arithmetic  32.3 us (9%)
  matrix products  20.3 us (6%)
  waiting for transfers between devices  11.8 us (3%)
  between operations  6.75 us (2%)
    psum x1, blocking collectives, per_device(): lax.psum((qkv_total, proj_total, up_total, down_total), ('lon', 'lat'))  118 us
    gather x1, local copies, waits for them, and re-layouts, window_terms(): gathered = table_rows[:, :, :, bias_index].astype(jnp.float32)  51.2 us
    convert_element_type x1, local copies, waits for them, and re-layouts, window_terms(): gathered = table_rows[:, :, :, bias_index].astype(jnp.float32)  31.1 us
    ppermute x4, starting transfers between devices, passed_along(): return lax.ppermute(block, axis, route)  20.4 us
    ppermute x4, starting transfers between devices, from_behind(): return lax.ppermute(x, axis, pairs)  12.3 us
    convert_element_type x1, other arithmetic, window_terms(): gathered = table_rows[:, :, :, bias_index].astype(jnp.float32)  11.4 us
    unnamed x91, local copies, waits for them, and re-layouts  8.48 us
    ppermute x4, waiting for transfers between devices, from_behind(): return lax.ppermute(x, axis, pairs)  8.37 us
  transfers between devices with their start and end apart: 8, of which 5 were waited for; matrix products, arithmetic and copies ran while one was open for 33% of the time, Pallas kernels for 0%

commit v1 on v0

v1 whole, which is shorter than its diff:
```python
import math

import jax
import jax.numpy as jnp
from jax import lax
from jax.experimental import pallas as pl
from jax.experimental.pallas import tpu as pltpu
from jax.sharding import Mesh
from jax.sharding import PartitionSpec as P

C = 192
HEADS = 6
FF = 768
HEAD_DIM = 32
WLAT = 6
WLON = 12
LAT_PAD = 11
WTOK = 144
POS = 3312

ROWS = 12
COLS = 12
LEVS = 2
OFF = WLAT // 2
HALF = WLON // 2
SUB = 8
FRAME = LEVS * ROWS * 2 * SUB
BLOCK = FRAME // 4
STACK = HEADS * BLOCK
CHUNKS = -(-POS // 128)

EPSILON = 1e-05
MASKED = -1000000000.0
F32 = jnp.float32
BF16 = jnp.bfloat16
VMEM_LIMIT = 56 * 1024 * 1024

LAT = ("y", "xl")
LON = ("z", "xh", "c")
NEAR = ("xh", "c", "xl")
FAR = ("y", "z")


def iota(shape, dim):
    return lax.broadcasted_iota(jnp.int32, shape, dim)


def product(left, right):
    return lax.dot_general(left, right, (((1,), (0,)), ((), ())), preferred_element_type=F32)


def across(left, right):
    return lax.dot_general(left, right, (((1,), (1,)), ((), ())), preferred_element_type=F32)


def crossed(left, right):
    return lax.dot_general(left, right, (((0,), (0,)), ((), ())), preferred_element_type=F32)


def pack_kernel(tok_ref, cot_ref, own_ref, lat_ref, lon_ref, diag_ref, wide):
    wide[...] = jnp.zeros_like(wide)
    wide[:, :, 0:COLS, :] = jnp.concatenate(
        [tok_ref[...].astype(F32), cot_ref[...].astype(F32)], axis=-1
    )
    left = wide[:, :, 0:SUB, :]
    right = wide[:, :, HALF : HALF + SUB, :]

    def flat(piece):
        return piece.reshape(-1, 2 * C).astype(BF16)

    own_ref[...] = flat(left[:, : ROWS - OFF])
    lat_ref[...] = flat(left[:, ROWS - OFF :])
    lon_ref[...] = flat(right[:, : ROWS - OFF])
    diag_ref[...] = flat(right[:, ROWS - OFF :])


def prep_kernel(
    lat_ref,
    lim_ref,
    fac_ref,
    idx_ref,
    tab_ref,
    cq_ref,
    cp_ref,
    cu_ref,
    cd_ref,
    wq_ref,
    wp_ref,
    wu_ref,
    wd_ref,
    bias_ref,
    rows,
):
    def dequant(codes, layer):
        limit = lim_ref[layer]
        clipped = jnp.minimum(jnp.maximum(codes, -limit), limit).astype(F32)
        return clipped * fac_ref[layer]

    full = dequant(cq_ref[...], 0)
    for part in range(3):
        wq_ref[part] = full[:, part * C : (part + 1) * C].astype(BF16)
    wp_ref[...] = dequant(cp_ref[...], 1).astype(BF16)
    wu_ref[...] = dequant(cu_ref[...], 2).astype(BF16)
    wd_ref[...] = dequant(cd_ref[...], 3).astype(BF16)

    for win in range(2):
        table = tab_ref[win, 0].astype(F32)
        for chunk in range(CHUNKS):
            width = min(128, POS - chunk * 128)
            rows[chunk, win * SUB : win * SUB + HEADS, 0:width] = table[
                :, chunk * 128 : chunk * 128 + width
            ]

    index = idx_ref[...]
    high = lax.shift_right_logical(index, 7).astype(F32).astype(BF16)
    low = jnp.bitwise_and(index, 127).astype(F32).astype(BF16)

    def place(where):
        sub = jnp.bitwise_and(where, SUB - 1)
        token = (where >> 4) * WLON + jnp.bitwise_and(where >> 3, 1) * HALF + sub
        return jnp.where((sub < HALF) & (where < BLOCK), token, -1000)

    key = iota((BLOCK, 128), 1)
    for lev in range(LEVS):
        base = (1 - lev) * (WTOK // 2)
        pick_q = (iota((BLOCK, WTOK), 1) == place(iota((BLOCK, WTOK), 0)) + base).astype(F32)
        pick_k = (iota((WTOK, 128), 0) == place(iota((WTOK, 128), 1)) + base).astype(F32)
        pick_q = pick_q.astype(BF16)
        pick_k = pick_k.astype(BF16)
        hi = product(product(pick_q, high).astype(BF16), pick_k).astype(jnp.int32)
        lo = product(product(pick_q, low).astype(BF16), pick_k).astype(jnp.int32)
        for win in range(2):
            row = lat_ref[0] * ROWS - OFF + win * WLAT + (key >> 4)
            usable = (row >= 0) & (row < lat_ref[1])
            usable = usable & (jnp.bitwise_and(key, SUB - 1) < HALF) & (key < BLOCK)

            def one_head(head, carry):
                found = jnp.zeros((BLOCK, 128), F32)
                for chunk in range(CHUNKS):
                    line = rows[chunk, pl.ds(win * SUB + head, 1), :]
                    taken = jnp.take_along_axis(
                        jnp.broadcast_to(line, (BLOCK, 128)), lo, axis=1
                    )
                    found = jnp.where(hi == chunk, taken, found)
                found = jnp.where(usable, found, MASKED)
                at = pl.multiple_of(head * BLOCK, BLOCK)
                bias_ref[lev * 2 + win, pl.ds(at, BLOCK), :] = found.astype(BF16)
                return carry

            lax.fori_loop(0, HEADS, one_head, 0)


def unit(values):
    center = values - jnp.mean(values, axis=-1, keepdims=True)
    spread = jnp.mean(center * center, axis=-1, keepdims=True)
    scale = lax.rsqrt(spread + EPSILON)
    return center * scale, scale


def unit_back(normal, scale, upstream):
    level = jnp.mean(upstream, axis=-1, keepdims=True)
    along = jnp.mean(upstream * normal, axis=-1, keepdims=True)
    return scale * (upstream - level - normal * along)


def main_kernel(
    lat_ref,
    own_ref,
    lat_part_ref,
    lon_part_ref,
    diag_part_ref,
    wq_ref,
    wp_ref,
    wu_ref,
    wd_ref,
    bias_ref,
    own_out,
    lat_out,
    lon_out,
    diag_out,
    sums_ref,
    frame,
):
    below = ROWS - OFF

    def piece(ref, rows):
        return ref[...].astype(F32).reshape(LEVS, rows, SUB, 2 * C)

    frame[:, OFF:, 1] = piece(own_ref, below)
    frame[:, :OFF, 1] = piece(lat_part_ref, OFF)
    frame[:, OFF:, 0] = piece(lon_part_ref, below)
    frame[:, :OFF, 0] = piece(diag_part_ref, OFF)
    both = frame[...].reshape(FRAME, 2 * C)

    place = iota((FRAME, C), 0)
    row = lat_ref[0] * ROWS - OFF + (place >> 4) - jnp.where(place >= FRAME // 2, ROWS, 0)
    valid = (row >= 0) & (row < lat_ref[1]) & (jnp.bitwise_and(place, SUB - 1) < HALF)
    start = jnp.where(valid, both[:, :C], 0.0)
    d_out = jnp.where(valid, both[:, C:], 0.0)
    d_out_low = d_out.astype(BF16)

    normal, scale = unit(start)
    normed = normal.astype(BF16)
    query = product(normed, wq_ref[0]).astype(BF16)
    key = product(normed, wq_ref[1]).astype(BF16)
    value = product(normed, wq_ref[2]).astype(BF16)

    lane_head = iota((HEADS, 1, C), 2) >> 5
    head_mask = lane_head == iota((HEADS, 1, C), 0)
    mask_low = head_mask.astype(F32).astype(BF16)
    mask_full = head_mask.astype(F32)

    def spread_heads(block):
        return (block[None] * mask_low).reshape(STACK, C)

    def join_heads(stacked):
        return jnp.sum(stacked.reshape(HEADS, BLOCK, C) * mask_full, axis=0)

    saved = []
    heads_parts = []
    for block in range(4):
        at = slice(block * BLOCK, (block + 1) * BLOCK)
        q_stack = spread_heads(query[at])
        scores = across(q_stack, key[at]) * HEAD_DIM ** (-0.5)
        scores = scores + bias_ref[block][:, :BLOCK].astype(F32)
        weights = jnp.exp(scores - jnp.max(scores, axis=-1, keepdims=True))
        weights = weights / jnp.sum(weights, axis=-1, keepdims=True)
        weights_low = weights.astype(BF16)
        heads_parts.append(join_heads(product(weights_low, value[at])))
        saved.append((q_stack, weights, weights_low))
    heads = jnp.concatenate(heads_parts, axis=0).astype(BF16)

    resid = (start + product(heads, wp_ref[...])).astype(BF16).astype(F32)
    normal_two, scale_two = unit(resid)
    normed_two = normal_two.astype(BF16)
    pre_act = product(normed_two, wu_ref[...])
    inner = math.sqrt(2 / math.pi)
    square = pre_act * pre_act
    bend = jnp.tanh(inner * (pre_act + 0.044715 * (square * pre_act)))
    half = 0.5 * (1.0 + bend)
    hidden = (pre_act * half).astype(BF16)
    slope = half + 0.5 * pre_act * (1.0 - bend * bend) * (
        inner * (1.0 + (3 * 0.044715) * square)
    )
    final = jnp.where(valid, resid + product(hidden, wd_ref[...]), 0.0)

    d_hidden = across(d_out_low, wd_ref[...]).astype(BF16).astype(F32)
    d_pre = (slope * d_hidden).astype(BF16)
    d_normed_two = across(d_pre, wu_ref[...]).astype(BF16).astype(F32)
    d_resid = (d_out + unit_back(normal_two, scale_two, d_normed_two)).astype(BF16)
    d_heads = across(d_resid, wp_ref[...]).astype(BF16)

    dq_parts = []
    dk_parts = []
    dv_parts = []
    for block in range(4):
        at = slice(block * BLOCK, (block + 1) * BLOCK)
        q_stack, weights, weights_low = saved[block]
        d_stack = spread_heads(d_heads[at])
        d_weights = across(d_stack, value[at]).astype(BF16).astype(F32)
        dv_parts.append(crossed(weights_low, d_stack))
        inside = jnp.sum(weights * d_weights, axis=-1, keepdims=True)
        d_scores = (weights * (d_weights - inside) * HEAD_DIM ** (-0.5)).astype(BF16)
        dq_parts.append(join_heads(product(d_scores, key[at])))
        dk_parts.append(crossed(d_scores, q_stack))
    d_query = jnp.concatenate(dq_parts, axis=0).astype(BF16)
    d_key = jnp.concatenate(dk_parts, axis=0).astype(BF16)
    d_value = jnp.concatenate(dv_parts, axis=0).astype(BF16)

    d_normed = across(d_query, wq_ref[0]) + across(d_key, wq_ref[1]) + across(d_value, wq_ref[2])
    d_normed = d_normed.astype(BF16).astype(F32)
    grad = jnp.where(valid, d_resid.astype(F32) + unit_back(normal, scale, d_normed), 0.0)

    result = jnp.concatenate([final, grad], axis=-1).reshape(LEVS, ROWS, 2, SUB, 2 * C)

    def flat(part):
        return part.reshape(-1, 2 * C).astype(BF16)

    own_out[...] = flat(result[:, OFF:, 1])
    lat_out[...] = flat(result[:, :OFF, 1])
    lon_out[...] = flat(result[:, OFF:, 0])
    diag_out[...] = flat(result[:, :OFF, 0])

    small = [
        crossed(normed, d_query),
        crossed(normed, d_key),
        crossed(normed, d_value),
        crossed(heads, d_resid),
    ]
    tiles = [total[:, :128] for total in small]
    tiles += [
        jnp.concatenate([small[i][:, 128:], small[i + 1][:, 128:]], axis=-1) for i in (0, 2)
    ]
    for wide in (crossed(normed_two, d_pre), crossed(d_out_low, hidden)):
        tiles += [wide[:, i * 128 : (i + 1) * 128] for i in range(6)]
    for i, tile in enumerate(tiles):
        sums_ref[i * C : (i + 1) * C, :] = tile.astype(BF16)


def spread_kernel(sums_ref, qkv_ref, proj_ref, up_ref, down_ref):
    def tile(i):
        return sums_ref[i * C : (i + 1) * C, :].astype(F32)

    ends = [tile(4)[:, :64], tile(4)[:, 64:], tile(5)[:, :64], tile(5)[:, 64:]]
    small = [jnp.concatenate([tile(i), ends[i]], axis=-1) for i in range(4)]
    qkv_ref[...] = jnp.concatenate(small[:3], axis=-1).astype(BF16)
    proj_ref[...] = small[3].astype(BF16)
    for i in range(6):
        up_ref[:, i * 128 : (i + 1) * 128] = sums_ref[(6 + i) * C : (7 + i) * C, :]
        down_ref[i * 128 : (i + 1) * 128, :] = tile(12 + i).T.astype(BF16)


def finish_kernel(
    own_ref, lat_ref, lon_ref, diag_ref, weight_ref, merged_ref, grad_ref, frame
):
    above = ROWS - OFF

    def piece(ref, rows):
        return ref[...].astype(F32).reshape(LEVS, rows, SUB, 2 * C)

    frame[:, :above, 0] = piece(own_ref, above)
    frame[:, above:, 0] = piece(lat_ref, OFF)
    frame[:, :above, 1] = piece(lon_ref, above)
    frame[:, above:, 1] = piece(diag_ref, OFF)
    both = frame[...].reshape(FRAME, 2 * C)
    final = both[:, :C].astype(BF16)
    grad = both[:, C:].astype(BF16)

    def source(col):
        return jnp.where(col >= HALF, col + (SUB - HALF), col)

    to = iota((FRAME, FRAME), 0)
    col = jnp.bitwise_and(to, 15)
    pick = (iota((FRAME, FRAME), 1) == to - col + source(col)) & (col < COLS)
    moved = product(pick.astype(F32).astype(BF16), grad).reshape(LEVS, ROWS, 16, C)
    grad_ref[...] = moved[:, :, :COLS, :].astype(BF16)

    count = LEVS * (ROWS // 2) * SUB
    to = iota((count, FRAME), 0)
    lev = jnp.where(to >= count // 2, 1, 0)
    pair = (to >> 3) - lev * (ROWS // 2)
    parts = []
    for down in range(2):
        for right in range(2):
            col = 2 * jnp.bitwise_and(to, SUB - 1) + right
            wanted = lev * (FRAME // 2) + (2 * pair + down) * 16 + source(col)
            pick = (iota((count, FRAME), 1) == wanted) & (col < COLS)
            parts.append(product(pick.astype(F32).astype(BF16), final))
    width = 4 * C
    mean = sum(jnp.sum(part, axis=-1, keepdims=True) for part in parts) / width
    centers = [part - mean for part in parts]
    spread = sum(jnp.sum(part * part, axis=-1, keepdims=True) for part in centers) / width
    scale = lax.rsqrt(spread + EPSILON)
    total = jnp.zeros((count, 2 * C), F32)
    for i, part in enumerate(centers):
        total = total + product((part * scale).astype(BF16), weight_ref[i * C : (i + 1) * C, :])
    merged_ref[...] = total.reshape(LEVS, ROWS // 2, SUB, 2 * C)[:, :, :HALF, :].astype(BF16)


def call(kernel, outs, args, scratch=(), scalars=0, flops=0):
    vmem = pl.BlockSpec(memory_space=pltpu.VMEM)
    smem = pl.BlockSpec(memory_space=pltpu.SMEM)
    moved = sum(math.prod(a.shape) * a.dtype.itemsize for a in args)
    moved += sum(math.prod(s) * jnp.dtype(t).itemsize for s, t in outs)
    return pl.pallas_call(
        kernel,
        out_shape=[jax.ShapeDtypeStruct(s, t) for s, t in outs],
        in_specs=[smem] * scalars + [vmem] * (len(args) - scalars),
        out_specs=[vmem] * len(outs),
        scratch_shapes=list(scratch),
        compiler_params=pltpu.CompilerParams(vmem_limit_bytes=VMEM_LIMIT),
        cost_estimate=pl.CostEstimate(flops=flops, bytes_accessed=moved, transcendentals=0),
    )(*args)


def shifted(block, lat_step, lon_step):
    rows = lax.axis_size(LAT)
    cols = lax.axis_size(LON)
    if lat_step and lon_step:
        route = [
            (col * rows + row, (col + lon_step) % cols * rows + row + lat_step)
            for col in range(cols)
            for row in range(rows)
            if 0 <= row + lat_step < rows
        ]
        return lax.ppermute(block, LON + LAT, route)
    if lat_step:
        route = [(r, r + lat_step) for r in range(rows) if 0 <= r + lat_step < rows]
        return lax.ppermute(block, LAT, route)
    return lax.ppermute(block, LON, [(c, (c + lon_step) % cols) for c in range(cols)])


def exchange(parts, axes):
    return lax.all_to_all(parts, axes, 0, 0)


def total_of(parts):
    return jnp.sum(parts.astype(F32), axis=0).astype(BF16)


def summed_everywhere(sums):
    near = lax.axis_size(NEAR)
    far = lax.axis_size(FAR)
    rows = sums.shape[0] // near
    padded = -(-rows // (8 * far)) * (8 * far)
    part = total_of(exchange(sums.reshape(near, rows, 128), NEAR))
    part = jnp.pad(part, ((0, padded - rows), (0, 0)))
    part = total_of(exchange(part.reshape(far, padded // far, 128), FAR))
    part = exchange(jnp.broadcast_to(part[None], (far,) + part.shape), FAR)
    part = part.reshape(padded, 128)[:rows]
    whole = exchange(jnp.broadcast_to(part[None], (near,) + part.shape), NEAR)
    return whole.reshape(near * rows, 128)


def per_device(
    tokens,
    cotangent,
    qkv_codes,
    proj_codes,
    up_codes,
    down_codes,
    bit_widths,
    quant_scales,
    bias_table,
    bias_index,
    merge_weight,
):
    lat_limit = lax.axis_size(LAT) * ROWS - LAT_PAD
    lat_info = jnp.stack([lax.axis_index(LAT), lat_limit]).astype(jnp.int32)
    limits = jnp.left_shift(jnp.ones((4,), jnp.int32), bit_widths - 1) - 1
    fan_in = jnp.array([1.0, 1.0, 1.0, math.sqrt(C / FF)], F32)
    factors = fan_in / quant_scales.astype(F32)

    big = ROWS - OFF
    big_shape = (LEVS * big * SUB, 2 * C)
    thin_shape = (LEVS * OFF * SUB, 2 * C)
    pieces = [(big_shape, BF16), (thin_shape, BF16), (big_shape, BF16), (thin_shape, BF16)]
    own, lat_part, lon_part, diag_part = call(
        pack_kernel,
        pieces,
        (tokens, cotangent),
        [pltpu.VMEM((LEVS, ROWS, 16, 2 * C), F32)],
    )
    lon_part = shifted(lon_part, 0, 1)
    lat_part = shifted(lat_part, 1, 0)
    diag_part = shifted(diag_part, 1, 1)

    w_qkv, w_proj, w_up, w_down, bias = call(
        prep_kernel,
        [
            ((3, C, C), BF16),
            ((C, C), BF16),
            ((C, FF), BF16),
            ((FF, C), BF16),
            ((4, STACK, 128), BF16),
        ],
        (
            lat_info,
            limits,
            factors,
            bias_index.reshape(WTOK, WTOK),
            bias_table,
            qkv_codes,
            proj_codes,
            up_codes,
            down_codes,
        ),
        [pltpu.VMEM((CHUNKS, 16, 128), F32)],
        scalars=3,
        flops=2_000_000_000,
    )
    own, lat_part, lon_part, diag_part, sums = call(
        main_kernel,
        pieces + [((18 * C, 128), BF16)],
        (lat_info, own, lat_part, lon_part, diag_part, w_qkv, w_proj, w_up, w_down, bias),
        [pltpu.VMEM((LEVS, ROWS, 2, SUB, 2 * C), F32)],
        scalars=1,
        flops=2_000_000_000,
    )
    lon_part = shifted(lon_part, 0, -1)
    lat_part = shifted(lat_part, -1, 0)
    diag_part = shifted(diag_part, -1, -1)
    whole = summed_everywhere(sums)
    merged, grad_tokens = call(
        finish_kernel,
        [((LEVS, ROWS // 2, COLS // 2, 2 * C), BF16), ((LEVS, ROWS, COLS, C), BF16)],
        (own, lat_part, lon_part, diag_part, merge_weight),
        [pltpu.VMEM((LEVS, ROWS, 2, SUB, 2 * C), F32)],
        flops=400_000_000,
    )
    grads = call(
        spread_kernel,
        [((C, 3 * C), BF16), ((C, C), BF16), ((C, FF), BF16), ((FF, C), BF16)],
        (whole,),
    )
    return (merged, grad_tokens, *grads)


def solution(mesh):
    cols, rows = mesh.devices.shape
    fine = Mesh(mesh.devices.reshape(cols // 4, 2, 2, rows // 2, 2), LON + LAT)
    cells = P(None, LAT, LON, None)
    placed = (
        cells,
        cells,
        P(),
        P(),
        P(),
        P(),
        P(),
        P(),
        P(LAT, None, None, None),
        P(),
        P(),
    )
    return jax.shard_map(
        per_device,
        mesh=fine,
        in_specs=placed,
        out_specs=(cells, cells, P(), P(), P(), P()),
        check_vma=False,
    )
```

time: 349 us -> 143 us (0.41)
  local copies, waits for them, and re-layouts: 125 us -> 14.4 us
  blocking collectives: 118 us -> 58.8 us
  Pallas kernels: 0 us -> 31.7 us
  other arithmetic: 32.3 us -> 1.87 us
  matrix products: 20.3 us -> 0 us
  starting transfers between devices: 32.7 us -> 23.7 us
  between operations: 6.75 us -> 0.8 us
    psum x1 -> x0, blocking collectives: 118 us -> none  [per_device(): lax.psum((qkv_total, proj_total, up_total, down_total), ('lon', 'lat'))]
    all_to_all x0 -> x3, blocking collectives: none -> 58.8 us  [exchange(): return lax.all_to_all(parts, axes, 0, 0)]
    gather x1 -> x0, local copies, waits for them, and re-layouts: 51.2 us -> none  [window_terms(): gathered = table_rows[:, :, :, bias_index].astype(jnp.float32)]
    convert_element_type x5 -> x0, local copies, waits for them, and re-layouts: 37.4 us -> none  [the longest x1 31.1 us: window_terms(): gathered = table_rows[:, :, :, bias_index].astype(jnp.float32)]
    pallas_call x0 -> x5, Pallas kernels: none -> 31.7 us  [call(): pl.pallas_call(kernel, out_shape=[jax.ShapeDtypeStruct(s, t) for s, t in...]
    dot_general x19 -> x0, matrix products: 20.3 us -> none  [the longest x9 8.22 us: product(): return jnp.dot(left, right, preferred_element_type=jnp.float32)]
    ppermute x8 -> x6, starting transfers between devices: 32.7 us -> 16.6 us  [the longest x2 6.87 us: shifted(): return lax.ppermute(block, LON + LAT, route)]
    convert_element_type x5 -> x0, other arithmetic: 13.5 us -> none  [the longest x1 11.4 us: window_terms(): gathered = table_rows[:, :, :, bias_index].astype(jnp.float32)]
  transfers between devices with their start and end apart: 8 -> 7, of which waited for: 5 -> 2; matrix products, arithmetic and copies ran while one was open for 33% -> 5% of each run, Pallas kernels for 0% -> 13%
where the time goes in v1:
time: 143 us
  blocking collectives  58.8 us (41%)
  Pallas kernels  31.7 us (22%)
  starting transfers between devices  23.7 us (17%)
  local copies, waits for them, and re-layouts  14.4 us (10%)
  waiting for transfers between devices  11.3 us (8%)
  other arithmetic  1.87 us (1%)
    all_to_all x3, blocking collectives, exchange(): return lax.all_to_all(parts, axes, 0, 0)  58.8 us
    pallas_call x5, Pallas kernels, call(): pl.pallas_call(kernel, out_shape=[jax.ShapeDtypeStruct(s, t) for s, t in...  31.7 us
    unnamed x41, local copies, waits for them, and re-layouts  12.5 us
    ppermute x2, waiting for transfers between devices, shifted(): return lax.ppermute(block, LAT, route)  9.21 us
    all_to_all x1, starting transfers between devices, exchange(): return lax.all_to_all(parts, axes, 0, 0)  7.02 us
    ppermute x2, starting transfers between devices, shifted(): return lax.ppermute(block, LON + LAT, route)  6.87 us
    ppermute x2, starting transfers between devices, shifted(): return lax.ppermute(block, LAT, route)  5.23 us
    ppermute x2, starting transfers between devices, shifted(): lax.ppermute(block, LON, [(c, (c + lon_step) % cols) for c in range(cols)])  4.54 us
  transfers between devices with their start and end apart: 7, of which 2 were waited for; matrix products, arithmetic and copies ran while one was open for 5% of the time, Pallas kernels for 13%

profile of v1, /device:TPU:1, one launch (start us, length us, event | category | flops | bytes accessed | tf_op | source)
XLA Modules:
  0.0 142.6 jit_solution(547419569175676129)
XLA Ops:
  0.6 1.6 %copy.25.tok_ref = bf16[2,12,12,192]{3,2,1,0:T(8,128)(2,1)} copy(bf16[2,12,12,192]{3,0,2,1:T(2,128)(2,1)} %param.12) | data formatting | bytes 221184 | tf_op args[0]
  2.3 0.7 copy.26.cot_ref
  3.0 1.9 %shard_map.163 = (bf16[144,384]{1,0:T(8,128)(2,1)}, bf16[48,384]{1,0:T(8,128)(2,1)}, bf16[144,384]{1,0:T(8,128)(2,1)}, bf16[48,384]{1,0:T(8,128)(2,1)}) custom-call(bf16[2,12,12,192]{3,2,1,0:T(8,128)(2,1)} %copy.25.tok_ref, bf16[2,12,12,192]{3,2,1,0:T(8,128)(2,1)} %copy.26.cot_ref), custom_call_target="tpu_custom_call" | custom-call | bytes 516096 | tf_op jit(solution)/shard_map/pallas_call | solution.py:365
  4.9 3.9 %collective-permute-start = (bf16[48,384]{1,0:T(8,128)(2,1)}, bf16[48,384]{1,0:T(8,128)(2,1)S(1)}, u32[]{:S(2)}, u32[]{:S(2)}) collective-permute-start(bf16[48,384]{1,0:T(8,128)(2,1)} %get-tuple-element.27), channel_id=1, source_target_pairs={{0,1},{1,2},{2,3},{3,4},{4,5},{5,6},{6,7},{7,8},{8,9},{9,10},{10,1... | collective-permute-start | bytes 110600 | tf_op jit(solution)/shard_map/ppermute | solution.py:389
  8.8 5.6 %collective-permute-start.2 = (bf16[48,384]{1,0:T(8,128)(2,1)}, bf16[48,384]{1,0:T(8,128)(2,1)S(1)}, u32[]{:S(2)}, u32[]{:S(2)}) collective-permute-start(bf16[48,384]{1,0:T(8,128)(2,1)} %get-tuple-element.29), channel_id=1, source_target_pairs={{0,17},{1,18},{2,19},{3,20},{4,21},{5,22},{6,23},{7,24},{8,25},{9,... | collective-permute-start | bytes 110600 | tf_op jit(solution)/shard_map/ppermute | solution.py:386
  14.4 2.5 %collective-permute-start.1 = (bf16[144,384]{1,0:T(8,128)(2,1)}, bf16[144,384]{1,0:T(8,128)(2,1)S(1)}, u32[]{:S(2)}, u32[]{:S(2)}) collective-permute-start(bf16[144,384]{1,0:T(8,128)(2,1)} %get-tuple-element.28), channel_id=1, source_target_pairs={{0,16},{16,32},{32,48},{48,64},{64,80},{80,96},{96,112},{112,128},... | collective-permute-start | bytes 331784 | tf_op jit(solution)/shard_map/ppermute | solution.py:390
  17.0 0.0 copy-start.14
  17.0 0.6 copy-done.14
  17.6 0.5 shift-left_add_fusion.lim_ref
  18.1 0.7 copy.27.tab_ref
  18.8 0.3 copy-done.3
  19.1 0.8 reshape.29.idx_ref
  19.8 0.0 copy-done.1
  19.8 1.1 copy.28.cd_ref
  21.0 0.6 pad_add_fusion.lat_ref
  21.6 0.1 copy-done.15
  21.7 0.0 copy-done.16
  21.7 0.6 convert_divide_fusion.fac_ref
  22.3 15.7 %shard_map.164 = (bf16[3,192,192]{2,1,0:T(8,128)(2,1)}, bf16[192,192]{1,0:T(8,128)(2,1)}, bf16[192,768]{1,0:T(8,128)(2,1)}, bf16[768,192]{1,0:T(8,128)(2,1)}, bf16[4,576,128]{2,1,0:T(8,128)(2,1)}) custom-call(s32[2]{0:T(128)} %pad_add_fusion.lat_ref, s32[4]{0:T(128)} %shift-left_add_fusion.lim_ref, f32[4]{0:T(128)} %convert_divide_fusion.fac_ref, ...), custom_call_target="tpu_custom_call" | custom-call | flops 2000000000 | bytes 3406504 | tf_op jit(solution)/shard_map/pallas_call | solution.py:365
  38.0 0.0 collective-permute-done.lat_part_ref
  38.0 0.0 collective-permute-done.2.diag_part_ref
  38.0 0.0 collective-permute-done.1.lon_part_ref
  38.0 0.0 copy-start.5
  38.0 0.6 copy-done.8
  38.6 0.0 copy-done.9
  38.6 0.1 copy-done.5
  38.7 8.9 %shard_map.165 = (bf16[144,384]{1,0:T(8,128)(2,1)}, bf16[48,384]{1,0:T(8,128)(2,1)}, bf16[144,384]{1,0:T(8,128)(2,1)}, bf16[48,384]{1,0:T(8,128)(2,1)}, bf16[3456,128]{1,0:T(8,128)(2,1)}) custom-call(s32[2]{0:T(128)} %pad_add_fusion.lat_ref, bf16[144,384]{1,0:T(8,128)(2,1)} %get-tuple-element.26.own_ref, bf16[48,384]{1,0:T(8,128)(2,1)} %copy-done.8, ...), custom_call_target="tpu_custom_call" | custom-call | flops 2000000000 | bytes 2949128 | tf_op jit(solution)/shard_map/pallas_call | solution.py:365
  47.6 17.6 %all_to_all.20 = bf16[8,432,128]{2,1,0:T(8,128)(2,1)S(1)} all-to-all(bf16[8,432,128]{2,1,0:T(8,128)(2,1)} %bitcast.8), channel_id=1, replica_groups=mesh['z'=8,'xh'=2,'c'=2,'y'=8,'xl'=2] {'xh','c','xl'}, dimensions={0} | all-to-all | bytes 1769472 | tf_op jit(solution)/shard_map/all_to_all | solution.py:394
  65.2 0.1 reduce_sum.24
  65.3 25.8 %all_to_all.21 = bf16[64,8,128]{2,1,0:T(8,128)(2,1)S(1)} all-to-all(bf16[64,8,128]{2,1,0:T(8,128)(2,1)S(1)} %pad_bitcast_fusion), channel_id=1, replica_groups=mesh['z'=8,'xh'=2,'c'=2,'y'=8,'xl'=2] {'y','z'}, dimensions={0} | all-to-all | bytes 262144 | tf_op jit(solution)/shard_map/all_to_all | solution.py:394
  91.2 0.1 reduce_sum.25
  91.2 15.4 %all_to_all.22 = bf16[64,8,128]{2,1,0:T(8,128)(2,1)S(1)} all-to-all(bf16[64,8,128]{2,1,0:T(8,128)(2,1)S(1)} %broadcast_in_dim.6), channel_id=1, replica_groups=mesh['z'=8,'xh'=2,'c'=2,'y'=8,'xl'=2] {'y','z'}, dimensions={0} | all-to-all | bytes 262144 | tf_op jit(solution)/shard_map/all_to_all | solution.py:394
  106.7 1.0 broadcast_in_dim.16
  107.7 7.0 %all-to-all-start.3 = ((bf16[8,432,128]{2,1,0:T(8,128)(2,1)}), bf16[8,432,128]{2,1,0:T(8,128)(2,1)S(1)}, u32[]{:S(2)}, u32[]{:S(2)}) async-start(bf16[8,432,128]{2,1,0:T(8,128)(2,1)} %broadcast_in_dim.16), calls=%async_computation.3 | async-start | bytes 1769472 | tf_op jit(solution)/shard_map/all_to_all | solution.py:394
  114.8 2.0 %collective-permute-start.4 = (bf16[144,384]{1,0:T(8,128)(2,1)S(1)}, bf16[144,384]{1,0:T(8,128)(2,1)S(1)}, u32[]{:S(2)}, u32[]{:S(2)}) collective-permute-start(bf16[144,384]{1,0:T(8,128)(2,1)S(1)} %copy-done.6), channel_id=1, source_target_pairs={{0,496},{16,0},{32,16},{48,32},{64,48},{80,64},{96,80},{112,96},{1... | collective-permute-start | bytes 331784 | tf_op jit(solution)/shard_map/ppermute | solution.py:390
  116.8 1.3 collective-permute-start.3
  118.1 1.3 collective-permute-start.5
  119.4 9.2 %collective-permute-done.3.lat_ref = bf16[48,384]{1,0:T(8,128)(2,1)S(1)} collective-permute-done((bf16[48,384]{1,0:T(8,128)(2,1)S(1)}, bf16[48,384]{1,0:T(8,128)(2,1)S(1)}, u32[]{:S(2)}, u32[]{:S(2)}) %collective-permute-start.3) | collective-permute-done | bytes 36896 | tf_op jit(solution)/shard_map/ppermute | solution.py:389
  128.6 0.0 collective-permute-done.5.diag_ref
  128.6 2.1 %collective-permute-done.4.lon_ref = bf16[144,384]{1,0:T(8,128)(2,1)S(1)} collective-permute-done((bf16[144,384]{1,0:T(8,128)(2,1)S(1)}, bf16[144,384]{1,0:T(8,128)(2,1)S(1)}, u32[]{:S(2)}, u32[]{:S(2)}) %collective-permute-start.4) | collective-permute-done | bytes 110624 | tf_op jit(solution)/shard_map/ppermute | solution.py:390
  130.7 0.6 copy-done.7
  131.4 2.9 %shard_map.166 = (bf16[2,6,6,384]{3,2,1,0:T(8,128)(2,1)}, bf16[2,12,12,192]{3,2,1,0:T(8,128)(2,1)}) custom-call(bf16[144,384]{1,0:T(8,128)(2,1)} %get-tuple-element.35.own_ref, bf16[48,384]{1,0:T(8,128)(2,1)} %copy-done.12, bf16[144,384]{1,0:T(8,128)(2,1)} %copy-done.7, bf16[48,384]{1,0:T(8,128)(2,1)} %copy-done.13, bf16[768,384]{1,0:T(8,128)(2,1)} %weight_ref.1), custom_call_target="tpu_custom_call" | custom-call | flops 400000000 | bytes 1050624 | tf_op jit(solution)/shard_map/pallas_call | solution.py:365
  134.2 1.5 %copy.29 = bf16[2,6,6,384]{3,0,2,1:T(2,128)(2,1)} copy(bf16[2,6,6,384]{3,2,1,0:T(8,128)(2,1)} %get-tuple-element.52) | data formatting | bytes 110592
  135.8 1.7 %copy.30 = bf16[2,12,12,192]{3,0,2,1:T(2,128)(2,1)} copy(bf16[2,12,12,192]{3,2,1,0:T(8,128)(2,1)} %get-tuple-element.53) | data formatting | bytes 221184
  137.5 0.0 all-to-all-done.3
  137.5 0.9 copy-done
  138.5 2.3 %shard_map.167 = (bf16[192,576]{1,0:T(8,128)(2,1)}, bf16[192,192]{1,0:T(8,128)(2,1)}, bf16[192,768]{1,0:T(8,128)(2,1)}, bf16[768,192]{1,0:T(8,128)(2,1)}) custom-call(bf16[3456,128]{1,0:T(8,128)(2,1)} %bitcast.7), custom_call_target="tpu_custom_call" | custom-call | bytes 1769472 | tf_op jit(solution)/shard_map/pallas_call | solution.py:365
  140.8 1.9 %copy.31 = bf16[768,192]{0,1:T(8,128)(2,1)} copy(bf16[768,192]{1,0:T(8,128)(2,1)} %get-tuple-element.57) | data formatting | bytes 589824
  (25 shorter events, 0.1 us)
Async XLA Ops:
  0.6 1.7 %copy-start.2 = (bf16[2,12,12,192]{3,0,2,1:T(2,128)(2,1)S(1)}, bf16[2,12,12,192]{3,0,2,1:T(2,128)(2,1)}, u32[]{:S(2)}) copy-start(bf16[2,12,12,192]{3,0,2,1:T(2,128)(2,1)} %param.13) | copy-start | bytes 331780
  2.3 17.6 %copy-start.1 = (s32[768,192]{0,1:T(8,128)S(1)}, s32[768,192]{0,1:T(8,128)}, u32[]{:S(2)}) copy-start(s32[768,192]{0,1:T(8,128)} %param.17) | copy-start | bytes 1769476
  3.0 15.1 %copy-start.4 = (bf16[2,1,6,3312]{3,0,2,1:T(2,128)(2,1)S(1)}, bf16[2,1,6,3312]{3,0,2,1:T(2,128)(2,1)}, u32[]{:S(2)}) copy-start(bf16[2,1,6,3312]{3,0,2,1:T(2,128)(2,1)} %param.20) | copy-start | bytes 238468
  4.9 33.1 %collective-permute-start = (bf16[48,384]{1,0:T(8,128)(2,1)}, bf16[48,384]{1,0:T(8,128)(2,1)S(1)}, u32[]{:S(2)}, u32[]{:S(2)}) collective-permute-start(bf16[48,384]{1,0:T(8,128)(2,1)} %get-tuple-element.27), channel_id=1, source_target_pairs={{0,1},{1,2},{2,3},{3,4},{4,5},{5,6},{6,7},{7,8},{8,9},{9,10},{10,1... | collective-permute-start | bytes 110600 | tf_op jit(solution)/shard_map/ppermute | solution.py:389
  8.8 29.2 %collective-permute-start.2 = (bf16[48,384]{1,0:T(8,128)(2,1)}, bf16[48,384]{1,0:T(8,128)(2,1)S(1)}, u32[]{:S(2)}, u32[]{:S(2)}) collective-permute-start(bf16[48,384]{1,0:T(8,128)(2,1)} %get-tuple-element.29), channel_id=1, source_target_pairs={{0,17},{1,18},{2,19},{3,20},{4,21},{5,22},{6,23},{7,24},{8,25},{9,... | collective-permute-start | bytes 110600 | tf_op jit(solution)/shard_map/ppermute | solution.py:386
  14.4 23.6 %collective-permute-start.1 = (bf16[144,384]{1,0:T(8,128)(2,1)}, bf16[144,384]{1,0:T(8,128)(2,1)S(1)}, u32[]{:S(2)}, u32[]{:S(2)}) collective-permute-start(bf16[144,384]{1,0:T(8,128)(2,1)} %get-tuple-element.28), channel_id=1, source_target_pairs={{0,16},{16,32},{32,48},{48,64},{64,80},{80,96},{96,112},{112,128},... | collective-permute-start | bytes 331784 | tf_op jit(solution)/shard_map/ppermute | solution.py:390
  17.0 0.7 copy-start.14
  18.1 0.9 copy-start.3
  21.0 0.7 copy-start.15
  21.0 0.7 copy-start.16
  38.0 0.6 copy-start.8
  38.0 0.6 copy-start.9
  38.0 0.6 copy-start.5
  107.7 7.0 %copy-start.6 = (bf16[144,384]{1,0:T(8,128)(2,1)S(1)}, bf16[144,384]{1,0:T(8,128)(2,1)}, u32[]{:S(2)}) copy-start(bf16[144,384]{1,0:T(8,128)(2,1)} %get-tuple-element.37) | copy-start | bytes 331780
  107.7 9.1 %copy-start.11 = (bf16[48,384]{1,0:T(8,128)(2,1)S(1)}, bf16[48,384]{1,0:T(8,128)(2,1)}, u32[]{:S(2)}) copy-start(bf16[48,384]{1,0:T(8,128)(2,1)} %get-tuple-element.36) | copy-start | bytes 110596
  107.7 10.4 %copy-start.10 = (bf16[48,384]{1,0:T(8,128)(2,1)S(1)}, bf16[48,384]{1,0:T(8,128)(2,1)}, u32[]{:S(2)}) copy-start(bf16[48,384]{1,0:T(8,128)(2,1)} %get-tuple-element.38) | copy-start | bytes 110596
  107.7 29.8 %all-to-all-start.3 = ((bf16[8,432,128]{2,1,0:T(8,128)(2,1)}), bf16[8,432,128]{2,1,0:T(8,128)(2,1)S(1)}, u32[]{:S(2)}, u32[]{:S(2)}) async-start(bf16[8,432,128]{2,1,0:T(8,128)(2,1)} %broadcast_in_dim.16), calls=%async_computation.3 | async-start | bytes 1769472 | tf_op jit(solution)/shard_map/all_to_all | solution.py:394
  114.8 16.0 %collective-permute-start.4 = (bf16[144,384]{1,0:T(8,128)(2,1)S(1)}, bf16[144,384]{1,0:T(8,128)(2,1)S(1)}, u32[]{:S(2)}, u32[]{:S(2)}) collective-permute-start(bf16[144,384]{1,0:T(8,128)(2,1)S(1)} %copy-done.6), channel_id=1, source_target_pairs={{0,496},{16,0},{32,16},{48,32},{64,48},{80,64},{96,80},{112,96},{1... | collective-permute-start | bytes 331784 | tf_op jit(solution)/shard_map/ppermute | solution.py:390
  116.8 11.8 %collective-permute-start.3 = (bf16[48,384]{1,0:T(8,128)(2,1)S(1)}, bf16[48,384]{1,0:T(8,128)(2,1)S(1)}, u32[]{:S(2)}, u32[]{:S(2)}) collective-permute-start(bf16[48,384]{1,0:T(8,128)(2,1)S(1)} %copy-done.11), channel_id=1, source_target_pairs={{1,0},{2,1},{3,2},{4,3},{5,4},{6,5},{7,6},{8,7},{9,8},{10,9},{11,1... | collective-permute-start | bytes 110600 | tf_op jit(solution)/shard_map/ppermute | solution.py:389
  118.1 10.5 %collective-permute-start.5 = (bf16[48,384]{1,0:T(8,128)(2,1)S(1)}, bf16[48,384]{1,0:T(8,128)(2,1)S(1)}, u32[]{:S(2)}, u32[]{:S(2)}) collective-permute-start(bf16[48,384]{1,0:T(8,128)(2,1)S(1)} %copy-done.10), channel_id=1, source_target_pairs={{1,496},{2,497},{3,498},{4,499},{5,500},{6,501},{7,502},{8,503},{9... | collective-permute-start | bytes 110600 | tf_op jit(solution)/shard_map/ppermute | solution.py:386
  128.6 2.1 %copy-start.12 = (bf16[48,384]{1,0:T(8,128)(2,1)}, bf16[48,384]{1,0:T(8,128)(2,1)S(1)}, u32[]{:S(2)}) copy-start(bf16[48,384]{1,0:T(8,128)(2,1)S(1)} %collective-permute-done.3.lat_ref) | copy-start | bytes 110596
  128.6 2.1 %copy-start.13 = (bf16[48,384]{1,0:T(8,128)(2,1)}, bf16[48,384]{1,0:T(8,128)(2,1)S(1)}, u32[]{:S(2)}) copy-start(bf16[48,384]{1,0:T(8,128)(2,1)S(1)} %collective-permute-done.5.diag_ref) | copy-start | bytes 110596
  130.7 0.6 copy-start.7
  137.5 0.9 copy-start

commit v2 on v1

--- a/solution.py
+++ b/solution.py
@@ -27,7 +27,8 @@
 FRAME = LEVS * ROWS * 2 * SUB
 BLOCK = FRAME // 4
 STACK = HEADS * BLOCK
-CHUNKS = -(-POS // 128)
+LOWS = 256
+HIGHS = -(-POS // LOWS)
 
 EPSILON = 1e-05
 MASKED = -1000000000.0
@@ -57,27 +58,29 @@
     return lax.dot_general(left, right, (((0,), (0,)), ((), ())), preferred_element_type=F32)
 
 
-def pack_kernel(tok_ref, cot_ref, own_ref, lat_ref, lon_ref, diag_ref, wide):
-    wide[...] = jnp.zeros_like(wide)
-    wide[:, :, 0:COLS, :] = jnp.concatenate(
-        [tok_ref[...].astype(F32), cot_ref[...].astype(F32)], axis=-1
-    )
-    left = wide[:, :, 0:SUB, :]
-    right = wide[:, :, HALF : HALF + SUB, :]
-
-    def flat(piece):
-        return piece.reshape(-1, 2 * C).astype(BF16)
-
-    own_ref[...] = flat(left[:, : ROWS - OFF])
-    lat_ref[...] = flat(left[:, ROWS - OFF :])
-    lon_ref[...] = flat(right[:, : ROWS - OFF])
-    diag_ref[...] = flat(right[:, ROWS - OFF :])
+def pack_kernel(tok_ref, cot_ref, own_ref, lat_ref, lon_ref, diag_ref):
+    both = jnp.concatenate(
+        [ref[...].astype(F32).reshape(LEVS * ROWS * COLS, C) for ref in (tok_ref, cot_ref)], axis=-1
+    ).astype(BF16)
+
+    def pick(first, count, col):
+        shape = (LEVS * count * SUB, LEVS * ROWS * COLS)
+        to = iota(shape, 0)
+        lev = jnp.where(to >= count * SUB, 1, 0)
+        row = (to >> 3) - lev * count + first
+        sub = jnp.bitwise_and(to, SUB - 1)
+        hot = (iota(shape, 1) == (row * COLS + col + sub) * 2 + lev) & (sub < HALF)
+        return product(hot.astype(F32).astype(BF16), both).astype(BF16)
+
+    own_ref[...] = pick(0, ROWS - OFF, 0)
+    lat_ref[...] = pick(ROWS - OFF, OFF, 0)
+    lon_ref[...] = pick(0, ROWS - OFF, HALF)
+    diag_ref[...] = pick(ROWS - OFF, OFF, HALF)
 
 
 def prep_kernel(
-    lat_ref,
-    lim_ref,
-    fac_ref,
+    bits_ref,
+    scale_ref,
     idx_ref,
     tab_ref,
     cq_ref,
@@ -90,64 +93,82 @@
     wd_ref,
     bias_ref,
     rows,
+    places,
+    found,
 ):
-    def dequant(codes, layer):
-        limit = lim_ref[layer]
+    def dequant(codes, layer, fan_in):
+        limit = jnp.left_shift(1, bits_ref[layer] - 1) - 1
         clipped = jnp.minimum(jnp.maximum(codes, -limit), limit).astype(F32)
-        return clipped * fac_ref[layer]
-
-    full = dequant(cq_ref[...], 0)
+        whole = jnp.full((1, 128), scale_ref[layer], jnp.int32).astype(F32)
+        return clipped * (math.sqrt(C / fan_in) / whole)[:, :1]
+
+    full = dequant(cq_ref[...], 0, C)
     for part in range(3):
         wq_ref[part] = full[:, part * C : (part + 1) * C].astype(BF16)
-    wp_ref[...] = dequant(cp_ref[...], 1).astype(BF16)
-    wu_ref[...] = dequant(cu_ref[...], 2).astype(BF16)
-    wd_ref[...] = dequant(cd_ref[...], 3).astype(BF16)
-
-    for win in range(2):
-        table = tab_ref[win, 0].astype(F32)
-        for chunk in range(CHUNKS):
-            width = min(128, POS - chunk * 128)
-            rows[chunk, win * SUB : win * SUB + HEADS, 0:width] = table[
-                :, chunk * 128 : chunk * 128 + width
+    wp_ref[...] = dequant(cp_ref[...], 1, C).astype(BF16)
+    wu_ref[...] = dequant(cu_ref[...], 2, C).astype(BF16)
+    wd_ref[...] = dequant(cd_ref[...], 3, FF).astype(BF16)
+
+    rows[...] = jnp.zeros_like(rows)
+    for head in range(HEADS):
+        table = tab_ref[head].astype(F32)
+        for high in range(HIGHS):
+            width = min(LOWS, POS - high * LOWS)
+            rows[high * 16 + head * 2 : high * 16 + head * 2 + 2, 0:width] = table[
+                :, high * LOWS : high * LOWS + width
             ]
+    table = rows[...].astype(BF16)
 
     index = idx_ref[...]
-    high = lax.shift_right_logical(index, 7).astype(F32).astype(BF16)
-    low = jnp.bitwise_and(index, 127).astype(F32).astype(BF16)
-
-    def place(where):
+    parts = [
+        lax.shift_right_logical(index, 8).astype(F32).astype(BF16),
+        jnp.bitwise_and(index, LOWS - 1).astype(F32).astype(BF16),
+    ]
+
+    def token(where):
         sub = jnp.bitwise_and(where, SUB - 1)
-        token = (where >> 4) * WLON + jnp.bitwise_and(where >> 3, 1) * HALF + sub
-        return jnp.where((sub < HALF) & (where < BLOCK), token, -1000)
-
-    key = iota((BLOCK, 128), 1)
+        inside = (where >> 4) * WLON + jnp.bitwise_and(where >> 3, 1) * HALF + sub
+        return jnp.where((sub < HALF) & (where < BLOCK), inside, -1000)
+
     for lev in range(LEVS):
         base = (1 - lev) * (WTOK // 2)
-        pick_q = (iota((BLOCK, WTOK), 1) == place(iota((BLOCK, WTOK), 0)) + base).astype(F32)
-        pick_k = (iota((WTOK, 128), 0) == place(iota((WTOK, 128), 1)) + base).astype(F32)
-        pick_q = pick_q.astype(BF16)
-        pick_k = pick_k.astype(BF16)
-        hi = product(product(pick_q, high).astype(BF16), pick_k).astype(jnp.int32)
-        lo = product(product(pick_q, low).astype(BF16), pick_k).astype(jnp.int32)
-        for win in range(2):
-            row = lat_ref[0] * ROWS - OFF + win * WLAT + (key >> 4)
-            usable = (row >= 0) & (row < lat_ref[1])
-            usable = usable & (jnp.bitwise_and(key, SUB - 1) < HALF) & (key < BLOCK)
-
-            def one_head(head, carry):
-                found = jnp.zeros((BLOCK, 128), F32)
-                for chunk in range(CHUNKS):
-                    line = rows[chunk, pl.ds(win * SUB + head, 1), :]
-                    taken = jnp.take_along_axis(
-                        jnp.broadcast_to(line, (BLOCK, 128)), lo, axis=1
-                    )
-                    found = jnp.where(hi == chunk, taken, found)
-                found = jnp.where(usable, found, MASKED)
-                at = pl.multiple_of(head * BLOCK, BLOCK)
-                bias_ref[lev * 2 + win, pl.ds(at, BLOCK), :] = found.astype(BF16)
-                return carry
-
-            lax.fori_loop(0, HEADS, one_head, 0)
+        pick_q = (iota((BLOCK, WTOK), 1) == token(iota((BLOCK, WTOK), 0)) + base).astype(F32)
+        pick_k = (iota((WTOK, 128), 0) == token(iota((WTOK, 128), 1)) + base).astype(F32)
+        for i, part in enumerate(parts):
+            moved = product(product(pick_q.astype(BF16), part).astype(BF16), pick_k.astype(BF16))
+            places[i, lev * BLOCK : (lev + 1) * BLOCK, :] = moved
+
+    entry = iota((LOWS, 128), 0).astype(F32)
+
+    def eight(group, carry):
+        at = pl.multiple_of(group * SUB, SUB)
+        high = places[0, pl.ds(at, SUB), :]
+        low = places[1, pl.ds(at, SUB), :]
+        hot = [(entry == low[s : s + 1]).astype(F32).astype(BF16) for s in range(HALF)]
+        values = product(table, jnp.concatenate(hot, axis=1))
+        for s in range(HALF):
+            chosen = jnp.zeros((16, 128), F32)
+            here = jnp.broadcast_to(high[s : s + 1], (16, 128))
+            for i in range(HIGHS):
+                candidate = values[i * 16 : (i + 1) * 16, s * 128 : (s + 1) * 128]
+                chosen = jnp.where(here == float(i), candidate, chosen)
+            found[at + s] = chosen
+        found[at + HALF] = jnp.zeros((16, 128), F32)
+        found[at + HALF + 1] = jnp.zeros((16, 128), F32)
+        return carry
+
+    lax.fori_loop(0, LEVS * BLOCK // SUB, eight, 0, unroll=8)
+
+    key = iota((BLOCK, 128), 1)
+    for win in range(2):
+        row = lax.axis_index(LAT) * ROWS - OFF + win * WLAT + (key >> 4)
+        usable = (row >= 0) & (row < lax.axis_size(LAT) * ROWS - LAT_PAD)
+        usable = usable & (jnp.bitwise_and(key, SUB - 1) < HALF) & (key < BLOCK)
+        for lev in range(LEVS):
+            for head in range(HEADS):
+                values = found[lev * BLOCK : (lev + 1) * BLOCK, head * 2 + win, :]
+                values = jnp.where(usable, values, MASKED)
+                bias_ref[lev * 2 + win, head * BLOCK : (head + 1) * BLOCK, :] = values.astype(BF16)
 
 
 def unit(values):
@@ -164,7 +185,6 @@
 
 
 def main_kernel(
-    lat_ref,
     own_ref,
     lat_part_ref,
     lon_part_ref,
@@ -193,8 +213,9 @@
     both = frame[...].reshape(FRAME, 2 * C)
 
     place = iota((FRAME, C), 0)
-    row = lat_ref[0] * ROWS - OFF + (place >> 4) - jnp.where(place >= FRAME // 2, ROWS, 0)
-    valid = (row >= 0) & (row < lat_ref[1]) & (jnp.bitwise_and(place, SUB - 1) < HALF)
+    row = lax.axis_index(LAT) * ROWS - OFF + (place >> 4) - jnp.where(place >= FRAME // 2, ROWS, 0)
+    valid = (row >= 0) & (row < lax.axis_size(LAT) * ROWS - LAT_PAD)
+    valid = valid & (jnp.bitwise_and(place, SUB - 1) < HALF)
     start = jnp.where(valid, both[:, :C], 0.0)
     d_out = jnp.where(valid, both[:, C:], 0.0)
     d_out_low = d_out.astype(BF16)
@@ -242,9 +263,9 @@
     slope = half + 0.5 * pre_act * (1.0 - bend * bend) * (
         inner * (1.0 + (3 * 0.044715) * square)
     )
-    final = jnp.where(valid, resid + product(hidden, wd_ref[...]), 0.0)
-
-    d_hidden = across(d_out_low, wd_ref[...]).astype(BF16).astype(F32)
+    final = jnp.where(valid, resid + across(hidden, wd_ref[...]), 0.0)
+
+    d_hidden = product(d_out_low, wd_ref[...]).astype(BF16).astype(F32)
     d_pre = (slope * d_hidden).astype(BF16)
     d_normed_two = across(d_pre, wu_ref[...]).astype(BF16).astype(F32)
     d_resid = (d_out + unit_back(normal_two, scale_two, d_normed_two)).astype(BF16)
@@ -307,7 +328,7 @@
     proj_ref[...] = small[3].astype(BF16)
     for i in range(6):
         up_ref[:, i * 128 : (i + 1) * 128] = sums_ref[(6 + i) * C : (7 + i) * C, :]
-        down_ref[i * 128 : (i + 1) * 128, :] = tile(12 + i).T.astype(BF16)
+        down_ref[:, i * 128 : (i + 1) * 128] = sums_ref[(12 + i) * C : (13 + i) * C, :]
 
 
 def finish_kernel(
@@ -398,18 +419,20 @@
     return jnp.sum(parts.astype(F32), axis=0).astype(BF16)
 
 
-def summed_everywhere(sums):
+def summed_everywhere(sums, moved):
     near = lax.axis_size(NEAR)
     far = lax.axis_size(FAR)
     rows = sums.shape[0] // near
     padded = -(-rows // (8 * far)) * (8 * far)
-    part = total_of(exchange(sums.reshape(near, rows, 128), NEAR))
-    part = jnp.pad(part, ((0, padded - rows), (0, 0)))
+    part = exchange(sums.reshape(near, rows, 128), NEAR)
+    part, moved = lax.optimization_barrier((part, moved))
+    part = jnp.pad(total_of(part), ((0, padded - rows), (0, 0)))
     part = total_of(exchange(part.reshape(far, padded // far, 128), FAR))
     part = exchange(jnp.broadcast_to(part[None], (far,) + part.shape), FAR)
     part = part.reshape(padded, 128)[:rows]
+    part, moved = lax.optimization_barrier((part, moved))
     whole = exchange(jnp.broadcast_to(part[None], (near,) + part.shape), NEAR)
-    return whole.reshape(near * rows, 128)
+    return whole.reshape(near * rows, 128), moved
 
 
 def per_device(
@@ -425,12 +448,6 @@
     bias_index,
     merge_weight,
 ):
-    lat_limit = lax.axis_size(LAT) * ROWS - LAT_PAD
-    lat_info = jnp.stack([lax.axis_index(LAT), lat_limit]).astype(jnp.int32)
-    limits = jnp.left_shift(jnp.ones((4,), jnp.int32), bit_widths - 1) - 1
-    fan_in = jnp.array([1.0, 1.0, 1.0, math.sqrt(C / FF)], F32)
-    factors = fan_in / quant_scales.astype(F32)
-
     big = ROWS - OFF
     big_shape = (LEVS * big * SUB, 2 * C)
     thin_shape = (LEVS * OFF * SUB, 2 * C)
@@ -438,8 +455,7 @@
     own, lat_part, lon_part, diag_part = call(
         pack_kernel,
         pieces,
-        (tokens, cotangent),
-        [pltpu.VMEM((LEVS, ROWS, 16, 2 * C), F32)],
+        (tokens.transpose(1, 2, 0, 3), cotangent.transpose(1, 2, 0, 3)),
     )
     lon_part = shifted(lon_part, 0, 1)
     lat_part = shifted(lat_part, 1, 0)
@@ -451,49 +467,51 @@
             ((3, C, C), BF16),
             ((C, C), BF16),
             ((C, FF), BF16),
-            ((FF, C), BF16),
+            ((C, FF), BF16),
             ((4, STACK, 128), BF16),
         ],
         (
-            lat_info,
-            limits,
-            factors,
+            bit_widths,
+            quant_scales,
             bias_index.reshape(WTOK, WTOK),
-            bias_table,
+            bias_table.transpose(1, 2, 0, 3).reshape(HEADS, 2, POS),
             qkv_codes,
             proj_codes,
             up_codes,
-            down_codes,
+            down_codes.T,
         ),
-        [pltpu.VMEM((CHUNKS, 16, 128), F32)],
-        scalars=3,
+        [
+            pltpu.VMEM((HIGHS * 16, LOWS), F32),
+            pltpu.VMEM((2, LEVS * BLOCK, 128), F32),
+            pltpu.VMEM((LEVS * BLOCK, 16, 128), F32),
+        ],
+        scalars=2,
         flops=2_000_000_000,
     )
     own, lat_part, lon_part, diag_part, sums = call(
         main_kernel,
         pieces + [((18 * C, 128), BF16)],
-        (lat_info, own, lat_part, lon_part, diag_part, w_qkv, w_proj, w_up, w_down, bias),
+        (own, lat_part, lon_part, diag_part, w_qkv, w_proj, w_up, w_down, bias),
         [pltpu.VMEM((LEVS, ROWS, 2, SUB, 2 * C), F32)],
-        scalars=1,
         flops=2_000_000_000,
     )
     lon_part = shifted(lon_part, 0, -1)
     lat_part = shifted(lat_part, -1, 0)
     diag_part = shifted(diag_part, -1, -1)
-    whole = summed_everywhere(sums)
+    whole, moved = summed_everywhere(sums, (own, lat_part, lon_part, diag_part))
     merged, grad_tokens = call(
         finish_kernel,
         [((LEVS, ROWS // 2, COLS // 2, 2 * C), BF16), ((LEVS, ROWS, COLS, C), BF16)],
-        (own, lat_part, lon_part, diag_part, merge_weight),
+        (*moved, merge_weight),
         [pltpu.VMEM((LEVS, ROWS, 2, SUB, 2 * C), F32)],
         flops=400_000_000,
     )
-    grads = call(
+    qkv, proj, up, down = call(
         spread_kernel,
-        [((C, 3 * C), BF16), ((C, C), BF16), ((C, FF), BF16), ((FF, C), BF16)],
+        [((C, 3 * C), BF16), ((C, C), BF16), ((C, FF), BF16), ((C, FF), BF16)],
         (whole,),
     )
-    return (merged, grad_tokens, *grads)
+    return (merged, grad_tokens, qkv, proj, up, down.T)
 
 
 def solution(mesh):

time: 143 us -> 120 us (0.84)
  blocking collectives: 58.8 us -> 41.6 us
  Pallas kernels: 31.7 us -> 23 us
  waiting for transfers between devices: 11.3 us -> 18.5 us
  local copies, waits for them, and re-layouts: 14.4 us -> 7.23 us
  starting transfers between devices: 23.7 us -> 27.9 us
  other arithmetic: 1.87 us -> 0.19 us
    all_to_all x3 -> x2, blocking collectives: 58.8 us -> 41.6 us  [exchange(): return lax.all_to_all(parts, axes, 0, 0)]
    pallas_call x5, Pallas kernels: 31.7 us -> 23 us  [call(): pl.pallas_call(kernel, out_shape=[jax.ShapeDtypeStruct(s, t) for s, t in...]
    all_to_all x1 -> x2, waiting for transfers between devices: 0.01 us -> 7.22 us  [exchange(): return lax.all_to_all(parts, axes, 0, 0)]
    unnamed x41 -> x24, local copies, waits for them, and re-layouts: 12.5 us -> 5.36 us
    all_to_all x1 -> x2, starting transfers between devices: 7.02 us -> 11.2 us  [exchange(): return lax.all_to_all(parts, axes, 0, 0)]
  transfers between devices with their start and end apart: 7 -> 8, of which waited for: 2 -> 3; matrix products, arithmetic and copies ran while one was open for 5% -> 3% of each run, Pallas kernels for 13% -> 8%
where the time goes in v2:
time: 120 us; the launch traced here: 119 us
  blocking collectives  41.6 us (35%)
  starting transfers between devices  27.9 us (23%)
  Pallas kernels  23 us (19%)
  waiting for transfers between devices  18.5 us (15%)
  local copies, waits for them, and re-layouts  7.23 us (6%)
    all_to_all x2, blocking collectives, exchange(): return lax.all_to_all(parts, axes, 0, 0)  41.6 us
    pallas_call x5, Pallas kernels, call(): pl.pallas_call(kernel, out_shape=[jax.ShapeDtypeStruct(s, t) for s, t in...  23 us
    all_to_all x2, starting transfers between devices, exchange(): return lax.all_to_all(parts, axes, 0, 0)  11.2 us
    ppermute x2, waiting for transfers between devices, shifted(): return lax.ppermute(block, LAT, route)  9.21 us
    all_to_all x2, waiting for transfers between devices, exchange(): return lax.all_to_all(parts, axes, 0, 0)  7.22 us
    ppermute x2, starting transfers between devices, shifted(): return lax.ppermute(block, LON + LAT, route)  6.87 us
    unnamed x24, local copies, waits for them, and re-layouts  5.36 us
    ppermute x2, starting transfers between devices, shifted(): return lax.ppermute(block, LAT, route)  5.23 us
  transfers between devices with their start and end apart: 8, of which 3 were waited for; matrix products, arithmetic and copies ran while one was open for 3% of the time, Pallas kernels for 8%

profile of v2, /device:TPU:1, one launch (start us, length us, event | category | flops | bytes accessed | tf_op | source)
XLA Modules:
  0.0 119.2 jit_solution(4161683392539740013)
XLA Ops:
  0.6 0.0 copy-start.1
  0.6 2.1 %shard_map.154 = (bf16[144,384]{1,0:T(8,128)(2,1)}, bf16[48,384]{1,0:T(8,128)(2,1)}, bf16[144,384]{1,0:T(8,128)(2,1)}, bf16[48,384]{1,0:T(8,128)(2,1)}) custom-call(bf16[12,12,2,192]{3,2,1,0:T(2,128)(2,1)} %bitcast.15, bf16[12,12,2,192]{3,2,1,0:T(2,128)(2,1)} %bitcast.16), custom_call_target="tpu_custom_call" | custom-call | bytes 516096 | tf_op jit(solution)/shard_map/pallas_call | solution.py:386
  2.8 3.9 %collective-permute-start = (bf16[48,384]{1,0:T(8,128)(2,1)}, bf16[48,384]{1,0:T(8,128)(2,1)S(1)}, u32[]{:S(2)}, u32[]{:S(2)}) collective-permute-start(bf16[48,384]{1,0:T(8,128)(2,1)} %get-tuple-element.37), channel_id=1, source_target_pairs={{0,1},{1,2},{2,3},{3,4},{4,5},{5,6},{6,7},{7,8},{8,9},{9,10},{10,1... | collective-permute-start | bytes 110600 | tf_op jit(solution)/shard_map/ppermute | solution.py:410
  6.7 5.6 %collective-permute-start.2 = (bf16[48,384]{1,0:T(8,128)(2,1)}, bf16[48,384]{1,0:T(8,128)(2,1)S(1)}, u32[]{:S(2)}, u32[]{:S(2)}) collective-permute-start(bf16[48,384]{1,0:T(8,128)(2,1)} %get-tuple-element.39), channel_id=1, source_target_pairs={{0,17},{1,18},{2,19},{3,20},{4,21},{5,22},{6,23},{7,24},{8,25},{9,... | collective-permute-start | bytes 110600 | tf_op jit(solution)/shard_map/ppermute | solution.py:407
  12.3 2.5 %collective-permute-start.1 = (bf16[144,384]{1,0:T(8,128)(2,1)}, bf16[144,384]{1,0:T(8,128)(2,1)S(1)}, u32[]{:S(2)}, u32[]{:S(2)}) collective-permute-start(bf16[144,384]{1,0:T(8,128)(2,1)} %get-tuple-element.38), channel_id=1, source_target_pairs={{0,16},{16,32},{32,48},{48,64},{64,80},{80,96},{96,112},{112,128},... | collective-permute-start | bytes 331784 | tf_op jit(solution)/shard_map/ppermute | solution.py:411
  14.8 0.0 copy-done.1
  14.8 0.8 reshape.31.idx_ref
  15.6 6.9 %shard_map.155 = (bf16[3,192,192]{2,1,0:T(8,128)(2,1)}, bf16[192,192]{1,0:T(8,128)(2,1)}, bf16[192,768]{1,0:T(8,128)(2,1)}, bf16[192,768]{1,0:T(8,128)(2,1)}, bf16[4,576,128]{2,1,0:T(8,128)(2,1)}) custom-call(s32[4]{0:T(128)} %bits_ref.1, s32[4]{0:T(128)} %scale_ref.1, s32[144,144]{1,0:T(8,128)} %reshape.31.idx_ref, bf16[6,2,3312]{2,1,0:T(2,128)(2,1)} %bitcast.19, ...), custom_call_target="tpu_custom_call" | custom-call | flops 2000000000 | bytes 3406496 | tf_op jit(solution)/shard_map/pallas_call | solution.py:386
  22.5 0.0 collective-permute-done.lat_part_ref
  22.5 0.0 copy-start.7
  22.5 0.0 collective-permute-done.2.diag_part_ref
  22.5 0.0 copy-start.8
  22.5 0.0 collective-permute-done.1.lon_part_ref
  22.5 0.0 copy-start.4
  22.5 0.6 copy-done.7
  23.1 0.0 copy-done.8
  23.1 0.1 copy-done.4
  23.2 8.9 %shard_map.156 = (bf16[144,384]{1,0:T(8,128)(2,1)}, bf16[48,384]{1,0:T(8,128)(2,1)}, bf16[144,384]{1,0:T(8,128)(2,1)}, bf16[48,384]{1,0:T(8,128)(2,1)}, bf16[3456,128]{1,0:T(8,128)(2,1)}) custom-call(bf16[144,384]{1,0:T(8,128)(2,1)} %get-tuple-element.36.own_ref, bf16[48,384]{1,0:T(8,128)(2,1)} %copy-done.7, bf16[144,384]{1,0:T(8,128)(2,1)} %copy-done.4, ...), custom_call_target="tpu_custom_call" | custom-call | flops 2000000000 | bytes 2949120 | tf_op jit(solution)/shard_map/pallas_call | solution.py:386
  32.1 0.0 copy-start.3
  32.1 0.0 copy-start.10
  32.1 0.0 copy-start.9
  32.1 4.9 %all-to-all-start = ((bf16[8,432,128]{2,1,0:T(8,128)(2,1)}), bf16[8,432,128]{2,1,0:T(8,128)(2,1)S(1)}, u32[]{:S(2)}, u32[]{:S(2)}) async-start(bf16[8,432,128]{2,1,0:T(8,128)(2,1)} %bitcast.14), calls=%async_computation | async-start | bytes 1769472 | tf_op jit(solution)/shard_map/all_to_all | solution.py:415
  37.0 0.0 copy-done.3
  37.0 2.0 %collective-permute-start.4 = (bf16[144,384]{1,0:T(8,128)(2,1)S(1)}, bf16[144,384]{1,0:T(8,128)(2,1)S(1)}, u32[]{:S(2)}, u32[]{:S(2)}) collective-permute-start(bf16[144,384]{1,0:T(8,128)(2,1)S(1)} %copy-done.3), channel_id=1, source_target_pairs={{0,496},{16,0},{32,16},{48,32},{64,48},{80,64},{96,80},{112,96},{1... | collective-permute-start | bytes 331784 | tf_op jit(solution)/shard_map/ppermute | solution.py:411
  39.0 0.0 copy-done.10
  39.1 1.3 %collective-permute-start.3 = (bf16[48,384]{1,0:T(8,128)(2,1)S(1)}, bf16[48,384]{1,0:T(8,128)(2,1)S(1)}, u32[]{:S(2)}, u32[]{:S(2)}) collective-permute-start(bf16[48,384]{1,0:T(8,128)(2,1)S(1)} %copy-done.10), channel_id=1, source_target_pairs={{1,0},{2,1},{3,2},{4,3},{5,4},{6,5},{7,6},{8,7},{9,8},{10,9},{11,1... | collective-permute-start | bytes 110600 | tf_op jit(solution)/shard_map/ppermute | solution.py:410
  40.4 0.0 copy-done.9
  40.4 1.3 %collective-permute-start.5 = (bf16[48,384]{1,0:T(8,128)(2,1)S(1)}, bf16[48,384]{1,0:T(8,128)(2,1)S(1)}, u32[]{:S(2)}, u32[]{:S(2)}) collective-permute-start(bf16[48,384]{1,0:T(8,128)(2,1)S(1)} %copy-done.9), channel_id=1, source_target_pairs={{1,496},{2,497},{3,498},{4,499},{5,500},{6,501},{7,502},{8,503},{9... | collective-permute-start | bytes 110600 | tf_op jit(solution)/shard_map/ppermute | solution.py:407
  41.7 9.2 %collective-permute-done.3.lat_ref = bf16[48,384]{1,0:T(8,128)(2,1)S(1)} collective-permute-done((bf16[48,384]{1,0:T(8,128)(2,1)S(1)}, bf16[48,384]{1,0:T(8,128)(2,1)S(1)}, u32[]{:S(2)}, u32[]{:S(2)}) %collective-permute-start.3) | collective-permute-done | bytes 36896 | tf_op jit(solution)/shard_map/ppermute | solution.py:410
  50.9 0.0 copy-start.5
  50.9 0.0 collective-permute-done.5.diag_ref
  50.9 2.1 %collective-permute-done.4.lon_ref = bf16[144,384]{1,0:T(8,128)(2,1)S(1)} collective-permute-done((bf16[144,384]{1,0:T(8,128)(2,1)S(1)}, bf16[144,384]{1,0:T(8,128)(2,1)S(1)}, u32[]{:S(2)}, u32[]{:S(2)}) %collective-permute-start.4) | collective-permute-done | bytes 110624 | tf_op jit(solution)/shard_map/ppermute | solution.py:411
  53.0 0.0 all-to-all-done
  53.0 0.1 reduce_sum.24
  53.1 0.0 copy-done.5
  53.1 0.0 copy-done.6
  53.1 0.5 copy-done.2
  53.6 26.0 %all_to_all.20 = bf16[64,8,128]{2,1,0:T(8,128)(2,1)S(1)} all-to-all(bf16[64,8,128]{2,1,0:T(8,128)(2,1)S(1)} %pad_bitcast_fusion), channel_id=1, replica_groups=mesh['z'=8,'xh'=2,'c'=2,'y'=8,'xl'=2] {'y','z'}, dimensions={0} | all-to-all | bytes 262144 | tf_op jit(solution)/shard_map/all_to_all | solution.py:415
  79.6 0.1 reduce_sum.25
  79.7 15.6 %all_to_all.21 = bf16[64,8,128]{2,1,0:T(8,128)(2,1)S(1)} all-to-all(bf16[64,8,128]{2,1,0:T(8,128)(2,1)S(1)} %broadcast_in_dim.4), channel_id=1, replica_groups=mesh['z'=8,'xh'=2,'c'=2,'y'=8,'xl'=2] {'y','z'}, dimensions={0} | all-to-all | bytes 262144 | tf_op jit(solution)/shard_map/all_to_all | solution.py:415
  95.3 1.0 broadcast_in_dim.5
  96.3 6.3 %all-to-all-start.3 = ((bf16[8,432,128]{2,1,0:T(8,128)(2,1)}), bf16[8,432,128]{2,1,0:T(8,128)(2,1)S(1)}, u32[]{:S(2)}, u32[]{:S(2)}) async-start(bf16[8,432,128]{2,1,0:T(8,128)(2,1)} %broadcast_in_dim.5), calls=%async_computation.3 | async-start | bytes 1769472 | tf_op jit(solution)/shard_map/all_to_all | solution.py:415
  102.6 2.9 %shard_map.157 = (bf16[2,6,6,384]{3,2,1,0:T(8,128)(2,1)}, bf16[2,12,12,192]{3,2,1,0:T(8,128)(2,1)}) custom-call(bf16[144,384]{1,0:T(8,128)(2,1)} %get-tuple-element.55.own_ref, bf16[48,384]{1,0:T(8,128)(2,1)} %copy-done.5, bf16[144,384]{1,0:T(8,128)(2,1)} %copy-done.2, bf16[48,384]{1,0:T(8,128)(2,1)} %copy-done.6, bf16[768,384]{1,0:T(8,128)(2,1)} %weight_ref.1), custom_call_target="tpu_custom_call" | custom-call | flops 400000000 | bytes 1050624 | tf_op jit(solution)/shard_map/pallas_call | solution.py:386
  105.5 1.5 %copy.19 = bf16[2,6,6,384]{3,0,2,1:T(2,128)(2,1)} copy(bf16[2,6,6,384]{3,2,1,0:T(8,128)(2,1)} %get-tuple-element.72) | data formatting | bytes 110592
  107.1 1.7 %copy.20 = bf16[2,12,12,192]{3,0,2,1:T(2,128)(2,1)} copy(bf16[2,12,12,192]{3,2,1,0:T(8,128)(2,1)} %get-tuple-element.73) | data formatting | bytes 221184
  108.8 7.2 %all-to-all-done.3 = bf16[8,432,128]{2,1,0:T(8,128)(2,1)S(1)} async-done(((bf16[8,432,128]{2,1,0:T(8,128)(2,1)}), bf16[8,432,128]{2,1,0:T(8,128)(2,1)S(1)}, u32[]{:S(2)}, u32[]{:S(2)}) %all-to-all-start.3) | async-done | bytes 884768 | tf_op jit(solution)/shard_map/all_to_all | solution.py:415
  116.0 0.9 copy-done
  117.0 2.2 %shard_map.158 = (bf16[192,576]{1,0:T(8,128)(2,1)}, bf16[192,192]{1,0:T(8,128)(2,1)}, bf16[192,768]{1,0:T(8,128)(2,1)}, bf16[192,768]{1,0:T(8,128)(2,1)}) custom-call(bf16[3456,128]{1,0:T(8,128)(2,1)} %bitcast.13), custom_call_target="tpu_custom_call" | custom-call | bytes 1769472 | tf_op jit(solution)/shard_map/pallas_call | solution.py:386
  (6 shorter events, 0.0 us)
Async XLA Ops:
  0.6 14.2 %copy-start.1 = (s32[20736]{0:T(1024)S(1)}, s32[20736]{0:T(1024)}, u32[]{:S(2)}) copy-start(s32[20736]{0:T(1024)} %param.20) | copy-start | bytes 248836
  2.8 19.7 %collective-permute-start = (bf16[48,384]{1,0:T(8,128)(2,1)}, bf16[48,384]{1,0:T(8,128)(2,1)S(1)}, u32[]{:S(2)}, u32[]{:S(2)}) collective-permute-start(bf16[48,384]{1,0:T(8,128)(2,1)} %get-tuple-element.37), channel_id=1, source_target_pairs={{0,1},{1,2},{2,3},{3,4},{4,5},{5,6},{6,7},{7,8},{8,9},{9,10},{10,1... | collective-permute-start | bytes 110600 | tf_op jit(solution)/shard_map/ppermute | solution.py:410
  6.7 15.8 %collective-permute-start.2 = (bf16[48,384]{1,0:T(8,128)(2,1)}, bf16[48,384]{1,0:T(8,128)(2,1)S(1)}, u32[]{:S(2)}, u32[]{:S(2)}) collective-permute-start(bf16[48,384]{1,0:T(8,128)(2,1)} %get-tuple-element.39), channel_id=1, source_target_pairs={{0,17},{1,18},{2,19},{3,20},{4,21},{5,22},{6,23},{7,24},{8,25},{9,... | collective-permute-start | bytes 110600 | tf_op jit(solution)/shard_map/ppermute | solution.py:407
  12.3 10.2 %collective-permute-start.1 = (bf16[144,384]{1,0:T(8,128)(2,1)}, bf16[144,384]{1,0:T(8,128)(2,1)S(1)}, u32[]{:S(2)}, u32[]{:S(2)}) collective-permute-start(bf16[144,384]{1,0:T(8,128)(2,1)} %get-tuple-element.38), channel_id=1, source_target_pairs={{0,16},{16,32},{32,48},{48,64},{64,80},{80,96},{96,112},{112,128},... | collective-permute-start | bytes 331784 | tf_op jit(solution)/shard_map/ppermute | solution.py:411
  22.5 0.6 copy-start.7
  22.5 0.6 copy-start.8
  22.5 0.6 copy-start.4
  32.1 5.0 %copy-start.3 = (bf16[144,384]{1,0:T(8,128)(2,1)S(1)}, bf16[144,384]{1,0:T(8,128)(2,1)}, u32[]{:S(2)}) copy-start(bf16[144,384]{1,0:T(8,128)(2,1)} %get-tuple-element.48) | copy-start | bytes 331780
  32.1 7.0 %copy-start.10 = (bf16[48,384]{1,0:T(8,128)(2,1)S(1)}, bf16[48,384]{1,0:T(8,128)(2,1)}, u32[]{:S(2)}) copy-start(bf16[48,384]{1,0:T(8,128)(2,1)} %get-tuple-element.47) | copy-start | bytes 110596
  32.1 8.3 %copy-start.9 = (bf16[48,384]{1,0:T(8,128)(2,1)S(1)}, bf16[48,384]{1,0:T(8,128)(2,1)}, u32[]{:S(2)}) copy-start(bf16[48,384]{1,0:T(8,128)(2,1)} %get-tuple-element.49) | copy-start | bytes 110596
  32.1 20.9 %all-to-all-start = ((bf16[8,432,128]{2,1,0:T(8,128)(2,1)}), bf16[8,432,128]{2,1,0:T(8,128)(2,1)S(1)}, u32[]{:S(2)}, u32[]{:S(2)}) async-start(bf16[8,432,128]{2,1,0:T(8,128)(2,1)} %bitcast.14), calls=%async_computation | async-start | bytes 1769472 | tf_op jit(solution)/shard_map/all_to_all | solution.py:415
  37.0 16.0 %collective-permute-start.4 = (bf16[144,384]{1,0:T(8,128)(2,1)S(1)}, bf16[144,384]{1,0:T(8,128)(2,1)S(1)}, u32[]{:S(2)}, u32[]{:S(2)}) collective-permute-start(bf16[144,384]{1,0:T(8,128)(2,1)S(1)} %copy-done.3), channel_id=1, source_target_pairs={{0,496},{16,0},{32,16},{48,32},{64,48},{80,64},{96,80},{112,96},{1... | collective-permute-start | bytes 331784 | tf_op jit(solution)/shard_map/ppermute | solution.py:411
  39.1 11.8 %collective-permute-start.3 = (bf16[48,384]{1,0:T(8,128)(2,1)S(1)}, bf16[48,384]{1,0:T(8,128)(2,1)S(1)}, u32[]{:S(2)}, u32[]{:S(2)}) collective-permute-start(bf16[48,384]{1,0:T(8,128)(2,1)S(1)} %copy-done.10), channel_id=1, source_target_pairs={{1,0},{2,1},{3,2},{4,3},{5,4},{6,5},{7,6},{8,7},{9,8},{10,9},{11,1... | collective-permute-start | bytes 110600 | tf_op jit(solution)/shard_map/ppermute | solution.py:410
  40.4 10.5 %collective-permute-start.5 = (bf16[48,384]{1,0:T(8,128)(2,1)S(1)}, bf16[48,384]{1,0:T(8,128)(2,1)S(1)}, u32[]{:S(2)}, u32[]{:S(2)}) collective-permute-start(bf16[48,384]{1,0:T(8,128)(2,1)S(1)} %copy-done.9), channel_id=1, source_target_pairs={{1,496},{2,497},{3,498},{4,499},{5,500},{6,501},{7,502},{8,503},{9... | collective-permute-start | bytes 110600 | tf_op jit(solution)/shard_map/ppermute | solution.py:407
  50.9 2.2 %copy-start.5 = (bf16[48,384]{1,0:T(8,128)(2,1)}, bf16[48,384]{1,0:T(8,128)(2,1)S(1)}, u32[]{:S(2)}) copy-start(bf16[48,384]{1,0:T(8,128)(2,1)S(1)} %collective-permute-done.3.lat_ref) | copy-start | bytes 110596
  50.9 2.2 %copy-start.6 = (bf16[48,384]{1,0:T(8,128)(2,1)}, bf16[48,384]{1,0:T(8,128)(2,1)S(1)}, u32[]{:S(2)}) copy-start(bf16[48,384]{1,0:T(8,128)(2,1)S(1)} %collective-permute-done.5.diag_ref) | copy-start | bytes 110596
  53.0 0.6 copy-start.2
  96.3 19.7 %all-to-all-start.3 = ((bf16[8,432,128]{2,1,0:T(8,128)(2,1)}), bf16[8,432,128]{2,1,0:T(8,128)(2,1)S(1)}, u32[]{:S(2)}, u32[]{:S(2)}) async-start(bf16[8,432,128]{2,1,0:T(8,128)(2,1)} %broadcast_in_dim.5), calls=%async_computation.3 | async-start | bytes 1769472 | tf_op jit(solution)/shard_map/all_to_all | solution.py:415
  116.0 0.9 copy-start

commit v3 on v2

--- a/solution.py
+++ b/solution.py
@@ -27,6 +27,8 @@
 FRAME = LEVS * ROWS * 2 * SUB
 BLOCK = FRAME // 4
 STACK = HEADS * BLOCK
+BIG = LEVS * (ROWS - OFF) * SUB
+THIN = LEVS * OFF * SUB
 LOWS = 256
 HIGHS = -(-POS // LOWS)
 
@@ -34,7 +36,6 @@
 MASKED = -1000000000.0
 F32 = jnp.float32
 BF16 = jnp.bfloat16
-VMEM_LIMIT = 56 * 1024 * 1024
 
 LAT = ("y", "xl")
 LON = ("z", "xh", "c")
@@ -58,7 +59,7 @@
     return lax.dot_general(left, right, (((0,), (0,)), ((), ())), preferred_element_type=F32)
 
 
-def pack_kernel(tok_ref, cot_ref, own_ref, lat_ref, lon_ref, diag_ref):
+def pack_kernel(tok_ref, cot_ref, own_ref, low_ref, side_ref):
     both = jnp.concatenate(
         [ref[...].astype(F32).reshape(LEVS * ROWS * COLS, C) for ref in (tok_ref, cot_ref)], axis=-1
     ).astype(BF16)
@@ -73,28 +74,13 @@
         return product(hot.astype(F32).astype(BF16), both).astype(BF16)
 
     own_ref[...] = pick(0, ROWS - OFF, 0)
-    lat_ref[...] = pick(ROWS - OFF, OFF, 0)
-    lon_ref[...] = pick(0, ROWS - OFF, HALF)
-    diag_ref[...] = pick(ROWS - OFF, OFF, HALF)
-
-
-def prep_kernel(
-    bits_ref,
-    scale_ref,
-    idx_ref,
-    tab_ref,
-    cq_ref,
-    cp_ref,
-    cu_ref,
-    cd_ref,
-    wq_ref,
-    wp_ref,
-    wu_ref,
-    wd_ref,
-    bias_ref,
-    rows,
-    places,
-    found,
+    low_ref[...] = pick(ROWS - OFF, OFF, 0)
+    side_ref[0:BIG, :] = pick(0, ROWS - OFF, HALF)
+    side_ref[BIG:, :] = pick(ROWS - OFF, OFF, HALF)
+
+
+def weight_kernel(
+    bits_ref, scale_ref, cq_ref, cp_ref, cu_ref, cd_ref, wq_ref, wp_ref, wu_ref, wd_ref
 ):
     def dequant(codes, layer, fan_in):
         limit = jnp.left_shift(1, bits_ref[layer] - 1) - 1
@@ -109,6 +95,8 @@
     wu_ref[...] = dequant(cu_ref[...], 2, C).astype(BF16)
     wd_ref[...] = dequant(cd_ref[...], 3, FF).astype(BF16)
 
+
+def bias_kernel(idx_ref, tab_ref, bias_ref, rows, places, found):
     rows[...] = jnp.zeros_like(rows)
     for head in range(HEADS):
         table = tab_ref[head].astype(F32)
@@ -186,30 +174,28 @@
 
 def main_kernel(
     own_ref,
-    lat_part_ref,
-    lon_part_ref,
-    diag_part_ref,
+    side_ref,
+    edge_ref,
     wq_ref,
     wp_ref,
     wu_ref,
     wd_ref,
     bias_ref,
     own_out,
-    lat_out,
-    lon_out,
-    diag_out,
+    side_out,
+    edge_out,
     sums_ref,
     frame,
 ):
     below = ROWS - OFF
 
-    def piece(ref, rows):
-        return ref[...].astype(F32).reshape(LEVS, rows, SUB, 2 * C)
-
-    frame[:, OFF:, 1] = piece(own_ref, below)
-    frame[:, :OFF, 1] = piece(lat_part_ref, OFF)
-    frame[:, OFF:, 0] = piece(lon_part_ref, below)
-    frame[:, :OFF, 0] = piece(diag_part_ref, OFF)
+    def piece(block, rows):
+        return block.astype(F32).reshape(LEVS, rows, SUB, 2 * C)
+
+    frame[:, OFF:, 1] = piece(own_ref[...], below)
+    frame[:, OFF:, 0] = piece(side_ref[0:BIG, :], below)
+    frame[:, :OFF, 1] = piece(edge_ref[0:THIN, :], OFF)
+    frame[:, :OFF, 0] = piece(edge_ref[THIN:, :], OFF)
     both = frame[...].reshape(FRAME, 2 * C)
 
     place = iota((FRAME, C), 0)
@@ -298,9 +284,9 @@
         return part.reshape(-1, 2 * C).astype(BF16)
 
     own_out[...] = flat(result[:, OFF:, 1])
-    lat_out[...] = flat(result[:, :OFF, 1])
-    lon_out[...] = flat(result[:, OFF:, 0])
-    diag_out[...] = flat(result[:, :OFF, 0])
+    side_out[...] = flat(result[:, OFF:, 0])
+    edge_out[0:THIN, :] = flat(result[:, :OFF, 1])
+    edge_out[THIN:, :] = flat(result[:, :OFF, 0])
 
     small = [
         crossed(normed, d_query),
@@ -331,18 +317,16 @@
         down_ref[:, i * 128 : (i + 1) * 128] = sums_ref[(12 + i) * C : (13 + i) * C, :]
 
 
-def finish_kernel(
-    own_ref, lat_ref, lon_ref, diag_ref, weight_ref, merged_ref, grad_ref, frame
-):
+def finish_kernel(own_ref, edge_ref, side_ref, weight_ref, merged_ref, grad_ref, frame):
     above = ROWS - OFF
 
-    def piece(ref, rows):
-        return ref[...].astype(F32).reshape(LEVS, rows, SUB, 2 * C)
-
-    frame[:, :above, 0] = piece(own_ref, above)
-    frame[:, above:, 0] = piece(lat_ref, OFF)
-    frame[:, :above, 1] = piece(lon_ref, above)
-    frame[:, above:, 1] = piece(diag_ref, OFF)
+    def piece(block, rows):
+        return block.astype(F32).reshape(LEVS, rows, SUB, 2 * C)
+
+    frame[:, :above, 0] = piece(own_ref[...], above)
+    frame[:, above:, 0] = piece(edge_ref[0:THIN, :], OFF)
+    frame[:, :above, 1] = piece(side_ref[0:BIG, :], above)
+    frame[:, above:, 1] = piece(side_ref[BIG:, :], OFF)
     both = frame[...].reshape(FRAME, 2 * C)
     final = both[:, :C].astype(BF16)
     grad = both[:, C:].astype(BF16)
@@ -378,7 +362,7 @@
     merged_ref[...] = total.reshape(LEVS, ROWS // 2, SUB, 2 * C)[:, :, :HALF, :].astype(BF16)
 
 
-def call(kernel, outs, args, scratch=(), scalars=0, flops=0):
+def call(kernel, outs, args, scratch=(), scalars=0, flops=0, mib=16):
     vmem = pl.BlockSpec(memory_space=pltpu.VMEM)
     smem = pl.BlockSpec(memory_space=pltpu.SMEM)
     moved = sum(math.prod(a.shape) * a.dtype.itemsize for a in args)
@@ -389,26 +373,18 @@
         in_specs=[smem] * scalars + [vmem] * (len(args) - scalars),
         out_specs=[vmem] * len(outs),
         scratch_shapes=list(scratch),
-        compiler_params=pltpu.CompilerParams(vmem_limit_bytes=VMEM_LIMIT),
+        compiler_params=pltpu.CompilerParams(vmem_limit_bytes=mib * 1024 * 1024),
         cost_estimate=pl.CostEstimate(flops=flops, bytes_accessed=moved, transcendentals=0),
     )(*args)
 
 
-def shifted(block, lat_step, lon_step):
-    rows = lax.axis_size(LAT)
-    cols = lax.axis_size(LON)
-    if lat_step and lon_step:
-        route = [
-            (col * rows + row, (col + lon_step) % cols * rows + row + lat_step)
-            for col in range(cols)
-            for row in range(rows)
-            if 0 <= row + lat_step < rows
-        ]
-        return lax.ppermute(block, LON + LAT, route)
-    if lat_step:
-        route = [(r, r + lat_step) for r in range(rows) if 0 <= r + lat_step < rows]
-        return lax.ppermute(block, LAT, route)
-    return lax.ppermute(block, LON, [(c, (c + lon_step) % cols) for c in range(cols)])
+def shifted(block, axes, step):
+    count = lax.axis_size(axes)
+    if axes == LAT:
+        route = [(i, i + step) for i in range(count) if 0 <= i + step < count]
+    else:
+        route = [(i, (i + step) % count) for i in range(count)]
+    return lax.ppermute(block, axes, route)
 
 
 def exchange(parts, axes):
@@ -419,19 +395,30 @@
     return jnp.sum(parts.astype(F32), axis=0).astype(BF16)
 
 
-def summed_everywhere(sums, moved):
+def copies(part, count):
+    def kernel(part_ref, out_ref):
+        for i in range(count):
+            out_ref[i] = part_ref[...]
+
+    return call(kernel, [((count,) + part.shape, BF16)], (part,))[0]
+
+
+def summed_everywhere(sums, own, edge, side):
     near = lax.axis_size(NEAR)
     far = lax.axis_size(FAR)
     rows = sums.shape[0] // near
     padded = -(-rows // (8 * far)) * (8 * far)
+    edge = shifted(edge, LAT, -1)
     part = exchange(sums.reshape(near, rows, 128), NEAR)
-    part, moved = lax.optimization_barrier((part, moved))
+    part, edge = lax.optimization_barrier((part, edge))
+    side = shifted(jnp.concatenate([side, edge[THIN:]], axis=0), LON, -1)
     part = jnp.pad(total_of(part), ((0, padded - rows), (0, 0)))
-    part = total_of(exchange(part.reshape(far, padded // far, 128), FAR))
-    part = exchange(jnp.broadcast_to(part[None], (far,) + part.shape), FAR)
+    part = exchange(part.reshape(far, padded // far, 128), FAR)
+    part, side = lax.optimization_barrier((part, side))
+    part = exchange(jnp.broadcast_to(total_of(part)[None], part.shape), FAR)
     part = part.reshape(padded, 128)[:rows]
-    part, moved = lax.optimization_barrier((part, moved))
-    whole = exchange(jnp.broadcast_to(part[None], (near,) + part.shape), NEAR)
+    part, moved = lax.optimization_barrier((part, (own, edge, side)))
+    whole = exchange(copies(part, near), NEAR)
     return whole.reshape(near * rows, 128), moved
 
 
@@ -448,57 +435,52 @@
     bias_index,
     merge_weight,
 ):
-    big = ROWS - OFF
-    big_shape = (LEVS * big * SUB, 2 * C)
-    thin_shape = (LEVS * OFF * SUB, 2 * C)
-    pieces = [(big_shape, BF16), (thin_shape, BF16), (big_shape, BF16), (thin_shape, BF16)]
-    own, lat_part, lon_part, diag_part = call(
+    own, low, side = call(
         pack_kernel,
-        pieces,
+        [((BIG, 2 * C), BF16), ((THIN, 2 * C), BF16), ((BIG + THIN, 2 * C), BF16)],
         (tokens.transpose(1, 2, 0, 3), cotangent.transpose(1, 2, 0, 3)),
     )
-    lon_part = shifted(lon_part, 0, 1)
-    lat_part = shifted(lat_part, 1, 0)
-    diag_part = shifted(diag_part, 1, 1)
-
-    w_qkv, w_proj, w_up, w_down, bias = call(
-        prep_kernel,
-        [
-            ((3, C, C), BF16),
-            ((C, C), BF16),
-            ((C, FF), BF16),
-            ((C, FF), BF16),
-            ((4, STACK, 128), BF16),
-        ],
+    side = shifted(side, LON, 1)
+    (bias,) = call(
+        bias_kernel,
+        [((4, STACK, 128), BF16)],
         (
-            bit_widths,
-            quant_scales,
             bias_index.reshape(WTOK, WTOK),
             bias_table.transpose(1, 2, 0, 3).reshape(HEADS, 2, POS),
-            qkv_codes,
-            proj_codes,
-            up_codes,
-            down_codes.T,
         ),
         [
             pltpu.VMEM((HIGHS * 16, LOWS), F32),
             pltpu.VMEM((2, LEVS * BLOCK, 128), F32),
             pltpu.VMEM((LEVS * BLOCK, 16, 128), F32),
         ],
+        flops=2_000_000_000,
+    )
+    edge = jnp.concatenate([low, side[BIG:]], axis=0)
+    edge, bias, codes = lax.optimization_barrier(
+        (edge, bias, (qkv_codes, proj_codes, up_codes, down_codes.T))
+    )
+    edge = shifted(edge, LAT, 1)
+    weights = call(
+        weight_kernel,
+        [((3, C, C), BF16), ((C, C), BF16), ((C, FF), BF16), ((C, FF), BF16)],
+        (bit_widths, quant_scales, *codes),
         scalars=2,
-        flops=2_000_000_000,
-    )
-    own, lat_part, lon_part, diag_part, sums = call(
+        flops=1_000_000_000,
+    )
+    own, side, edge, sums = call(
         main_kernel,
-        pieces + [((18 * C, 128), BF16)],
-        (own, lat_part, lon_part, diag_part, w_qkv, w_proj, w_up, w_down, bias),
+        [
+            ((BIG, 2 * C), BF16),
+            ((BIG, 2 * C), BF16),
+            ((2 * THIN, 2 * C), BF16),
+            ((18 * C, 128), BF16),
+        ],
+        (own, side, edge, *weights, bias),
         [pltpu.VMEM((LEVS, ROWS, 2, SUB, 2 * C), F32)],
         flops=2_000_000_000,
-    )
-    lon_part = shifted(lon_part, 0, -1)
-    lat_part = shifted(lat_part, -1, 0)
-    diag_part = shifted(diag_part, -1, -1)
-    whole, moved = summed_everywhere(sums, (own, lat_part, lon_part, diag_part))
+        mib=32,
+    )
+    whole, moved = summed_everywhere(sums, own, edge, side)
     merged, grad_tokens = call(
         finish_kernel,
         [((LEVS, ROWS // 2, COLS // 2, 2 * C), BF16), ((LEVS, ROWS, COLS, C), BF16)],

time: 120 us -> 117 us (0.975)
  blocking collectives: 41.6 us -> 20 us
  waiting for transfers between devices: 18.5 us -> 33.3 us
  starting transfers between devices: 27.9 us -> 42.5 us
  Pallas kernels: 23 us -> 15.8 us
  local copies, waits for them, and re-layouts: 7.23 us -> 4.18 us
    all_to_all x2 -> x1, blocking collectives: 41.6 us -> 20 us  [exchange(): return lax.all_to_all(parts, axes, 0, 0)]
    all_to_all x2 -> x3, starting transfers between devices: 11.2 us -> 29.7 us  [exchange(): return lax.all_to_all(parts, axes, 0, 0)]
    all_to_all x2 -> x3, waiting for transfers between devices: 7.22 us -> 15.8 us  [exchange(): return lax.all_to_all(parts, axes, 0, 0)]
    pallas_call x5 -> x7, Pallas kernels: 23 us -> 15.8 us  [call(): pl.pallas_call(kernel, out_shape=[jax.ShapeDtypeStruct(s, t) for s, t in...]
    ppermute x6 -> x4, waiting for transfers between devices: 11.3 us -> 17.4 us  [shifted(): return lax.ppermute(block, axes, route)]
    ppermute x6 -> x4, starting transfers between devices: 16.6 us -> 12.9 us  [shifted(): return lax.ppermute(block, axes, route)]
    unnamed x24, local copies, waits for them, and re-layouts: 5.36 us -> 3.34 us
  transfers between devices with their start and end apart: 8 -> 7, of which waited for: 3 -> 6; matrix products, arithmetic and copies ran while one was open for 3% -> 1% of each run, Pallas kernels for 8% -> 5%
where the time goes in v3:
time: 117 us
  starting transfers between devices  42.5 us (36%)
  waiting for transfers between devices  33.3 us (28%)
  blocking collectives  20 us (17%)
  Pallas kernels  15.8 us (14%)
  local copies, waits for them, and re-layouts  4.18 us (4%)
    all_to_all x3, starting transfers between devices, exchange(): return lax.all_to_all(parts, axes, 0, 0)  29.7 us
    all_to_all x1, blocking collectives, exchange(): return lax.all_to_all(parts, axes, 0, 0)  20 us
    ppermute x4, waiting for transfers between devices, shifted(): return lax.ppermute(block, axes, route)  17.4 us
    all_to_all x3, waiting for transfers between devices, exchange(): return lax.all_to_all(parts, axes, 0, 0)  15.8 us
    pallas_call x7, Pallas kernels, call(): pl.pallas_call(kernel, out_shape=[jax.ShapeDtypeStruct(s, t) for s, t in...  15.8 us
    ppermute x4, starting transfers between devices, shifted(): return lax.ppermute(block, axes, route)  12.9 us
    unnamed x24, local copies, waits for them, and re-layouts  3.34 us
  transfers between devices with their start and end apart: 7, of which 6 were waited for; matrix products, arithmetic and copies ran while one was open for 1% of the time, Pallas kernels for 5%

profile of v3, /device:TPU:1, one launch (start us, length us, event | category | flops | bytes accessed | tf_op | source)
XLA Modules:
  0.0 116.9 jit_solution(14081793218256709149)
XLA Ops:
  0.6 0.0 copy-start
  0.6 0.9 copy-done
  1.5 0.0 copy-start.1
  1.5 0.9 copy-done.1
  2.5 0.5 shard_map.154
  3.0 0.0 copy-start.7
  3.0 6.2 %collective-permute-start = (bf16[192,384]{1,0:T(8,128)(2,1)S(1)}, bf16[192,384]{1,0:T(8,128)(2,1)S(1)}, u32[]{:S(2)}, u32[]{:S(2)}) collective-permute-start(bf16[192,384]{1,0:T(8,128)(2,1)S(1)} %get-tuple-element.38), channel_id=1, source_target_pairs={{0,16},{16,32},{32,48},{48,64},{64,80},{80,96},{96,112},{112,128},... | collective-permute-start | bytes 442376 | tf_op jit(solution)/shard_map/ppermute | solution.py:387
  9.2 0.0 copy-done.10
  9.2 0.1 reshape.30.idx_ref
  9.3 0.0 copy-done.7
  9.3 0.0 copy-start.2
  9.3 0.0 copy-start.3
  9.3 0.0 copy-start.5
  9.3 3.7 %shard_map.155.bias_ref = bf16[4,576,128]{2,1,0:T(8,128)(2,1)S(1)} custom-call(s32[144,144]{1,0:T(8,128)S(1)} %reshape.30.idx_ref, bf16[6,2,3312]{2,1,0:T(2,128)(2,1)S(1)} %bitcast.17), custom_call_target="tpu_custom_call" | custom-call | flops 2000000000 | bytes 752256 | tf_op jit(solution)/shard_map/pallas_call | solution.py:370
  13.0 0.0 copy-start.6
  13.0 0.0 collective-permute-done.side_ref
  13.1 0.0 copy-start.8
  13.1 0.0 copy-start.9
  13.1 2.4 %collective-permute-start.1 = (bf16[96,384]{1,0:T(8,128)(2,1)S(1)}, bf16[96,384]{1,0:T(8,128)(2,1)S(1)}, u32[]{:S(2)}, u32[]{:S(2)}) collective-permute-start(bf16[96,384]{1,0:T(8,128)(2,1)S(1)} %pad_maximum_fusion.1), channel_id=1, source_target_pairs={{0,1},{1,2},{2,3},{3,4},{4,5},{5,6},{6,7},{7,8},{8,9},{9,10},{10,1... | collective-permute-start | bytes 221192 | tf_op jit(solution)/shard_map/ppermute | solution.py:387
  15.4 0.0 copy-done.2
  15.5 0.0 copy-done.3
  15.5 0.0 copy-done.5
  15.5 0.0 copy-done.6
  15.5 0.0 copy-done.8
  15.5 0.0 copy-done.9
  15.5 1.1 shard_map.156
  16.6 0.2 collective-permute-done.1.edge_ref
  16.8 7.4 %shard_map.157 = (bf16[144,384]{1,0:T(8,128)(2,1)S(1)}, bf16[144,384]{1,0:T(8,128)(2,1)S(1)}, bf16[96,384]{1,0:T(8,128)(2,1)S(1)}, bf16[3456,128]{1,0:T(8,128)(2,1)}) custom-call(bf16[144,384]{1,0:T(8,128)(2,1)S(1)} %get-tuple-element.37.own_ref, bf16[192,384]{1,0:T(8,128)(2,1)S(1)} %collective-permute-done.side_ref, ...), custom_call_target="tpu_custom_call" | custom-call | flops 2000000000 | bytes 2985984 | tf_op jit(solution)/shard_map/pallas_call | solution.py:370
  24.3 11.7 %all-to-all-start = ((bf16[8,432,128]{2,1,0:T(8,128)(2,1)}), bf16[8,432,128]{2,1,0:T(8,128)(2,1)S(1)}, u32[]{:S(2)}, u32[]{:S(2)}) async-start(bf16[8,432,128]{2,1,0:T(8,128)(2,1)} %bitcast.5), calls=%async_computation | async-start | bytes 1769472 | tf_op jit(solution)/shard_map/all_to_all | solution.py:391
  35.9 1.3 %collective-permute-start.2 = (bf16[96,384]{1,0:T(8,128)(2,1)S(1)}, bf16[96,384]{1,0:T(8,128)(2,1)S(1)}, u32[]{:S(2)}, u32[]{:S(2)}) collective-permute-start(bf16[96,384]{1,0:T(8,128)(2,1)S(1)} %get-tuple-element.51), channel_id=1, source_target_pairs={{1,0},{2,1},{3,2},{4,3},{5,4},{6,5},{7,6},{8,7},{9,8},{10,9},{11,1... | collective-permute-start | bytes 221192 | tf_op jit(solution)/shard_map/ppermute | solution.py:387
  37.2 12.0 %collective-permute-done.2.edge_ref = bf16[96,384]{1,0:T(8,128)(2,1)S(1)} collective-permute-done((bf16[96,384]{1,0:T(8,128)(2,1)S(1)}, bf16[96,384]{1,0:T(8,128)(2,1)S(1)}, u32[]{:S(2)}, u32[]{:S(2)}) %collective-permute-start.2) | collective-permute-done | bytes 73760 | tf_op jit(solution)/shard_map/ppermute | solution.py:387
  49.2 1.7 %all-to-all-done = bf16[8,432,128]{2,1,0:T(8,128)(2,1)S(1)} async-done(((bf16[8,432,128]{2,1,0:T(8,128)(2,1)}), bf16[8,432,128]{2,1,0:T(8,128)(2,1)S(1)}, u32[]{:S(2)}, u32[]{:S(2)}) %all-to-all-start) | async-done | bytes 884768 | tf_op jit(solution)/shard_map/all_to_all | solution.py:391
  50.9 0.1 reduce_sum.24
  51.0 0.7 pad_bitcast_fusion
  51.7 14.3 %all-to-all-start.1 = ((bf16[64,8,128]{2,1,0:T(8,128)(2,1)}), bf16[64,8,128]{2,1,0:T(8,128)(2,1)S(1)}, u32[]{:S(2)}, u32[]{:S(2)}) async-start(bf16[64,8,128]{2,1,0:T(8,128)(2,1)} %pad_bitcast_fusion), calls=%async_computation.1 | async-start | bytes 262144 | tf_op jit(solution)/shard_map/all_to_all | solution.py:391
  66.0 3.1 %collective-permute-start.3 = (bf16[192,384]{1,0:T(8,128)(2,1)S(1)}, bf16[192,384]{1,0:T(8,128)(2,1)S(1)}, u32[]{:S(2)}, u32[]{:S(2)}) collective-permute-start(bf16[192,384]{1,0:T(8,128)(2,1)S(1)} %pad_maximum_fusion), channel_id=1, source_target_pairs={{0,496},{16,0},{32,16},{48,32},{64,48},{80,64},{96,80},{112,96},{1... | collective-permute-start | bytes 442376 | tf_op jit(solution)/shard_map/ppermute | solution.py:387
  69.1 5.2 %collective-permute-done.3.side_ref = bf16[192,384]{1,0:T(8,128)(2,1)S(1)} collective-permute-done((bf16[192,384]{1,0:T(8,128)(2,1)S(1)}, bf16[192,384]{1,0:T(8,128)(2,1)S(1)}, u32[]{:S(2)}, u32[]{:S(2)}) %collective-permute-start.3) | collective-permute-done | bytes 147488 | tf_op jit(solution)/shard_map/ppermute | solution.py:387
  74.3 3.3 %all-to-all-done.1 = bf16[64,8,128]{2,1,0:T(8,128)(2,1)S(1)} async-done(((bf16[64,8,128]{2,1,0:T(8,128)(2,1)}), bf16[64,8,128]{2,1,0:T(8,128)(2,1)S(1)}, u32[]{:S(2)}, u32[]{:S(2)}) %all-to-all-start.1) | async-done | bytes 131104 | tf_op jit(solution)/shard_map/all_to_all | solution.py:391
  77.6 0.1 reduce_sum.25
  77.7 20.0 %all_to_all.20 = bf16[64,8,128]{2,1,0:T(8,128)(2,1)S(1)} all-to-all(bf16[64,8,128]{2,1,0:T(8,128)(2,1)S(1)} %broadcast_in_dim.2), channel_id=1, replica_groups=mesh['z'=8,'xh'=2,'c'=2,'y'=8,'xl'=2] {'y','z'}, dimensions={0} | all-to-all | bytes 262144 | tf_op jit(solution)/shard_map/all_to_all | solution.py:391
  97.7 1.0 shard_map.159
  98.8 3.7 %all-to-all-start.3 = ((bf16[8,432,128]{2,1,0:T(8,128)(2,1)}), bf16[8,432,128]{2,1,0:T(8,128)(2,1)S(1)}, u32[]{:S(2)}, u32[]{:S(2)}) async-start(bf16[8,432,128]{2,1,0:T(8,128)(2,1)} %shard_map.159), calls=%async_computation.3 | async-start | bytes 1769472 | tf_op jit(solution)/shard_map/all_to_all | solution.py:391
  102.5 0.0 copy-done.4
  102.5 1.0 shard_map.158
  103.5 0.7 copy.17
  104.2 0.8 copy.18
  105.0 10.9 %all-to-all-done.3 = bf16[8,432,128]{2,1,0:T(8,128)(2,1)S(1)} async-done(((bf16[8,432,128]{2,1,0:T(8,128)(2,1)}), bf16[8,432,128]{2,1,0:T(8,128)(2,1)S(1)}, u32[]{:S(2)}, u32[]{:S(2)}) %all-to-all-start.3) | async-done | bytes 884768 | tf_op jit(solution)/shard_map/all_to_all | solution.py:391
  115.9 1.0 shard_map.160
  (8 shorter events, 0.1 us)
Async XLA Ops:
  0.6 0.9 copy-start
  1.5 0.9 copy-start.1
  2.5 6.7 %copy-start.10 = (s32[20736]{0:T(1024)S(1)}, s32[20736]{0:T(1024)}, u32[]{:S(2)}) copy-start(s32[20736]{0:T(1024)} %param.20) | copy-start | bytes 248836
  3.0 6.3 %copy-start.7 = (bf16[2,1,6,3312]{3,0,2,1:T(2,128)(2,1)S(1)}, bf16[2,1,6,3312]{3,0,2,1:T(2,128)(2,1)}, u32[]{:S(2)}) copy-start(bf16[2,1,6,3312]{3,0,2,1:T(2,128)(2,1)} %param.19) | copy-start | bytes 238468
  3.0 10.1 %collective-permute-start = (bf16[192,384]{1,0:T(8,128)(2,1)S(1)}, bf16[192,384]{1,0:T(8,128)(2,1)S(1)}, u32[]{:S(2)}, u32[]{:S(2)}) collective-permute-start(bf16[192,384]{1,0:T(8,128)(2,1)S(1)} %get-tuple-element.38), channel_id=1, source_target_pairs={{0,16},{16,32},{32,48},{48,64},{64,80},{80,96},{96,112},{112,128},... | collective-permute-start | bytes 442376 | tf_op jit(solution)/shard_map/ppermute | solution.py:387
  9.3 6.1 %copy-start.2 = (s32[192,768]{1,0:T(8,128)S(1)}, s32[192,768]{1,0:T(8,128)}, u32[]{:S(2)}) copy-start(s32[192,768]{1,0:T(8,128)} %cu_ref) | copy-start | bytes 1769476
  9.3 6.1 %copy-start.3 = (s32[768,192]{0,1:T(8,128)S(1)}, s32[768,192]{0,1:T(8,128)}, u32[]{:S(2)}) copy-start(s32[768,192]{0,1:T(8,128)} %param.16) | copy-start | bytes 1769476
  9.3 6.1 %copy-start.5 = (s32[192,576]{1,0:T(8,128)S(1)}, s32[192,576]{1,0:T(8,128)}, u32[]{:S(2)}) copy-start(s32[192,576]{1,0:T(8,128)} %cq_ref) | copy-start | bytes 1327108
  13.0 2.5 %copy-start.6 = (s32[192,192]{1,0:T(8,128)S(1)}, s32[192,192]{1,0:T(8,128)}, u32[]{:S(2)}) copy-start(s32[192,192]{1,0:T(8,128)} %cp_ref) | copy-start | bytes 442372
  13.1 2.4 %copy-start.8 = (s32[4]{0:T(128)S(1)}, s32[4]{0:T(128)}, u32[]{:S(2)}) copy-start(s32[4]{0:T(128)} %bits_ref.1) | copy-start | bytes 52
  13.1 2.4 %copy-start.9 = (s32[4]{0:T(128)S(1)}, s32[4]{0:T(128)}, u32[]{:S(2)}) copy-start(s32[4]{0:T(128)} %scale_ref.1) | copy-start | bytes 52
  13.1 3.7 %collective-permute-start.1 = (bf16[96,384]{1,0:T(8,128)(2,1)S(1)}, bf16[96,384]{1,0:T(8,128)(2,1)S(1)}, u32[]{:S(2)}, u32[]{:S(2)}) collective-permute-start(bf16[96,384]{1,0:T(8,128)(2,1)S(1)} %pad_maximum_fusion.1), channel_id=1, source_target_pairs={{0,1},{1,2},{2,3},{3,4},{4,5},{5,6},{6,7},{7,8},{8,9},{9,10},{10,1... | collective-permute-start | bytes 221192 | tf_op jit(solution)/shard_map/ppermute | solution.py:387
  24.3 26.6 %all-to-all-start = ((bf16[8,432,128]{2,1,0:T(8,128)(2,1)}), bf16[8,432,128]{2,1,0:T(8,128)(2,1)S(1)}, u32[]{:S(2)}, u32[]{:S(2)}) async-start(bf16[8,432,128]{2,1,0:T(8,128)(2,1)} %bitcast.5), calls=%async_computation | async-start | bytes 1769472 | tf_op jit(solution)/shard_map/all_to_all | solution.py:391
  35.9 13.3 %collective-permute-start.2 = (bf16[96,384]{1,0:T(8,128)(2,1)S(1)}, bf16[96,384]{1,0:T(8,128)(2,1)S(1)}, u32[]{:S(2)}, u32[]{:S(2)}) collective-permute-start(bf16[96,384]{1,0:T(8,128)(2,1)S(1)} %get-tuple-element.51), channel_id=1, source_target_pairs={{1,0},{2,1},{3,2},{4,3},{5,4},{6,5},{7,6},{8,7},{9,8},{10,9},{11,1... | collective-permute-start | bytes 221192 | tf_op jit(solution)/shard_map/ppermute | solution.py:387
  51.7 25.9 %all-to-all-start.1 = ((bf16[64,8,128]{2,1,0:T(8,128)(2,1)}), bf16[64,8,128]{2,1,0:T(8,128)(2,1)S(1)}, u32[]{:S(2)}, u32[]{:S(2)}) async-start(bf16[64,8,128]{2,1,0:T(8,128)(2,1)} %pad_bitcast_fusion), calls=%async_computation.1 | async-start | bytes 262144 | tf_op jit(solution)/shard_map/all_to_all | solution.py:391
  66.0 8.3 %collective-permute-start.3 = (bf16[192,384]{1,0:T(8,128)(2,1)S(1)}, bf16[192,384]{1,0:T(8,128)(2,1)S(1)}, u32[]{:S(2)}, u32[]{:S(2)}) collective-permute-start(bf16[192,384]{1,0:T(8,128)(2,1)S(1)} %pad_maximum_fusion), channel_id=1, source_target_pairs={{0,496},{16,0},{32,16},{48,32},{64,48},{80,64},{96,80},{112,96},{1... | collective-permute-start | bytes 442376 | tf_op jit(solution)/shard_map/ppermute | solution.py:387
  98.8 3.7 %copy-start.4 = (bf16[768,384]{1,0:T(8,128)(2,1)S(1)}, bf16[768,384]{1,0:T(8,128)(2,1)}, u32[]{:S(2)}) copy-start(bf16[768,384]{1,0:T(8,128)(2,1)} %weight_ref.1) | copy-start | bytes 1769476
  98.8 17.1 %all-to-all-start.3 = ((bf16[8,432,128]{2,1,0:T(8,128)(2,1)}), bf16[8,432,128]{2,1,0:T(8,128)(2,1)S(1)}, u32[]{:S(2)}, u32[]{:S(2)}) async-start(bf16[8,432,128]{2,1,0:T(8,128)(2,1)} %shard_map.159), calls=%async_computation.3 | async-start | bytes 1769472 | tf_op jit(solution)/shard_map/all_to_all | solution.py:391

commit v4 on v3

--- a/solution.py
+++ b/solution.py
@@ -39,7 +39,7 @@
 
 LAT = ("y", "xl")
 LON = ("z", "xh", "c")
-NEAR = ("xh", "c", "xl")
+NEAR = ("xh", "xl")
 FAR = ("y", "z")
 
 
@@ -183,8 +183,10 @@
     bias_ref,
     own_out,
     side_out,
-    edge_out,
-    sums_ref,
+    low_out,
+    corner_out,
+    keep_ref,
+    give_ref,
     frame,
 ):
     below = ROWS - OFF
@@ -285,8 +287,8 @@
 
     own_out[...] = flat(result[:, OFF:, 1])
     side_out[...] = flat(result[:, OFF:, 0])
-    edge_out[0:THIN, :] = flat(result[:, :OFF, 1])
-    edge_out[THIN:, :] = flat(result[:, :OFF, 0])
+    low_out[...] = flat(result[:, :OFF, 1])
+    corner_out[...] = flat(result[:, :OFF, 0])
 
     small = [
         crossed(normed, d_query),
@@ -300,33 +302,55 @@
     ]
     for wide in (crossed(normed_two, d_pre), crossed(d_out_low, hidden)):
         tiles += [wide[:, i * 128 : (i + 1) * 128] for i in range(6)]
-    for i, tile in enumerate(tiles):
-        sums_ref[i * C : (i + 1) * C, :] = tile.astype(BF16)
-
-
-def spread_kernel(sums_ref, qkv_ref, proj_ref, up_ref, down_ref):
+    half_tiles = len(tiles) // 2
+
+    def store(ref, first):
+        for i in range(half_tiles):
+            ref[i * C : (i + 1) * C, :] = tiles[first + i].astype(BF16)
+
+    core = lax.axis_index("c")
+
+    @pl.when(core == 0)
+    def _():
+        store(keep_ref, 0)
+        store(give_ref, half_tiles)
+
+    @pl.when(core != 0)
+    def _():
+        store(keep_ref, half_tiles)
+        store(give_ref, 0)
+
+
+def spread_kernel(own_ref, other_ref, qkv_ref, proj_ref, up_ref, down_ref):
+    first = lax.axis_index("c") == 0
+    half_tiles = own_ref.shape[0] // C
+
     def tile(i):
-        return sums_ref[i * C : (i + 1) * C, :].astype(F32)
+        at = slice(i % half_tiles * C, (i % half_tiles + 1) * C)
+        mine = first if i < half_tiles else jnp.logical_not(first)
+        return jnp.where(mine, own_ref[at, :].astype(F32), other_ref[at, :].astype(F32))
 
     ends = [tile(4)[:, :64], tile(4)[:, 64:], tile(5)[:, :64], tile(5)[:, 64:]]
     small = [jnp.concatenate([tile(i), ends[i]], axis=-1) for i in range(4)]
     qkv_ref[...] = jnp.concatenate(small[:3], axis=-1).astype(BF16)
     proj_ref[...] = small[3].astype(BF16)
     for i in range(6):
-        up_ref[:, i * 128 : (i + 1) * 128] = sums_ref[(6 + i) * C : (7 + i) * C, :]
-        down_ref[:, i * 128 : (i + 1) * 128] = sums_ref[(12 + i) * C : (13 + i) * C, :]
-
-
-def finish_kernel(own_ref, edge_ref, side_ref, weight_ref, merged_ref, grad_ref, frame):
+        up_ref[:, i * 128 : (i + 1) * 128] = tile(6 + i).astype(BF16)
+        down_ref[:, i * 128 : (i + 1) * 128] = tile(12 + i).astype(BF16)
+
+
+def finish_kernel(
+    own_ref, side_ref, low_ref, corner_ref, weight_ref, merged_ref, grad_ref, frame
+):
     above = ROWS - OFF
 
-    def piece(block, rows):
-        return block.astype(F32).reshape(LEVS, rows, SUB, 2 * C)
-
-    frame[:, :above, 0] = piece(own_ref[...], above)
-    frame[:, above:, 0] = piece(edge_ref[0:THIN, :], OFF)
-    frame[:, :above, 1] = piece(side_ref[0:BIG, :], above)
-    frame[:, above:, 1] = piece(side_ref[BIG:, :], OFF)
+    def piece(ref, rows):
+        return ref[...].astype(F32).reshape(LEVS, rows, SUB, 2 * C)
+
+    frame[:, :above, 0] = piece(own_ref, above)
+    frame[:, above:, 0] = piece(low_ref, OFF)
+    frame[:, :above, 1] = piece(side_ref, above)
+    frame[:, above:, 1] = piece(corner_ref, OFF)
     both = frame[...].reshape(FRAME, 2 * C)
     final = both[:, :C].astype(BF16)
     grad = both[:, C:].astype(BF16)
@@ -378,48 +402,50 @@
     )(*args)
 
 
-def shifted(block, axes, step):
-    count = lax.axis_size(axes)
-    if axes == LAT:
-        route = [(i, i + step) for i in range(count) if 0 <= i + step < count]
-    else:
-        route = [(i, (i + step) % count) for i in range(count)]
-    return lax.ppermute(block, axes, route)
+def shifted(block, lat_step, lon_step):
+    rows = lax.axis_size(LAT)
+    cols = lax.axis_size(LON)
+    if lat_step and lon_step:
+        route = [
+            (col * rows + row, (col + lon_step) % cols * rows + row + lat_step)
+            for col in range(cols)
+            for row in range(rows)
+            if 0 <= row + lat_step < rows
+        ]
+        return lax.ppermute(block, LON + LAT, route)
+    if lat_step:
+        route = [(r, r + lat_step) for r in range(rows) if 0 <= r + lat_step < rows]
+        return lax.ppermute(block, LAT, route)
+    return lax.ppermute(block, LON, [(c, (c + lon_step) % cols) for c in range(cols)])
 
 
 def exchange(parts, axes):
     return lax.all_to_all(parts, axes, 0, 0)
 
 
-def total_of(parts):
-    return jnp.sum(parts.astype(F32), axis=0).astype(BF16)
-
-
-def copies(part, count):
-    def kernel(part_ref, out_ref):
-        for i in range(count):
-            out_ref[i] = part_ref[...]
-
-    return call(kernel, [((count,) + part.shape, BF16)], (part,))[0]
-
-
-def summed_everywhere(sums, own, edge, side):
-    near = lax.axis_size(NEAR)
-    far = lax.axis_size(FAR)
-    rows = sums.shape[0] // near
-    padded = -(-rows // (8 * far)) * (8 * far)
-    edge = shifted(edge, LAT, -1)
-    part = exchange(sums.reshape(near, rows, 128), NEAR)
-    part, edge = lax.optimization_barrier((part, edge))
-    side = shifted(jnp.concatenate([side, edge[THIN:]], axis=0), LON, -1)
-    part = jnp.pad(total_of(part), ((0, padded - rows), (0, 0)))
-    part = exchange(part.reshape(far, padded // far, 128), FAR)
-    part, side = lax.optimization_barrier((part, side))
-    part = exchange(jnp.broadcast_to(total_of(part)[None], part.shape), FAR)
-    part = part.reshape(padded, 128)[:rows]
-    part, moved = lax.optimization_barrier((part, (own, edge, side)))
-    whole = exchange(copies(part, near), NEAR)
-    return whole.reshape(near * rows, 128), moved
+def swapped(block):
+    return lax.ppermute(block, "c", [(0, 1), (1, 0)])
+
+
+def sum_kernel(parts_ref, out_ref):
+    count, rows, _ = parts_ref.shape
+    total = parts_ref[0].astype(F32)
+    for i in range(1, count):
+        total = total + parts_ref[i].astype(F32)
+    out_ref[0:rows, :] = total.astype(BF16)
+    if rows < out_ref.shape[0]:
+        out_ref[rows:, :] = jnp.zeros((out_ref.shape[0] - rows, 128), BF16)
+
+
+def sum_spread_kernel(parts_ref, out_ref):
+    total = jnp.sum(parts_ref[...].astype(F32), axis=0).astype(BF16)
+    out_ref[...] = jnp.broadcast_to(total[None], out_ref.shape)
+
+
+def copies_kernel(part_ref, out_ref):
+    count, rows, _ = out_ref.shape
+    for i in range(count):
+        out_ref[i] = part_ref[0:rows, :]
 
 
 def per_device(
@@ -440,7 +466,7 @@
         [((BIG, 2 * C), BF16), ((THIN, 2 * C), BF16), ((BIG + THIN, 2 * C), BF16)],
         (tokens.transpose(1, 2, 0, 3), cotangent.transpose(1, 2, 0, 3)),
     )
-    side = shifted(side, LON, 1)
+    side = shifted(side, 0, 1)
     (bias,) = call(
         bias_kernel,
         [((4, STACK, 128), BF16)],
@@ -459,7 +485,7 @@
     edge, bias, codes = lax.optimization_barrier(
         (edge, bias, (qkv_codes, proj_codes, up_codes, down_codes.T))
     )
-    edge = shifted(edge, LAT, 1)
+    edge = shifted(edge, 1, 0)
     weights = call(
         weight_kernel,
         [((3, C, C), BF16), ((C, C), BF16), ((C, FF), BF16), ((C, FF), BF16)],
@@ -467,31 +493,51 @@
         scalars=2,
         flops=1_000_000_000,
     )
-    own, side, edge, sums = call(
+    own, side, low, corner, keep, give = call(
         main_kernel,
         [
             ((BIG, 2 * C), BF16),
             ((BIG, 2 * C), BF16),
-            ((2 * THIN, 2 * C), BF16),
-            ((18 * C, 128), BF16),
+            ((THIN, 2 * C), BF16),
+            ((THIN, 2 * C), BF16),
+            ((9 * C, 128), BF16),
+            ((9 * C, 128), BF16),
         ],
         (own, side, edge, *weights, bias),
         [pltpu.VMEM((LEVS, ROWS, 2, SUB, 2 * C), F32)],
         flops=2_000_000_000,
         mib=32,
     )
-    whole, moved = summed_everywhere(sums, own, edge, side)
+
+    near = lax.axis_size(NEAR)
+    far = lax.axis_size(FAR)
+    rows = 9 * C // near
+    padded = -(-rows // (8 * far)) * (8 * far)
+    part = (keep.astype(F32) + swapped(give).astype(F32)).astype(BF16)
+    part = exchange(part.reshape(near, rows, 128), NEAR)
+    side, low = shifted(side, 0, -1), shifted(low, -1, 0)
+    part, side, low = lax.optimization_barrier((part, side, low))
+    (part,) = call(sum_kernel, [((padded, 128), BF16)], (part,))
+    part = exchange(part.reshape(far, padded // far, 128), FAR)
+    (part,) = call(sum_spread_kernel, [(part.shape, BF16)], (part,))
+    part = exchange(part, FAR).reshape(padded, 128)
+    part, own, corner = lax.optimization_barrier((part, own, corner))
+    corner = shifted(corner, -1, -1)
+    (spread,) = call(copies_kernel, [((near, rows, 128), BF16)], (part,))
+    half = exchange(spread, NEAR)
     merged, grad_tokens = call(
         finish_kernel,
         [((LEVS, ROWS // 2, COLS // 2, 2 * C), BF16), ((LEVS, ROWS, COLS, C), BF16)],
-        (*moved, merge_weight),
+        (own, side, low, corner, merge_weight),
         [pltpu.VMEM((LEVS, ROWS, 2, SUB, 2 * C), F32)],
         flops=400_000_000,
     )
+    half, merged, grad_tokens = lax.optimization_barrier((half, merged, grad_tokens))
+    half = half.reshape(near * rows, 128)
     qkv, proj, up, down = call(
         spread_kernel,
         [((C, 3 * C), BF16), ((C, C), BF16), ((C, FF), BF16), ((C, FF), BF16)],
-        (whole,),
+        (half, swapped(half)),
     )
     return (merged, grad_tokens, qkv, proj, up, down.T)
 

time: 117 us -> 112 us (0.957)
  blocking collectives: 20 us -> 41.3 us
  waiting for transfers between devices: 33.3 us -> 17.7 us
  starting transfers between devices: 42.5 us -> 32.3 us
    all_to_all x3 -> x2, starting transfers between devices: 29.7 us -> 6.93 us  [exchange(): return lax.all_to_all(parts, axes, 0, 0)]
    all_to_all x1 -> x2, blocking collectives: 20 us -> 41.3 us  [exchange(): return lax.all_to_all(parts, axes, 0, 0)]
    all_to_all x3 -> x2, waiting for transfers between devices: 15.8 us -> 0.01 us  [exchange(): return lax.all_to_all(parts, axes, 0, 0)]
    ppermute x4 -> x7, starting transfers between devices: 12.9 us -> 25.4 us  [the longest x2 11.8 us: swapped(): return lax.ppermute(block, 'c', [(0, 1), (1, 0)])]
    pallas_call x7 -> x9, Pallas kernels: 15.8 us -> 14.9 us  [call(): pl.pallas_call(kernel, out_shape=[jax.ShapeDtypeStruct(s, t) for s, t in...]
    ppermute x4 -> x7, waiting for transfers between devices: 17.4 us -> 17.7 us  [the longest x1 9.61 us: shifted(): return lax.ppermute(block, LON + LAT, route)]
  transfers between devices with their start and end apart: 7 -> 9, of which waited for: 6 -> 6; matrix products, arithmetic and copies ran while one was open for 1% -> 1% of each run, Pallas kernels for 5% -> 5%
where the time goes in v4:
time: 112 us
  blocking collectives  41.3 us (37%)
  starting transfers between devices  32.3 us (29%)
  waiting for transfers between devices  17.7 us (16%)
  Pallas kernels  14.9 us (13%)
  local copies, waits for them, and re-layouts  3.47 us (3%)
    all_to_all x2, blocking collectives, exchange(): return lax.all_to_all(parts, axes, 0, 0)  41.3 us
    pallas_call x9, Pallas kernels, call(): pl.pallas_call(kernel, out_shape=[jax.ShapeDtypeStruct(s, t) for s, t in...  14.9 us
    ppermute x2, starting transfers between devices, swapped(): return lax.ppermute(block, 'c', [(0, 1), (1, 0)])  11.8 us
    ppermute x1, waiting for transfers between devices, shifted(): return lax.ppermute(block, LON + LAT, route)  9.61 us
    ppermute x2, starting transfers between devices, shifted(): lax.ppermute(block, LON, [(c, (c + lon_step) % cols) for c in range(cols)])  8.69 us
    all_to_all x2, starting transfers between devices, exchange(): return lax.all_to_all(parts, axes, 0, 0)  6.93 us
    ppermute x2, waiting for transfers between devices, shifted(): return lax.ppermute(block, LAT, route)  5.94 us
    ppermute x2, starting transfers between devices, shifted(): return lax.ppermute(block, LAT, route)  3.64 us
  transfers between devices with their start and end apart: 9, of which 6 were waited for; matrix products, arithmetic and copies ran while one was open for 1% of the time, Pallas kernels for 5%

profile of v4, /device:TPU:1, one launch (start us, length us, event | category | flops | bytes accessed | tf_op | source)
XLA Modules:
  0.0 111.5 jit_solution(6326174825025122343)
XLA Ops:
  0.6 0.0 copy-start
  0.6 0.9 copy-done
  1.5 0.9 copy-done.1
  2.5 0.5 shard_map.154
  3.0 0.0 copy-start.7
  3.0 6.2 %collective-permute-start = (bf16[192,384]{1,0:T(8,128)(2,1)S(1)}, bf16[192,384]{1,0:T(8,128)(2,1)S(1)}, u32[]{:S(2)}, u32[]{:S(2)}) collective-permute-start(bf16[192,384]{1,0:T(8,128)(2,1)S(1)} %get-tuple-element.41), channel_id=1, source_target_pairs={{0,16},{16,32},{32,48},{48,64},{64,80},{80,96},{96,112},{112,128},... | collective-permute-start | bytes 442376 | tf_op jit(solution)/shard_map/ppermute | solution.py:419
  9.2 0.0 copy-done.10
  9.2 0.1 reshape.30.idx_ref
  9.3 0.0 copy-done.7
  9.3 0.0 copy-start.2
  9.3 0.0 copy-start.3
  9.3 0.0 copy-start.5
  9.3 3.7 %shard_map.155.bias_ref = bf16[4,576,128]{2,1,0:T(8,128)(2,1)S(1)} custom-call(s32[144,144]{1,0:T(8,128)S(1)} %reshape.30.idx_ref, bf16[6,2,3312]{2,1,0:T(2,128)(2,1)S(1)} %bitcast.18), custom_call_target="tpu_custom_call" | custom-call | flops 2000000000 | bytes 752256 | tf_op jit(solution)/shard_map/pallas_call | solution.py:394
  13.0 0.0 copy-start.6
  13.0 0.0 collective-permute-done.side_ref
  13.1 0.0 copy-start.8
  13.1 0.0 copy-start.9
  13.1 2.4 %collective-permute-start.1 = (bf16[96,384]{1,0:T(8,128)(2,1)S(1)}, bf16[96,384]{1,0:T(8,128)(2,1)S(1)}, u32[]{:S(2)}, u32[]{:S(2)}) collective-permute-start(bf16[96,384]{1,0:T(8,128)(2,1)S(1)} %pad_maximum_fusion), channel_id=1, source_target_pairs={{0,1},{1,2},{2,3},{3,4},{4,5},{5,6},{6,7},{7,8},{8,9},{9,10},{10,1... | collective-permute-start | bytes 221192 | tf_op jit(solution)/shard_map/ppermute | solution.py:418
  15.4 0.0 copy-done.2
  15.5 0.0 copy-done.3
  15.5 0.0 copy-done.5
  15.5 1.1 shard_map.156
  16.6 0.2 collective-permute-done.1.edge_ref
  16.8 6.6 %shard_map.157 = (bf16[144,384]{1,0:T(8,128)(2,1)S(1)}, bf16[144,384]{1,0:T(8,128)(2,1)S(1)}, bf16[48,384]{1,0:T(8,128)(2,1)S(1)}, bf16[48,384]{1,0:T(8,128)(2,1...) custom-call(bf16[144,384]{1,0:T(8,128)(2,1)S(1)} %get-tuple-element.40.own_ref, ...), custom_call_target="tpu_custom_call" | custom-call | flops 2000000000 | bytes 2985984 | tf_op jit(solution)/shard_map/pallas_call | solution.py:394
  23.4 9.9 %collective-permute-start.2 = (bf16[1728,128]{1,0:T(8,128)(2,1)S(1)}, bf16[1728,128]{1,0:T(8,128)(2,1)S(1)}, u32[]{:S(2)}, u32[]{:S(2)}) collective-permute-start(bf16[1728,128]{1,0:T(8,128)(2,1)S(1)} %get-tuple-element.54), channel_id=1, source_target_pairs={{0,16},{16,0},{1,17},{17,1},{2,18},{18,2},{3,19},{19,3},{4,20},{20... | collective-permute-start | bytes 1327112 | tf_op jit(solution)/shard_map/ppermute | solution.py:427
  33.3 1.4 %collective-permute-done.2 = bf16[1728,128]{1,0:T(8,128)(2,1)S(1)} collective-permute-done((bf16[1728,128]{1,0:T(8,128)(2,1)S(1)}, bf16[1728,128]{1,0:T(8,128)(2,1)S(1)}, u32[]{:S(2)}, u32[]{:S(2)}) %collective-permute-start.2) | collective-permute-done | bytes 442400 | tf_op jit(solution)/shard_map/ppermute | solution.py:427
  34.7 0.9 add_convert_fusion
  35.6 3.5 %all-to-all-start = ((bf16[4,432,128]{2,1,0:T(8,128)(2,1)}), bf16[4,432,128]{2,1,0:T(8,128)(2,1)S(1)}, u32[]{:S(2)}, u32[]{:S(2)}) async-start(bf16[4,432,128]{2,1,0:T(8,128)(2,1)} %bitcast.5), calls=%async_computation | async-start | bytes 884736 | tf_op jit(solution)/shard_map/all_to_all | solution.py:423
  39.1 2.5 %collective-permute-start.3 = (bf16[144,384]{1,0:T(8,128)(2,1)S(1)}, bf16[144,384]{1,0:T(8,128)(2,1)S(1)}, u32[]{:S(2)}, u32[]{:S(2)}) collective-permute-start(bf16[144,384]{1,0:T(8,128)(2,1)S(1)} %get-tuple-element.55), channel_id=1, source_target_pairs={{0,496},{16,0},{32,16},{48,32},{64,48},{80,64},{96,80},{112,96},{1... | collective-permute-start | bytes 331784 | tf_op jit(solution)/shard_map/ppermute | solution.py:419
  41.6 1.3 %collective-permute-start.4 = (bf16[48,384]{1,0:T(8,128)(2,1)S(1)}, bf16[48,384]{1,0:T(8,128)(2,1)S(1)}, u32[]{:S(2)}, u32[]{:S(2)}) collective-permute-start(bf16[48,384]{1,0:T(8,128)(2,1)S(1)} %get-tuple-element.56), channel_id=1, source_target_pairs={{1,0},{2,1},{3,2},{4,3},{5,4},{6,5},{7,6},{8,7},{9,8},{10,9},{11,1... | collective-permute-start | bytes 110600 | tf_op jit(solution)/shard_map/ppermute | solution.py:418
  42.9 5.7 %collective-permute-done.4.low_ref = bf16[48,384]{1,0:T(8,128)(2,1)S(1)} collective-permute-done((bf16[48,384]{1,0:T(8,128)(2,1)S(1)}, bf16[48,384]{1,0:T(8,128)(2,1)S(1)}, u32[]{:S(2)}, u32[]{:S(2)}) %collective-permute-start.4) | collective-permute-done | bytes 36896 | tf_op jit(solution)/shard_map/ppermute | solution.py:418
  48.6 0.5 collective-permute-done.3.side_ref
  49.1 0.0 all-to-all-done.parts_ref
  49.1 0.1 shard_map.158
  49.1 25.9 %all_to_all.20.parts_ref = bf16[64,8,128]{2,1,0:T(8,128)(2,1)S(1)} all-to-all(bf16[64,8,128]{2,1,0:T(8,128)(2,1)S(1)} %bitcast.14), channel_id=1, replica_groups=mesh['z'=8,'xh'=2,'c'=2,'y'=8,'xl'=2] {'y','z'}, dimensions={0} | all-to-all | bytes 262144 | tf_op jit(solution)/shard_map/all_to_all | solution.py:423
  75.0 0.1 shard_map.159
  75.1 15.4 %all_to_all.21 = bf16[64,8,128]{2,1,0:T(8,128)(2,1)S(1)} all-to-all(bf16[64,8,128]{2,1,0:T(8,128)(2,1)S(1)} %shard_map.159), channel_id=1, replica_groups=mesh['z'=8,'xh'=2,'c'=2,'y'=8,'xl'=2] {'y','z'}, dimensions={0} | all-to-all | bytes 262144 | tf_op jit(solution)/shard_map/all_to_all | solution.py:423
  90.5 0.8 shard_map.160
  91.3 3.5 %all-to-all-start.3 = ((bf16[4,432,128]{2,1,0:T(8,128)(2,1)}), bf16[4,432,128]{2,1,0:T(8,128)(2,1)S(1)}, u32[]{:S(2)}, u32[]{:S(2)}) async-start(bf16[4,432,128]{2,1,0:T(8,128)(2,1)} %shard_map.160), calls=%async_computation.3 | async-start | bytes 884736 | tf_op jit(solution)/shard_map/all_to_all | solution.py:423
  94.8 1.3 %collective-permute-start.5 = (bf16[48,384]{1,0:T(8,128)(2,1)S(1)}, bf16[48,384]{1,0:T(8,128)(2,1)S(1)}, u32[]{:S(2)}, u32[]{:S(2)}) collective-permute-start(bf16[48,384]{1,0:T(8,128)(2,1)S(1)} %get-tuple-element.64), channel_id=1, source_target_pairs={{1,496},{2,497},{3,498},{4,499},{5,500},{6,501},{7,502},{8,503},{9... | collective-permute-start | bytes 110600 | tf_op jit(solution)/shard_map/ppermute | solution.py:415
  96.1 9.6 %collective-permute-done.5.corner_ref = bf16[48,384]{1,0:T(8,128)(2,1)S(1)} collective-permute-done((bf16[48,384]{1,0:T(8,128)(2,1)S(1)}, bf16[48,384]{1,0:T(8,128)(2,1)S(1)}, u32[]{:S(2)}, u32[]{:S(2)}) %collective-permute-start.5) | collective-permute-done | bytes 36896 | tf_op jit(solution)/shard_map/ppermute | solution.py:415
  105.7 1.0 shard_map.161
  106.8 0.0 all-to-all-done.3
  106.8 1.9 %collective-permute-start.6 = (bf16[1728,128]{1,0:T(8,128)(2,1)S(1)}, bf16[1728,128]{1,0:T(8,128)(2,1)S(1)}, u32[]{:S(2)}, u32[]{:S(2)}) collective-permute-start(bf16[1728,128]{1,0:T(8,128)(2,1)S(1)} %bitcast.11), channel_id=1, source_target_pairs={{0,16},{16,0},{1,17},{17,1},{2,18},{18,2},{3,19},{19,3},{4,20},{20... | collective-permute-start | bytes 1327112 | tf_op jit(solution)/shard_map/ppermute | solution.py:427
  108.7 0.7 copy.17
  109.4 0.8 copy.18
  110.2 0.3 collective-permute-done.6.other_ref
  110.5 1.1 shard_map.162
  (9 shorter events, 0.0 us)
Async XLA Ops:
  0.6 0.9 copy-start
  1.5 0.9 copy-start.1
  2.5 6.7 %copy-start.10 = (s32[20736]{0:T(1024)S(1)}, s32[20736]{0:T(1024)}, u32[]{:S(2)}) copy-start(s32[20736]{0:T(1024)} %param.20) | copy-start | bytes 248836
  3.0 6.3 %copy-start.7 = (bf16[2,1,6,3312]{3,0,2,1:T(2,128)(2,1)S(1)}, bf16[2,1,6,3312]{3,0,2,1:T(2,128)(2,1)}, u32[]{:S(2)}) copy-start(bf16[2,1,6,3312]{3,0,2,1:T(2,128)(2,1)} %param.19) | copy-start | bytes 238468
  3.0 10.1 %collective-permute-start = (bf16[192,384]{1,0:T(8,128)(2,1)S(1)}, bf16[192,384]{1,0:T(8,128)(2,1)S(1)}, u32[]{:S(2)}, u32[]{:S(2)}) collective-permute-start(bf16[192,384]{1,0:T(8,128)(2,1)S(1)} %get-tuple-element.41), channel_id=1, source_target_pairs={{0,16},{16,32},{32,48},{48,64},{64,80},{80,96},{96,112},{112,128},... | collective-permute-start | bytes 442376 | tf_op jit(solution)/shard_map/ppermute | solution.py:419
  9.3 6.1 %copy-start.2 = (s32[192,768]{1,0:T(8,128)S(1)}, s32[192,768]{1,0:T(8,128)}, u32[]{:S(2)}) copy-start(s32[192,768]{1,0:T(8,128)} %cu_ref) | copy-start | bytes 1769476
  9.3 6.1 %copy-start.3 = (s32[768,192]{0,1:T(8,128)S(1)}, s32[768,192]{0,1:T(8,128)}, u32[]{:S(2)}) copy-start(s32[768,192]{0,1:T(8,128)} %param.16) | copy-start | bytes 1769476
  9.3 6.1 %copy-start.5 = (s32[192,576]{1,0:T(8,128)S(1)}, s32[192,576]{1,0:T(8,128)}, u32[]{:S(2)}) copy-start(s32[192,576]{1,0:T(8,128)} %cq_ref) | copy-start | bytes 1327108
  13.0 2.5 %copy-start.6 = (s32[192,192]{1,0:T(8,128)S(1)}, s32[192,192]{1,0:T(8,128)}, u32[]{:S(2)}) copy-start(s32[192,192]{1,0:T(8,128)} %cp_ref) | copy-start | bytes 442372
  13.1 2.4 %copy-start.8 = (s32[4]{0:T(128)S(1)}, s32[4]{0:T(128)}, u32[]{:S(2)}) copy-start(s32[4]{0:T(128)} %bits_ref.1) | copy-start | bytes 52
  13.1 2.4 %copy-start.9 = (s32[4]{0:T(128)S(1)}, s32[4]{0:T(128)}, u32[]{:S(2)}) copy-start(s32[4]{0:T(128)} %scale_ref.1) | copy-start | bytes 52
  13.1 3.7 %collective-permute-start.1 = (bf16[96,384]{1,0:T(8,128)(2,1)S(1)}, bf16[96,384]{1,0:T(8,128)(2,1)S(1)}, u32[]{:S(2)}, u32[]{:S(2)}) collective-permute-start(bf16[96,384]{1,0:T(8,128)(2,1)S(1)} %pad_maximum_fusion), channel_id=1, source_target_pairs={{0,1},{1,2},{2,3},{3,4},{4,5},{5,6},{6,7},{7,8},{8,9},{9,10},{10,1... | collective-permute-start | bytes 221192 | tf_op jit(solution)/shard_map/ppermute | solution.py:418
  23.4 11.3 %collective-permute-start.2 = (bf16[1728,128]{1,0:T(8,128)(2,1)S(1)}, bf16[1728,128]{1,0:T(8,128)(2,1)S(1)}, u32[]{:S(2)}, u32[]{:S(2)}) collective-permute-start(bf16[1728,128]{1,0:T(8,128)(2,1)S(1)} %get-tuple-element.54), channel_id=1, source_target_pairs={{0,16},{16,0},{1,17},{17,1},{2,18},{18,2},{3,19},{19,3},{4,20},{20... | collective-permute-start | bytes 1327112 | tf_op jit(solution)/shard_map/ppermute | solution.py:427
  35.6 13.5 %all-to-all-start = ((bf16[4,432,128]{2,1,0:T(8,128)(2,1)}), bf16[4,432,128]{2,1,0:T(8,128)(2,1)S(1)}, u32[]{:S(2)}, u32[]{:S(2)}) async-start(bf16[4,432,128]{2,1,0:T(8,128)(2,1)} %bitcast.5), calls=%async_computation | async-start | bytes 884736 | tf_op jit(solution)/shard_map/all_to_all | solution.py:423
  39.1 10.0 %collective-permute-start.3 = (bf16[144,384]{1,0:T(8,128)(2,1)S(1)}, bf16[144,384]{1,0:T(8,128)(2,1)S(1)}, u32[]{:S(2)}, u32[]{:S(2)}) collective-permute-start(bf16[144,384]{1,0:T(8,128)(2,1)S(1)} %get-tuple-element.55), channel_id=1, source_target_pairs={{0,496},{16,0},{32,16},{48,32},{64,48},{80,64},{96,80},{112,96},{1... | collective-permute-start | bytes 331784 | tf_op jit(solution)/shard_map/ppermute | solution.py:419
  41.6 7.0 %collective-permute-start.4 = (bf16[48,384]{1,0:T(8,128)(2,1)S(1)}, bf16[48,384]{1,0:T(8,128)(2,1)S(1)}, u32[]{:S(2)}, u32[]{:S(2)}) collective-permute-start(bf16[48,384]{1,0:T(8,128)(2,1)S(1)} %get-tuple-element.56), channel_id=1, source_target_pairs={{1,0},{2,1},{3,2},{4,3},{5,4},{6,5},{7,6},{8,7},{9,8},{10,9},{11,1... | collective-permute-start | bytes 110600 | tf_op jit(solution)/shard_map/ppermute | solution.py:418
  90.5 15.2 %copy-start.4 = (bf16[768,384]{1,0:T(8,128)(2,1)S(1)}, bf16[768,384]{1,0:T(8,128)(2,1)}, u32[]{:S(2)}) copy-start(bf16[768,384]{1,0:T(8,128)(2,1)} %weight_ref.1) | copy-start | bytes 1769476
  91.3 15.4 %all-to-all-start.3 = ((bf16[4,432,128]{2,1,0:T(8,128)(2,1)}), bf16[4,432,128]{2,1,0:T(8,128)(2,1)S(1)}, u32[]{:S(2)}, u32[]{:S(2)}) async-start(bf16[4,432,128]{2,1,0:T(8,128)(2,1)} %shard_map.160), calls=%async_computation.3 | async-start | bytes 884736 | tf_op jit(solution)/shard_map/all_to_all | solution.py:423
  94.8 10.9 %collective-permute-start.5 = (bf16[48,384]{1,0:T(8,128)(2,1)S(1)}, bf16[48,384]{1,0:T(8,128)(2,1)S(1)}, u32[]{:S(2)}, u32[]{:S(2)}) collective-permute-start(bf16[48,384]{1,0:T(8,128)(2,1)S(1)} %get-tuple-element.64), channel_id=1, source_target_pairs={{1,496},{2,497},{3,498},{4,499},{5,500},{6,501},{7,502},{8,503},{9... | collective-permute-start | bytes 110600 | tf_op jit(solution)/shard_map/ppermute | solution.py:415
  106.8 3.7 %collective-permute-start.6 = (bf16[1728,128]{1,0:T(8,128)(2,1)S(1)}, bf16[1728,128]{1,0:T(8,128)(2,1)S(1)}, u32[]{:S(2)}, u32[]{:S(2)}) collective-permute-start(bf16[1728,128]{1,0:T(8,128)(2,1)S(1)} %bitcast.11), channel_id=1, source_target_pairs={{0,16},{16,0},{1,17},{17,1},{2,18},{18,2},{3,19},{19,3},{4,20},{20... | collective-permute-start | bytes 1327112 | tf_op jit(solution)/shard_map/ppermute | solution.py:427

commit v5 on v4

--- a/solution.py
+++ b/solution.py
@@ -145,7 +145,7 @@
         found[at + HALF + 1] = jnp.zeros((16, 128), F32)
         return carry
 
-    lax.fori_loop(0, LEVS * BLOCK // SUB, eight, 0, unroll=8)
+    lax.fori_loop(0, LEVS * BLOCK // SUB, eight, 0, unroll=24)
 
     key = iota((BLOCK, 128), 1)
     for win in range(2):
@@ -182,9 +182,8 @@
     wd_ref,
     bias_ref,
     own_out,
+    low_out,
     side_out,
-    low_out,
-    corner_out,
     keep_ref,
     give_ref,
     frame,
@@ -286,9 +285,9 @@
         return part.reshape(-1, 2 * C).astype(BF16)
 
     own_out[...] = flat(result[:, OFF:, 1])
-    side_out[...] = flat(result[:, OFF:, 0])
     low_out[...] = flat(result[:, :OFF, 1])
-    corner_out[...] = flat(result[:, :OFF, 0])
+    side_out[0:BIG, :] = flat(result[:, OFF:, 0])
+    side_out[BIG:, :] = flat(result[:, :OFF, 0])
 
     small = [
         crossed(normed, d_query),
@@ -339,18 +338,16 @@
         down_ref[:, i * 128 : (i + 1) * 128] = tile(12 + i).astype(BF16)
 
 
-def finish_kernel(
-    own_ref, side_ref, low_ref, corner_ref, weight_ref, merged_ref, grad_ref, frame
-):
+def finish_kernel(own_ref, side_ref, edge_ref, weight_ref, merged_ref, grad_ref, frame):
     above = ROWS - OFF
 
-    def piece(ref, rows):
-        return ref[...].astype(F32).reshape(LEVS, rows, SUB, 2 * C)
-
-    frame[:, :above, 0] = piece(own_ref, above)
-    frame[:, above:, 0] = piece(low_ref, OFF)
-    frame[:, :above, 1] = piece(side_ref, above)
-    frame[:, above:, 1] = piece(corner_ref, OFF)
+    def piece(block, rows):
+        return block.astype(F32).reshape(LEVS, rows, SUB, 2 * C)
+
+    frame[:, :above, 0] = piece(own_ref[...], above)
+    frame[:, above:, 0] = piece(edge_ref[0:THIN, :], OFF)
+    frame[:, :above, 1] = piece(side_ref[0:BIG, :], above)
+    frame[:, above:, 1] = piece(edge_ref[THIN:, :], OFF)
     both = frame[...].reshape(FRAME, 2 * C)
     final = both[:, :C].astype(BF16)
     grad = both[:, C:].astype(BF16)
@@ -402,21 +399,13 @@
     )(*args)
 
 
-def shifted(block, lat_step, lon_step):
-    rows = lax.axis_size(LAT)
-    cols = lax.axis_size(LON)
-    if lat_step and lon_step:
-        route = [
-            (col * rows + row, (col + lon_step) % cols * rows + row + lat_step)
-            for col in range(cols)
-            for row in range(rows)
-            if 0 <= row + lat_step < rows
-        ]
-        return lax.ppermute(block, LON + LAT, route)
-    if lat_step:
-        route = [(r, r + lat_step) for r in range(rows) if 0 <= r + lat_step < rows]
-        return lax.ppermute(block, LAT, route)
-    return lax.ppermute(block, LON, [(c, (c + lon_step) % cols) for c in range(cols)])
+def shifted(block, axes, step):
+    count = lax.axis_size(axes)
+    if axes == LAT:
+        route = [(i, i + step) for i in range(count) if 0 <= i + step < count]
+    else:
+        route = [(i, (i + step) % count) for i in range(count)]
+    return lax.ppermute(block, axes, route)
 
 
 def exchange(parts, axes):
@@ -427,7 +416,9 @@
     return lax.ppermute(block, "c", [(0, 1), (1, 0)])
 
 
-def sum_kernel(parts_ref, out_ref):
+def sum_kernel(parts_ref, low_ref, side_ref, out_ref, edge_ref):
+    edge_ref[0:THIN, :] = low_ref[...]
+    edge_ref[THIN:, :] = side_ref[BIG:, :]
     count, rows, _ = parts_ref.shape
     total = parts_ref[0].astype(F32)
     for i in range(1, count):
@@ -466,7 +457,7 @@
         [((BIG, 2 * C), BF16), ((THIN, 2 * C), BF16), ((BIG + THIN, 2 * C), BF16)],
         (tokens.transpose(1, 2, 0, 3), cotangent.transpose(1, 2, 0, 3)),
     )
-    side = shifted(side, 0, 1)
+    side = shifted(side, LON, 1)
     (bias,) = call(
         bias_kernel,
         [((4, STACK, 128), BF16)],
@@ -485,7 +476,7 @@
     edge, bias, codes = lax.optimization_barrier(
         (edge, bias, (qkv_codes, proj_codes, up_codes, down_codes.T))
     )
-    edge = shifted(edge, 1, 0)
+    edge = shifted(edge, LAT, 1)
     weights = call(
         weight_kernel,
         [((3, C, C), BF16), ((C, C), BF16), ((C, FF), BF16), ((C, FF), BF16)],
@@ -493,13 +484,12 @@
         scalars=2,
         flops=1_000_000_000,
     )
-    own, side, low, corner, keep, give = call(
+    own, low, side, keep, give = call(
         main_kernel,
         [
             ((BIG, 2 * C), BF16),
-            ((BIG, 2 * C), BF16),
             ((THIN, 2 * C), BF16),
-            ((THIN, 2 * C), BF16),
+            ((BIG + THIN, 2 * C), BF16),
             ((9 * C, 128), BF16),
             ((9 * C, 128), BF16),
         ],
@@ -515,20 +505,23 @@
     padded = -(-rows // (8 * far)) * (8 * far)
     part = (keep.astype(F32) + swapped(give).astype(F32)).astype(BF16)
     part = exchange(part.reshape(near, rows, 128), NEAR)
-    side, low = shifted(side, 0, -1), shifted(low, -1, 0)
-    part, side, low = lax.optimization_barrier((part, side, low))
-    (part,) = call(sum_kernel, [((padded, 128), BF16)], (part,))
+    side = shifted(side, LON, -1)
+    part, edge = call(
+        sum_kernel,
+        [((padded, 128), BF16), ((2 * THIN, 2 * C), BF16)],
+        (part, low, side),
+    )
     part = exchange(part.reshape(far, padded // far, 128), FAR)
     (part,) = call(sum_spread_kernel, [(part.shape, BF16)], (part,))
     part = exchange(part, FAR).reshape(padded, 128)
-    part, own, corner = lax.optimization_barrier((part, own, corner))
-    corner = shifted(corner, -1, -1)
+    part, edge = lax.optimization_barrier((part, edge))
+    edge = shifted(edge, LAT, -1)
     (spread,) = call(copies_kernel, [((near, rows, 128), BF16)], (part,))
     half = exchange(spread, NEAR)
     merged, grad_tokens = call(
         finish_kernel,
         [((LEVS, ROWS // 2, COLS // 2, 2 * C), BF16), ((LEVS, ROWS, COLS, C), BF16)],
-        (own, side, low, corner, merge_weight),
+        (own, side, edge, merge_weight),
         [pltpu.VMEM((LEVS, ROWS, 2, SUB, 2 * C), F32)],
         flops=400_000_000,
     )

time: 112 us -> 112 us (level)
  waiting for transfers between devices: 17.7 us -> 15 us
  starting transfers between devices: 32.3 us -> 34.2 us
    ppermute x2, starting transfers between devices: 11.8 us -> 15 us  [swapped(): return lax.ppermute(block, 'c', [(0, 1), (1, 0)])]
    ppermute x5 -> x4, waiting for transfers between devices: 16 us -> 13.6 us  [shifted(): return lax.ppermute(block, axes, route)]
    ppermute x5 -> x4, starting transfers between devices: 13.6 us -> 12.3 us  [shifted(): return lax.ppermute(block, axes, route)]
  transfers between devices with their start and end apart: 9 -> 8, of which waited for: 6 -> 5; matrix products, arithmetic and copies ran while one was open for 1% -> 1% of each run, Pallas kernels for 5% -> 5%
where the time goes in v5:
time: 112 us; the launch traced here: 111 us
  blocking collectives  42.3 us (38%)
  starting transfers between devices  34.2 us (31%)
  waiting for transfers between devices  15 us (13%)
  Pallas kernels  14.6 us (13%)
  local copies, waits for them, and re-layouts  3.47 us (3%)
    all_to_all x2, blocking collectives, exchange(): return lax.all_to_all(parts, axes, 0, 0)  42.3 us
    ppermute x2, starting transfers between devices, swapped(): return lax.ppermute(block, 'c', [(0, 1), (1, 0)])  15 us
    pallas_call x9, Pallas kernels, call(): pl.pallas_call(kernel, out_shape=[jax.ShapeDtypeStruct(s, t) for s, t in...  14.6 us
    ppermute x4, waiting for transfers between devices, shifted(): return lax.ppermute(block, axes, route)  13.6 us
    ppermute x4, starting transfers between devices, shifted(): return lax.ppermute(block, axes, route)  12.3 us
    all_to_all x2, starting transfers between devices, exchange(): return lax.all_to_all(parts, axes, 0, 0)  6.93 us
    unnamed x24, local copies, waits for them, and re-layouts  3.34 us
  transfers between devices with their start and end apart: 8, of which 5 were waited for; matrix products, arithmetic and copies ran while one was open for 1% of the time, Pallas kernels for 5%

profile of v5, /device:TPU:1, one launch (start us, length us, event | category | flops | bytes accessed | tf_op | source)
XLA Modules:
  0.0 111.4 jit_solution(4662019746000213293)
XLA Ops:
  0.6 0.0 copy-start
  0.6 0.9 copy-done
  1.5 0.9 copy-done.1
  2.5 0.5 shard_map.154
  3.0 0.0 copy-start.7
  3.0 6.2 %collective-permute-start = (bf16[192,384]{1,0:T(8,128)(2,1)S(1)}, bf16[192,384]{1,0:T(8,128)(2,1)S(1)}, u32[]{:S(2)}, u32[]{:S(2)}) collective-permute-start(bf16[192,384]{1,0:T(8,128)(2,1)S(1)} %get-tuple-element.38), channel_id=1, source_target_pairs={{0,16},{16,32},{32,48},{48,64},{64,80},{80,96},{96,112},{112,128},... | collective-permute-start | bytes 442376 | tf_op jit(solution)/shard_map/ppermute | solution.py:408
  9.2 0.0 copy-done.10
  9.2 0.1 reshape.30.idx_ref
  9.3 0.0 copy-done.7
  9.3 0.0 copy-start.2
  9.3 0.0 copy-start.3
  9.3 0.0 copy-start.5
  9.3 3.3 %shard_map.155.bias_ref = bf16[4,576,128]{2,1,0:T(8,128)(2,1)S(1)} custom-call(s32[144,144]{1,0:T(8,128)S(1)} %reshape.30.idx_ref, bf16[6,2,3312]{2,1,0:T(2,128)(2,1)S(1)} %bitcast.18), custom_call_target="tpu_custom_call" | custom-call | flops 2000000000 | bytes 752256 | tf_op jit(solution)/shard_map/pallas_call | solution.py:391
  12.7 0.0 copy-start.6
  12.7 0.1 collective-permute-done.side_ref
  12.8 0.0 copy-start.8
  12.8 0.0 copy-start.9
  12.8 2.3 %collective-permute-start.1 = (bf16[96,384]{1,0:T(8,128)(2,1)S(1)}, bf16[96,384]{1,0:T(8,128)(2,1)S(1)}, u32[]{:S(2)}, u32[]{:S(2)}) collective-permute-start(bf16[96,384]{1,0:T(8,128)(2,1)S(1)} %pad_maximum_fusion), channel_id=1, source_target_pairs={{0,1},{1,2},{2,3},{3,4},{4,5},{5,6},{6,7},{7,8},{8,9},{9,10},{10,1... | collective-permute-start | bytes 221192 | tf_op jit(solution)/shard_map/ppermute | solution.py:408
  15.1 0.0 copy-done.2
  15.1 0.0 copy-done.3
  15.1 0.0 copy-done.5
  15.1 0.0 copy-done.6
  15.2 1.1 shard_map.156
  16.3 0.2 collective-permute-done.1.edge_ref
  16.5 6.6 %shard_map.157 = (bf16[144,384]{1,0:T(8,128)(2,1)S(1)}, bf16[48,384]{1,0:T(8,128)(2,1)S(1)}, bf16[192,384]{1,0:T(8,128)(2,1)S(1)}, bf16[1728,128]{1,0:T(8,128)(2,1)S(1)}, bf16[1728,128]{1,0:T(8,128)(2,1)S(1)}) custom-call(bf16[144,384]{1,0:T(8,128)(2,1)S(1)} %get-tuple-element.37.own_ref, bf16[192,384]{1,0:T(8,128)(2,1)S(1)} %collective-permute-done.side_ref, ...), custom_call_target="tpu_custom_call" | custom-call | flops 2000000000 | bytes 2985984 | tf_op jit(solution)/shard_map/pallas_call | solution.py:391
  23.1 10.2 %collective-permute-start.2 = (bf16[1728,128]{1,0:T(8,128)(2,1)S(1)}, bf16[1728,128]{1,0:T(8,128)(2,1)S(1)}, u32[]{:S(2)}, u32[]{:S(2)}) collective-permute-start(bf16[1728,128]{1,0:T(8,128)(2,1)S(1)} %get-tuple-element.51), channel_id=1, source_target_pairs={{0,16},{16,0},{1,17},{17,1},{2,18},{18,2},{3,19},{19,3},{4,20},{20... | collective-permute-start | bytes 1327112 | tf_op jit(solution)/shard_map/ppermute | solution.py:416
  33.3 1.4 %collective-permute-done.2 = bf16[1728,128]{1,0:T(8,128)(2,1)S(1)} collective-permute-done((bf16[1728,128]{1,0:T(8,128)(2,1)S(1)}, bf16[1728,128]{1,0:T(8,128)(2,1)S(1)}, u32[]{:S(2)}, u32[]{:S(2)}) %collective-permute-start.2) | collective-permute-done | bytes 442400 | tf_op jit(solution)/shard_map/ppermute | solution.py:416
  34.7 0.9 add_convert_fusion
  35.6 3.5 %all-to-all-start = ((bf16[4,432,128]{2,1,0:T(8,128)(2,1)}), bf16[4,432,128]{2,1,0:T(8,128)(2,1)S(1)}, u32[]{:S(2)}, u32[]{:S(2)}) async-start(bf16[4,432,128]{2,1,0:T(8,128)(2,1)} %bitcast.5), calls=%async_computation | async-start | bytes 884736 | tf_op jit(solution)/shard_map/all_to_all | solution.py:412
  39.1 2.5 %collective-permute-start.3 = (bf16[192,384]{1,0:T(8,128)(2,1)S(1)}, bf16[192,384]{1,0:T(8,128)(2,1)S(1)}, u32[]{:S(2)}, u32[]{:S(2)}) collective-permute-start(bf16[192,384]{1,0:T(8,128)(2,1)S(1)} %get-tuple-element.53), channel_id=1, source_target_pairs={{0,496},{16,0},{32,16},{48,32},{64,48},{80,64},{96,80},{112,96},{1... | collective-permute-start | bytes 442376 | tf_op jit(solution)/shard_map/ppermute | solution.py:408
  41.6 7.9 %collective-permute-done.3.side_ref = bf16[192,384]{1,0:T(8,128)(2,1)S(1)} collective-permute-done((bf16[192,384]{1,0:T(8,128)(2,1)S(1)}, bf16[192,384]{1,0:T(8,128)(2,1)S(1)}, u32[]{:S(2)}, u32[]{:S(2)}) %collective-permute-start.3) | collective-permute-done | bytes 147488 | tf_op jit(solution)/shard_map/ppermute | solution.py:408
  49.5 0.0 all-to-all-done.parts_ref
  49.5 0.1 shard_map.158
  49.5 26.8 %all_to_all.20.parts_ref = bf16[64,8,128]{2,1,0:T(8,128)(2,1)S(1)} all-to-all(bf16[64,8,128]{2,1,0:T(8,128)(2,1)S(1)} %bitcast.16), channel_id=1, replica_groups=mesh['z'=8,'xh'=2,'c'=2,'y'=8,'xl'=2] {'y','z'}, dimensions={0} | all-to-all | bytes 262144 | tf_op jit(solution)/shard_map/all_to_all | solution.py:412
  76.4 0.1 shard_map.159
  76.5 15.5 %all_to_all.21 = bf16[64,8,128]{2,1,0:T(8,128)(2,1)S(1)} all-to-all(bf16[64,8,128]{2,1,0:T(8,128)(2,1)S(1)} %shard_map.159), channel_id=1, replica_groups=mesh['z'=8,'xh'=2,'c'=2,'y'=8,'xl'=2] {'y','z'}, dimensions={0} | all-to-all | bytes 262144 | tf_op jit(solution)/shard_map/all_to_all | solution.py:412
  91.9 0.8 shard_map.160
  92.7 3.5 %all-to-all-start.3 = ((bf16[4,432,128]{2,1,0:T(8,128)(2,1)}), bf16[4,432,128]{2,1,0:T(8,128)(2,1)S(1)}, u32[]{:S(2)}, u32[]{:S(2)}) async-start(bf16[4,432,128]{2,1,0:T(8,128)(2,1)} %shard_map.160), calls=%async_computation.3 | async-start | bytes 884736 | tf_op jit(solution)/shard_map/all_to_all | solution.py:412
  96.2 1.3 %collective-permute-start.4 = (bf16[96,384]{1,0:T(8,128)(2,1)S(1)}, bf16[96,384]{1,0:T(8,128)(2,1)S(1)}, u32[]{:S(2)}, u32[]{:S(2)}) collective-permute-start(bf16[96,384]{1,0:T(8,128)(2,1)S(1)} %get-tuple-element.58), channel_id=1, source_target_pairs={{1,0},{2,1},{3,2},{4,3},{5,4},{6,5},{7,6},{8,7},{9,8},{10,9},{11,1... | collective-permute-start | bytes 221192 | tf_op jit(solution)/shard_map/ppermute | solution.py:408
  97.5 5.4 %collective-permute-done.4.edge_ref = bf16[96,384]{1,0:T(8,128)(2,1)S(1)} collective-permute-done((bf16[96,384]{1,0:T(8,128)(2,1)S(1)}, bf16[96,384]{1,0:T(8,128)(2,1)S(1)}, u32[]{:S(2)}, u32[]{:S(2)}) %collective-permute-start.4) | collective-permute-done | bytes 73760 | tf_op jit(solution)/shard_map/ppermute | solution.py:408
  102.9 0.0 copy-done.4
  102.9 1.0 shard_map.161
  104.0 0.0 all-to-all-done.3
  104.0 4.8 %collective-permute-start.5 = (bf16[1728,128]{1,0:T(8,128)(2,1)S(1)}, bf16[1728,128]{1,0:T(8,128)(2,1)S(1)}, u32[]{:S(2)}, u32[]{:S(2)}) collective-permute-start(bf16[1728,128]{1,0:T(8,128)(2,1)S(1)} %bitcast.11), channel_id=1, source_target_pairs={{0,16},{16,0},{1,17},{17,1},{2,18},{18,2},{3,19},{19,3},{4,20},{20... | collective-permute-start | bytes 1327112 | tf_op jit(solution)/shard_map/ppermute | solution.py:416
  108.8 0.7 copy.17
  109.5 0.8 copy.18
  110.3 0.0 collective-permute-done.5.other_ref
  110.3 1.1 shard_map.162
  (7 shorter events, 0.0 us)
Async XLA Ops:
  0.6 0.9 copy-start
  1.5 0.9 copy-start.1
  2.5 6.7 %copy-start.10 = (s32[20736]{0:T(1024)S(1)}, s32[20736]{0:T(1024)}, u32[]{:S(2)}) copy-start(s32[20736]{0:T(1024)} %param.20) | copy-start | bytes 248836
  3.0 6.3 %copy-start.7 = (bf16[2,1,6,3312]{3,0,2,1:T(2,128)(2,1)S(1)}, bf16[2,1,6,3312]{3,0,2,1:T(2,128)(2,1)}, u32[]{:S(2)}) copy-start(bf16[2,1,6,3312]{3,0,2,1:T(2,128)(2,1)} %param.19) | copy-start | bytes 238468
  3.0 9.8 %collective-permute-start = (bf16[192,384]{1,0:T(8,128)(2,1)S(1)}, bf16[192,384]{1,0:T(8,128)(2,1)S(1)}, u32[]{:S(2)}, u32[]{:S(2)}) collective-permute-start(bf16[192,384]{1,0:T(8,128)(2,1)S(1)} %get-tuple-element.38), channel_id=1, source_target_pairs={{0,16},{16,32},{32,48},{48,64},{64,80},{80,96},{96,112},{112,128},... | collective-permute-start | bytes 442376 | tf_op jit(solution)/shard_map/ppermute | solution.py:408
  9.3 5.8 %copy-start.2 = (s32[192,768]{1,0:T(8,128)S(1)}, s32[192,768]{1,0:T(8,128)}, u32[]{:S(2)}) copy-start(s32[192,768]{1,0:T(8,128)} %cu_ref) | copy-start | bytes 1769476
  9.3 5.8 %copy-start.3 = (s32[768,192]{0,1:T(8,128)S(1)}, s32[768,192]{0,1:T(8,128)}, u32[]{:S(2)}) copy-start(s32[768,192]{0,1:T(8,128)} %param.16) | copy-start | bytes 1769476
  9.3 5.8 %copy-start.5 = (s32[192,576]{1,0:T(8,128)S(1)}, s32[192,576]{1,0:T(8,128)}, u32[]{:S(2)}) copy-start(s32[192,576]{1,0:T(8,128)} %cq_ref) | copy-start | bytes 1327108
  12.7 2.5 %copy-start.6 = (s32[192,192]{1,0:T(8,128)S(1)}, s32[192,192]{1,0:T(8,128)}, u32[]{:S(2)}) copy-start(s32[192,192]{1,0:T(8,128)} %cp_ref) | copy-start | bytes 442372
  12.8 2.4 %copy-start.8 = (s32[4]{0:T(128)S(1)}, s32[4]{0:T(128)}, u32[]{:S(2)}) copy-start(s32[4]{0:T(128)} %bits_ref.1) | copy-start | bytes 52
  12.8 2.4 %copy-start.9 = (s32[4]{0:T(128)S(1)}, s32[4]{0:T(128)}, u32[]{:S(2)}) copy-start(s32[4]{0:T(128)} %scale_ref.1) | copy-start | bytes 52
  12.8 3.7 %collective-permute-start.1 = (bf16[96,384]{1,0:T(8,128)(2,1)S(1)}, bf16[96,384]{1,0:T(8,128)(2,1)S(1)}, u32[]{:S(2)}, u32[]{:S(2)}) collective-permute-start(bf16[96,384]{1,0:T(8,128)(2,1)S(1)} %pad_maximum_fusion), channel_id=1, source_target_pairs={{0,1},{1,2},{2,3},{3,4},{4,5},{5,6},{6,7},{7,8},{8,9},{9,10},{10,1... | collective-permute-start | bytes 221192 | tf_op jit(solution)/shard_map/ppermute | solution.py:408
  23.1 11.6 %collective-permute-start.2 = (bf16[1728,128]{1,0:T(8,128)(2,1)S(1)}, bf16[1728,128]{1,0:T(8,128)(2,1)S(1)}, u32[]{:S(2)}, u32[]{:S(2)}) collective-permute-start(bf16[1728,128]{1,0:T(8,128)(2,1)S(1)} %get-tuple-element.51), channel_id=1, source_target_pairs={{0,16},{16,0},{1,17},{17,1},{2,18},{18,2},{3,19},{19,3},{4,20},{20... | collective-permute-start | bytes 1327112 | tf_op jit(solution)/shard_map/ppermute | solution.py:416
  35.6 13.9 %all-to-all-start = ((bf16[4,432,128]{2,1,0:T(8,128)(2,1)}), bf16[4,432,128]{2,1,0:T(8,128)(2,1)S(1)}, u32[]{:S(2)}, u32[]{:S(2)}) async-start(bf16[4,432,128]{2,1,0:T(8,128)(2,1)} %bitcast.5), calls=%async_computation | async-start | bytes 884736 | tf_op jit(solution)/shard_map/all_to_all | solution.py:412
  39.1 10.4 %collective-permute-start.3 = (bf16[192,384]{1,0:T(8,128)(2,1)S(1)}, bf16[192,384]{1,0:T(8,128)(2,1)S(1)}, u32[]{:S(2)}, u32[]{:S(2)}) collective-permute-start(bf16[192,384]{1,0:T(8,128)(2,1)S(1)} %get-tuple-element.53), channel_id=1, source_target_pairs={{0,496},{16,0},{32,16},{48,32},{64,48},{80,64},{96,80},{112,96},{1... | collective-permute-start | bytes 442376 | tf_op jit(solution)/shard_map/ppermute | solution.py:408
  91.9 11.0 %copy-start.4 = (bf16[768,384]{1,0:T(8,128)(2,1)S(1)}, bf16[768,384]{1,0:T(8,128)(2,1)}, u32[]{:S(2)}) copy-start(bf16[768,384]{1,0:T(8,128)(2,1)} %weight_ref.1) | copy-start | bytes 1769476
  92.7 11.2 %all-to-all-start.3 = ((bf16[4,432,128]{2,1,0:T(8,128)(2,1)}), bf16[4,432,128]{2,1,0:T(8,128)(2,1)S(1)}, u32[]{:S(2)}, u32[]{:S(2)}) async-start(bf16[4,432,128]{2,1,0:T(8,128)(2,1)} %shard_map.160), calls=%async_computation.3 | async-start | bytes 884736 | tf_op jit(solution)/shard_map/all_to_all | solution.py:412
  96.2 6.7 %collective-permute-start.4 = (bf16[96,384]{1,0:T(8,128)(2,1)S(1)}, bf16[96,384]{1,0:T(8,128)(2,1)S(1)}, u32[]{:S(2)}, u32[]{:S(2)}) collective-permute-start(bf16[96,384]{1,0:T(8,128)(2,1)S(1)} %get-tuple-element.58), channel_id=1, source_target_pairs={{1,0},{2,1},{3,2},{4,3},{5,4},{6,5},{7,6},{8,7},{9,8},{10,9},{11,1... | collective-permute-start | bytes 221192 | tf_op jit(solution)/shard_map/ppermute | solution.py:408
  104.0 6.3 %collective-permute-start.5 = (bf16[1728,128]{1,0:T(8,128)(2,1)S(1)}, bf16[1728,128]{1,0:T(8,128)(2,1)S(1)}, u32[]{:S(2)}, u32[]{:S(2)}) collective-permute-start(bf16[1728,128]{1,0:T(8,128)(2,1)S(1)} %bitcast.11), channel_id=1, source_target_pairs={{0,16},{16,0},{1,17},{17,1},{2,18},{18,2},{3,19},{19,3},{4,20},{20... | collective-permute-start | bytes 1327112 | tf_op jit(solution)/shard_map/ppermute | solution.py:416

commit v6 on v5

--- a/solution.py
+++ b/solution.py
@@ -59,7 +59,7 @@
     return lax.dot_general(left, right, (((0,), (0,)), ((), ())), preferred_element_type=F32)
 
 
-def pack_kernel(tok_ref, cot_ref, own_ref, low_ref, side_ref):
+def pack_kernel(tok_ref, cot_ref, own_ref, side_ref, low_ref, corner_ref):
     both = jnp.concatenate(
         [ref[...].astype(F32).reshape(LEVS * ROWS * COLS, C) for ref in (tok_ref, cot_ref)], axis=-1
     ).astype(BF16)
@@ -74,9 +74,9 @@
         return product(hot.astype(F32).astype(BF16), both).astype(BF16)
 
     own_ref[...] = pick(0, ROWS - OFF, 0)
+    side_ref[...] = pick(0, ROWS - OFF, HALF)
     low_ref[...] = pick(ROWS - OFF, OFF, 0)
-    side_ref[0:BIG, :] = pick(0, ROWS - OFF, HALF)
-    side_ref[BIG:, :] = pick(ROWS - OFF, OFF, HALF)
+    corner_ref[...] = pick(ROWS - OFF, OFF, HALF)
 
 
 def weight_kernel(
@@ -175,7 +175,8 @@
 def main_kernel(
     own_ref,
     side_ref,
-    edge_ref,
+    low_ref,
+    corner_ref,
     wq_ref,
     wp_ref,
     wu_ref,
@@ -190,13 +191,13 @@
 ):
     below = ROWS - OFF
 
-    def piece(block, rows):
-        return block.astype(F32).reshape(LEVS, rows, SUB, 2 * C)
-
-    frame[:, OFF:, 1] = piece(own_ref[...], below)
-    frame[:, OFF:, 0] = piece(side_ref[0:BIG, :], below)
-    frame[:, :OFF, 1] = piece(edge_ref[0:THIN, :], OFF)
-    frame[:, :OFF, 0] = piece(edge_ref[THIN:, :], OFF)
+    def piece(ref, rows):
+        return ref[...].astype(F32).reshape(LEVS, rows, SUB, 2 * C)
+
+    frame[:, OFF:, 1] = piece(own_ref, below)
+    frame[:, OFF:, 0] = piece(side_ref, below)
+    frame[:, :OFF, 1] = piece(low_ref, OFF)
+    frame[:, :OFF, 0] = piece(corner_ref, OFF)
     both = frame[...].reshape(FRAME, 2 * C)
 
     place = iota((FRAME, C), 0)
@@ -399,13 +400,21 @@
     )(*args)
 
 
-def shifted(block, axes, step):
-    count = lax.axis_size(axes)
-    if axes == LAT:
-        route = [(i, i + step) for i in range(count) if 0 <= i + step < count]
-    else:
-        route = [(i, (i + step) % count) for i in range(count)]
-    return lax.ppermute(block, axes, route)
+def shifted(block, lat_step, lon_step):
+    rows = lax.axis_size(LAT)
+    cols = lax.axis_size(LON)
+    if lat_step and lon_step:
+        route = [
+            (col * rows + row, (col + lon_step) % cols * rows + row + lat_step)
+            for col in range(cols)
+            for row in range(rows)
+            if 0 <= row + lat_step < rows
+        ]
+        return lax.ppermute(block, LON + LAT, route)
+    if lat_step:
+        route = [(r, r + lat_step) for r in range(rows) if 0 <= r + lat_step < rows]
+        return lax.ppermute(block, LAT, route)
+    return lax.ppermute(block, LON, [(c, (c + lon_step) % cols) for c in range(cols)])
 
 
 def exchange(parts, axes):
@@ -452,12 +461,12 @@
     bias_index,
     merge_weight,
 ):
-    own, low, side = call(
+    own, side, low, corner = call(
         pack_kernel,
-        [((BIG, 2 * C), BF16), ((THIN, 2 * C), BF16), ((BIG + THIN, 2 * C), BF16)],
+        [((BIG, 2 * C), BF16)] * 2 + [((THIN, 2 * C), BF16)] * 2,
         (tokens.transpose(1, 2, 0, 3), cotangent.transpose(1, 2, 0, 3)),
     )
-    side = shifted(side, LON, 1)
+    side, low, corner = shifted(side, 0, 1), shifted(low, 1, 0), shifted(corner, 1, 1)
     (bias,) = call(
         bias_kernel,
         [((4, STACK, 128), BF16)],
@@ -472,15 +481,10 @@
         ],
         flops=2_000_000_000,
     )
-    edge = jnp.concatenate([low, side[BIG:]], axis=0)
-    edge, bias, codes = lax.optimization_barrier(
-        (edge, bias, (qkv_codes, proj_codes, up_codes, down_codes.T))
-    )
-    edge = shifted(edge, LAT, 1)
     weights = call(
         weight_kernel,
         [((3, C, C), BF16), ((C, C), BF16), ((C, FF), BF16), ((C, FF), BF16)],
-        (bit_widths, quant_scales, *codes),
+        (bit_widths, quant_scales, qkv_codes, proj_codes, up_codes, down_codes.T),
         scalars=2,
         flops=1_000_000_000,
     )
@@ -493,7 +497,7 @@
             ((9 * C, 128), BF16),
             ((9 * C, 128), BF16),
         ],
-        (own, side, edge, *weights, bias),
+        (own, side, low, corner, *weights, bias),
         [pltpu.VMEM((LEVS, ROWS, 2, SUB, 2 * C), F32)],
         flops=2_000_000_000,
         mib=32,
@@ -505,7 +509,7 @@
     padded = -(-rows // (8 * far)) * (8 * far)
     part = (keep.astype(F32) + swapped(give).astype(F32)).astype(BF16)
     part = exchange(part.reshape(near, rows, 128), NEAR)
-    side = shifted(side, LON, -1)
+    side = shifted(side, 0, -1)
     part, edge = call(
         sum_kernel,
         [((padded, 128), BF16), ((2 * THIN, 2 * C), BF16)],
@@ -515,7 +519,7 @@
     (part,) = call(sum_spread_kernel, [(part.shape, BF16)], (part,))
     part = exchange(part, FAR).reshape(padded, 128)
     part, edge = lax.optimization_barrier((part, edge))
-    edge = shifted(edge, LAT, -1)
+    edge = shifted(edge, -1, 0)
     (spread,) = call(copies_kernel, [((near, rows, 128), BF16)], (part,))
     half = exchange(spread, NEAR)
     merged, grad_tokens = call(

time: 112 us -> 109 us (0.973)
  blocking collectives: 42.3 us -> 40 us
  starting transfers between devices: 34.2 us -> 32.9 us
    ppermute x2, starting transfers between devices: 15 us -> 10.2 us  [swapped(): return lax.ppermute(block, 'c', [(0, 1), (1, 0)])]
    ppermute x4 -> x5, starting transfers between devices: 12.3 us -> 15.7 us  [the longest x1 5.58 us: shifted(): return lax.ppermute(block, LON + LAT, route)]
    all_to_all x2, blocking collectives: 42.3 us -> 40 us  [exchange(): return lax.all_to_all(parts, axes, 0, 0)]
    ppermute x4 -> x5, waiting for transfers between devices: 13.6 us -> 13.6 us  [the longest x2 8.12 us: shifted(): lax.ppermute(block, LON, [(c, (c + lon_step) % cols) for c in range(cols)])]
  transfers between devices with their start and end apart: 8 -> 9, of which waited for: 5 -> 3; matrix products, arithmetic and copies ran while one was open for 1% -> 1% of each run, Pallas kernels for 5% -> 5%
where the time goes in v6:
time: 109 us; the launch traced here: 108 us
  blocking collectives  40 us (37%)
  starting transfers between devices  32.9 us (30%)
  waiting for transfers between devices  15.1 us (14%)
  Pallas kernels  14.6 us (13%)
  local copies, waits for them, and re-layouts  4.07 us (4%)
    all_to_all x2, blocking collectives, exchange(): return lax.all_to_all(parts, axes, 0, 0)  40 us
    pallas_call x9, Pallas kernels, call(): pl.pallas_call(kernel, out_shape=[jax.ShapeDtypeStruct(s, t) for s, t in...  14.6 us
    ppermute x2, starting transfers between devices, swapped(): return lax.ppermute(block, 'c', [(0, 1), (1, 0)])  10.2 us
    ppermute x2, waiting for transfers between devices, shifted(): lax.ppermute(block, LON, [(c, (c + lon_step) % cols) for c in range(cols)])  8.12 us
    all_to_all x2, starting transfers between devices, exchange(): return lax.all_to_all(parts, axes, 0, 0)  6.96 us
    ppermute x1, starting transfers between devices, shifted(): return lax.ppermute(block, LON + LAT, route)  5.58 us
    ppermute x2, waiting for transfers between devices, shifted(): return lax.ppermute(block, LAT, route)  5.53 us
    ppermute x2, starting transfers between devices, shifted(): return lax.ppermute(block, LAT, route)  5.23 us
  transfers between devices with their start and end apart: 9, of which 3 were waited for; matrix products, arithmetic and copies ran while one was open for 1% of the time, Pallas kernels for 5%

profile of v6, /device:TPU:1, one launch (start us, length us, event | category | flops | bytes accessed | tf_op | source)
XLA Modules:
  0.0 108.4 jit_solution(5755937055727806250)
XLA Ops:
  0.6 0.0 copy-start
  0.6 0.9 copy-done
  1.5 0.9 copy-done.1
  2.5 0.5 shard_map.154
  3.0 3.9 %collective-permute-start.1 = (bf16[48,384]{1,0:T(8,128)(2,1)S(1)}, bf16[48,384]{1,0:T(8,128)(2,1)S(1)}, u32[]{:S(2)}, u32[]{:S(2)}) collective-permute-start(bf16[48,384]{1,0:T(8,128)(2,1)S(1)} %get-tuple-element.34), channel_id=1, source_target_pairs={{0,1},{1,2},{2,3},{3,4},{4,5},{5,6},{6,7},{7,8},{8,9},{9,10},{10,1... | collective-permute-start | bytes 110600 | tf_op jit(solution)/shard_map/ppermute | solution.py:416
  6.9 5.6 %collective-permute-start.2 = (bf16[48,384]{1,0:T(8,128)(2,1)S(1)}, bf16[48,384]{1,0:T(8,128)(2,1)S(1)}, u32[]{:S(2)}, u32[]{:S(2)}) collective-permute-start(bf16[48,384]{1,0:T(8,128)(2,1)S(1)} %get-tuple-element.35), channel_id=1, source_target_pairs={{0,17},{1,18},{2,19},{3,20},{4,21},{5,22},{6,23},{7,24},{8,25},{9,... | collective-permute-start | bytes 110600 | tf_op jit(solution)/shard_map/ppermute | solution.py:413
  12.5 0.0 copy-start.7
  12.5 2.7 %collective-permute-start = (bf16[144,384]{1,0:T(8,128)(2,1)S(1)}, bf16[144,384]{1,0:T(8,128)(2,1)S(1)}, u32[]{:S(2)}, u32[]{:S(2)}) collective-permute-start(bf16[144,384]{1,0:T(8,128)(2,1)S(1)} %get-tuple-element.33), channel_id=1, source_target_pairs={{0,16},{16,32},{32,48},{48,64},{64,80},{80,96},{96,112},{112,128},... | collective-permute-start | bytes 331784 | tf_op jit(solution)/shard_map/ppermute | solution.py:417
  15.2 0.0 copy-done.10
  15.2 0.1 reshape.30.idx_ref
  15.3 0.0 copy-done.7
  15.4 0.0 copy-start.2
  15.4 0.0 copy-start.3
  15.4 0.0 copy-start.5
  15.4 0.0 copy-start.6
  15.4 3.3 %shard_map.156.bias_ref = bf16[4,576,128]{2,1,0:T(8,128)(2,1)S(1)} custom-call(s32[144,144]{1,0:T(8,128)S(1)} %reshape.30.idx_ref, bf16[6,2,3312]{2,1,0:T(2,128)(2,1)S(1)} %bitcast.18), custom_call_target="tpu_custom_call" | custom-call | flops 2000000000 | bytes 752256 | tf_op jit(solution)/shard_map/pallas_call | solution.py:392
  18.7 0.0 copy-start.8
  18.7 0.0 copy-start.9
  18.7 0.0 copy-done.2
  18.8 0.6 copy-done.8
  19.4 0.0 copy-done.9
  19.4 1.1 shard_map.155
  20.5 0.0 collective-permute-done.1.low_ref
  20.5 0.0 collective-permute-done.2.corner_ref
  20.5 0.0 collective-permute-done.side_ref
  20.5 6.6 %shard_map.157 = (bf16[144,384]{1,0:T(8,128)(2,1)S(1)}, bf16[48,384]{1,0:T(8,128)(2,1)S(1)}, bf16[192,384]{1,0:T(8,128)(2,1)S(1)}, bf16[1728,128]{1,0:T(8,128)(2,1)S(1)}, bf16[1728,128]{1,0:T(8,128)(2,1)S(1)}) custom-call(bf16[144,384]{1,0:T(8,128)(2,1)S(1)} %get-tuple-element.32.own_ref, bf16[144,384]{1,0:T(8,128)(2,1)S(1)} %collective-permute-done.side_ref, ...), custom_call_target="tpu_custom_call" | custom-call | flops 2000000000 | bytes 2949120 | tf_op jit(solution)/shard_map/pallas_call | solution.py:392
  27.1 5.4 %collective-permute-start.3 = (bf16[1728,128]{1,0:T(8,128)(2,1)S(1)}, bf16[1728,128]{1,0:T(8,128)(2,1)S(1)}, u32[]{:S(2)}, u32[]{:S(2)}) collective-permute-start(bf16[1728,128]{1,0:T(8,128)(2,1)S(1)} %get-tuple-element.41), channel_id=1, source_target_pairs={{0,16},{16,0},{1,17},{17,1},{2,18},{18,2},{3,19},{19,3},{4,20},{20... | collective-permute-start | bytes 1327112 | tf_op jit(solution)/shard_map/ppermute | solution.py:425
  32.5 1.4 %collective-permute-done.3 = bf16[1728,128]{1,0:T(8,128)(2,1)S(1)} collective-permute-done((bf16[1728,128]{1,0:T(8,128)(2,1)S(1)}, bf16[1728,128]{1,0:T(8,128)(2,1)S(1)}, u32[]{:S(2)}, u32[]{:S(2)}) %collective-permute-start.3) | collective-permute-done | bytes 442400 | tf_op jit(solution)/shard_map/ppermute | solution.py:425
  33.9 0.9 add_convert_fusion
  34.8 3.5 %all-to-all-start = ((bf16[4,432,128]{2,1,0:T(8,128)(2,1)}), bf16[4,432,128]{2,1,0:T(8,128)(2,1)S(1)}, u32[]{:S(2)}, u32[]{:S(2)}) async-start(bf16[4,432,128]{2,1,0:T(8,128)(2,1)} %bitcast.5), calls=%async_computation | async-start | bytes 884736 | tf_op jit(solution)/shard_map/all_to_all | solution.py:421
  38.3 2.3 %collective-permute-start.4 = (bf16[192,384]{1,0:T(8,128)(2,1)S(1)}, bf16[192,384]{1,0:T(8,128)(2,1)S(1)}, u32[]{:S(2)}, u32[]{:S(2)}) collective-permute-start(bf16[192,384]{1,0:T(8,128)(2,1)S(1)} %get-tuple-element.43), channel_id=1, source_target_pairs={{0,496},{16,0},{32,16},{48,32},{64,48},{80,64},{96,80},{112,96},{1... | collective-permute-start | bytes 442376 | tf_op jit(solution)/shard_map/ppermute | solution.py:417
  40.6 8.1 %collective-permute-done.4.side_ref = bf16[192,384]{1,0:T(8,128)(2,1)S(1)} collective-permute-done((bf16[192,384]{1,0:T(8,128)(2,1)S(1)}, bf16[192,384]{1,0:T(8,128)(2,1)S(1)}, u32[]{:S(2)}, u32[]{:S(2)}) %collective-permute-start.4) | collective-permute-done | bytes 147488 | tf_op jit(solution)/shard_map/ppermute | solution.py:417
  48.7 0.0 all-to-all-done.parts_ref
  48.7 0.1 shard_map.158
  48.8 24.5 %all_to_all.20.parts_ref = bf16[64,8,128]{2,1,0:T(8,128)(2,1)S(1)} all-to-all(bf16[64,8,128]{2,1,0:T(8,128)(2,1)S(1)} %bitcast.16), channel_id=1, replica_groups=mesh['z'=8,'xh'=2,'c'=2,'y'=8,'xl'=2] {'y','z'}, dimensions={0} | all-to-all | bytes 262144 | tf_op jit(solution)/shard_map/all_to_all | solution.py:421
  73.3 0.1 shard_map.159
  73.4 15.5 %all_to_all.21 = bf16[64,8,128]{2,1,0:T(8,128)(2,1)S(1)} all-to-all(bf16[64,8,128]{2,1,0:T(8,128)(2,1)S(1)} %shard_map.159), channel_id=1, replica_groups=mesh['z'=8,'xh'=2,'c'=2,'y'=8,'xl'=2] {'y','z'}, dimensions={0} | all-to-all | bytes 262144 | tf_op jit(solution)/shard_map/all_to_all | solution.py:421
  88.8 0.8 shard_map.160
  89.7 3.5 %all-to-all-start.3 = ((bf16[4,432,128]{2,1,0:T(8,128)(2,1)}), bf16[4,432,128]{2,1,0:T(8,128)(2,1)S(1)}, u32[]{:S(2)}, u32[]{:S(2)}) async-start(bf16[4,432,128]{2,1,0:T(8,128)(2,1)} %shard_map.160), calls=%async_computation.3 | async-start | bytes 884736 | tf_op jit(solution)/shard_map/all_to_all | solution.py:421
  93.2 1.3 %collective-permute-start.5 = (bf16[96,384]{1,0:T(8,128)(2,1)S(1)}, bf16[96,384]{1,0:T(8,128)(2,1)S(1)}, u32[]{:S(2)}, u32[]{:S(2)}) collective-permute-start(bf16[96,384]{1,0:T(8,128)(2,1)S(1)} %get-tuple-element.48), channel_id=1, source_target_pairs={{1,0},{2,1},{3,2},{4,3},{5,4},{6,5},{7,6},{8,7},{9,8},{10,9},{11,1... | collective-permute-start | bytes 221192 | tf_op jit(solution)/shard_map/ppermute | solution.py:416
  94.5 5.5 %collective-permute-done.5.edge_ref = bf16[96,384]{1,0:T(8,128)(2,1)S(1)} collective-permute-done((bf16[96,384]{1,0:T(8,128)(2,1)S(1)}, bf16[96,384]{1,0:T(8,128)(2,1)S(1)}, u32[]{:S(2)}, u32[]{:S(2)}) %collective-permute-start.5) | collective-permute-done | bytes 73760 | tf_op jit(solution)/shard_map/ppermute | solution.py:416
  100.0 1.0 shard_map.161
  101.0 0.0 all-to-all-done.3
  101.1 4.8 %collective-permute-start.6 = (bf16[1728,128]{1,0:T(8,128)(2,1)S(1)}, bf16[1728,128]{1,0:T(8,128)(2,1)S(1)}, u32[]{:S(2)}, u32[]{:S(2)}) collective-permute-start(bf16[1728,128]{1,0:T(8,128)(2,1)S(1)} %bitcast.11), channel_id=1, source_target_pairs={{0,16},{16,0},{1,17},{17,1},{2,18},{18,2},{3,19},{19,3},{4,20},{20... | collective-permute-start | bytes 1327112 | tf_op jit(solution)/shard_map/ppermute | solution.py:425
  105.8 0.7 copy.17
  106.5 0.8 copy.18
  107.3 0.0 collective-permute-done.6.other_ref
  107.3 1.1 shard_map.162
  (7 shorter events, 0.0 us)
Async XLA Ops:
  0.6 0.9 copy-start
  1.5 0.9 copy-start.1
  2.5 12.7 %copy-start.10 = (s32[20736]{0:T(1024)S(1)}, s32[20736]{0:T(1024)}, u32[]{:S(2)}) copy-start(s32[20736]{0:T(1024)} %param.20) | copy-start | bytes 248836
  3.0 17.5 %collective-permute-start.1 = (bf16[48,384]{1,0:T(8,128)(2,1)S(1)}, bf16[48,384]{1,0:T(8,128)(2,1)S(1)}, u32[]{:S(2)}, u32[]{:S(2)}) collective-permute-start(bf16[48,384]{1,0:T(8,128)(2,1)S(1)} %get-tuple-element.34), channel_id=1, source_target_pairs={{0,1},{1,2},{2,3},{3,4},{4,5},{5,6},{6,7},{7,8},{8,9},{9,10},{10,1... | collective-permute-start | bytes 110600 | tf_op jit(solution)/shard_map/ppermute | solution.py:416
  6.9 13.6 %collective-permute-start.2 = (bf16[48,384]{1,0:T(8,128)(2,1)S(1)}, bf16[48,384]{1,0:T(8,128)(2,1)S(1)}, u32[]{:S(2)}, u32[]{:S(2)}) collective-permute-start(bf16[48,384]{1,0:T(8,128)(2,1)S(1)} %get-tuple-element.35), channel_id=1, source_target_pairs={{0,17},{1,18},{2,19},{3,20},{4,21},{5,22},{6,23},{7,24},{8,25},{9,... | collective-permute-start | bytes 110600 | tf_op jit(solution)/shard_map/ppermute | solution.py:413
  12.5 2.8 %copy-start.7 = (bf16[2,1,6,3312]{3,0,2,1:T(2,128)(2,1)S(1)}, bf16[2,1,6,3312]{3,0,2,1:T(2,128)(2,1)}, u32[]{:S(2)}) copy-start(bf16[2,1,6,3312]{3,0,2,1:T(2,128)(2,1)} %param.19) | copy-start | bytes 238468
  12.5 8.0 %collective-permute-start = (bf16[144,384]{1,0:T(8,128)(2,1)S(1)}, bf16[144,384]{1,0:T(8,128)(2,1)S(1)}, u32[]{:S(2)}, u32[]{:S(2)}) collective-permute-start(bf16[144,384]{1,0:T(8,128)(2,1)S(1)} %get-tuple-element.33), channel_id=1, source_target_pairs={{0,16},{16,32},{32,48},{48,64},{64,80},{80,96},{96,112},{112,128},... | collective-permute-start | bytes 331784 | tf_op jit(solution)/shard_map/ppermute | solution.py:417
  15.4 3.4 %copy-start.2 = (s32[192,768]{1,0:T(8,128)S(1)}, s32[192,768]{1,0:T(8,128)}, u32[]{:S(2)}) copy-start(s32[192,768]{1,0:T(8,128)} %cu_ref.1) | copy-start | bytes 1769476
  15.4 3.4 %copy-start.3 = (s32[768,192]{0,1:T(8,128)S(1)}, s32[768,192]{0,1:T(8,128)}, u32[]{:S(2)}) copy-start(s32[768,192]{0,1:T(8,128)} %param.16) | copy-start | bytes 1769476
  15.4 3.4 %copy-start.5 = (s32[192,576]{1,0:T(8,128)S(1)}, s32[192,576]{1,0:T(8,128)}, u32[]{:S(2)}) copy-start(s32[192,576]{1,0:T(8,128)} %cq_ref.1) | copy-start | bytes 1327108
  15.4 3.4 %copy-start.6 = (s32[192,192]{1,0:T(8,128)S(1)}, s32[192,192]{1,0:T(8,128)}, u32[]{:S(2)}) copy-start(s32[192,192]{1,0:T(8,128)} %cp_ref.1) | copy-start | bytes 442372
  18.7 0.7 copy-start.8
  18.7 0.7 copy-start.9
  27.1 6.8 %collective-permute-start.3 = (bf16[1728,128]{1,0:T(8,128)(2,1)S(1)}, bf16[1728,128]{1,0:T(8,128)(2,1)S(1)}, u32[]{:S(2)}, u32[]{:S(2)}) collective-permute-start(bf16[1728,128]{1,0:T(8,128)(2,1)S(1)} %get-tuple-element.41), channel_id=1, source_target_pairs={{0,16},{16,0},{1,17},{17,1},{2,18},{18,2},{3,19},{19,3},{4,20},{20... | collective-permute-start | bytes 1327112 | tf_op jit(solution)/shard_map/ppermute | solution.py:425
  34.8 13.9 %all-to-all-start = ((bf16[4,432,128]{2,1,0:T(8,128)(2,1)}), bf16[4,432,128]{2,1,0:T(8,128)(2,1)S(1)}, u32[]{:S(2)}, u32[]{:S(2)}) async-start(bf16[4,432,128]{2,1,0:T(8,128)(2,1)} %bitcast.5), calls=%async_computation | async-start | bytes 884736 | tf_op jit(solution)/shard_map/all_to_all | solution.py:421
  38.3 10.4 %collective-permute-start.4 = (bf16[192,384]{1,0:T(8,128)(2,1)S(1)}, bf16[192,384]{1,0:T(8,128)(2,1)S(1)}, u32[]{:S(2)}, u32[]{:S(2)}) collective-permute-start(bf16[192,384]{1,0:T(8,128)(2,1)S(1)} %get-tuple-element.43), channel_id=1, source_target_pairs={{0,496},{16,0},{32,16},{48,32},{64,48},{80,64},{96,80},{112,96},{1... | collective-permute-start | bytes 442376 | tf_op jit(solution)/shard_map/ppermute | solution.py:417
  88.8 11.2 %copy-start.4 = (bf16[768,384]{1,0:T(8,128)(2,1)S(1)}, bf16[768,384]{1,0:T(8,128)(2,1)}, u32[]{:S(2)}) copy-start(bf16[768,384]{1,0:T(8,128)(2,1)} %weight_ref.1) | copy-start | bytes 1769476
  89.7 11.4 %all-to-all-start.3 = ((bf16[4,432,128]{2,1,0:T(8,128)(2,1)}), bf16[4,432,128]{2,1,0:T(8,128)(2,1)S(1)}, u32[]{:S(2)}, u32[]{:S(2)}) async-start(bf16[4,432,128]{2,1,0:T(8,128)(2,1)} %shard_map.160), calls=%async_computation.3 | async-start | bytes 884736 | tf_op jit(solution)/shard_map/all_to_all | solution.py:421
  93.2 6.8 %collective-permute-start.5 = (bf16[96,384]{1,0:T(8,128)(2,1)S(1)}, bf16[96,384]{1,0:T(8,128)(2,1)S(1)}, u32[]{:S(2)}, u32[]{:S(2)}) collective-permute-start(bf16[96,384]{1,0:T(8,128)(2,1)S(1)} %get-tuple-element.48), channel_id=1, source_target_pairs={{1,0},{2,1},{3,2},{4,3},{5,4},{6,5},{7,6},{8,7},{9,8},{10,9},{11,1... | collective-permute-start | bytes 221192 | tf_op jit(solution)/shard_map/ppermute | solution.py:416
  101.1 6.3 %collective-permute-start.6 = (bf16[1728,128]{1,0:T(8,128)(2,1)S(1)}, bf16[1728,128]{1,0:T(8,128)(2,1)S(1)}, u32[]{:S(2)}, u32[]{:S(2)}) collective-permute-start(bf16[1728,128]{1,0:T(8,128)(2,1)S(1)} %bitcast.11), channel_id=1, source_target_pairs={{0,16},{16,0},{1,17},{17,1},{2,18},{18,2},{3,19},{19,3},{4,20},{20... | collective-permute-start | bytes 1327112 | tf_op jit(solution)/shard_map/ppermute | solution.py:425

commit v7 on v6

--- a/solution.py
+++ b/solution.py
@@ -24,11 +24,11 @@
 OFF = WLAT // 2
 HALF = WLON // 2
 SUB = 8
-FRAME = LEVS * ROWS * 2 * SUB
+FRAME = LEVS * ROWS * COLS
 BLOCK = FRAME // 4
 STACK = HEADS * BLOCK
-BIG = LEVS * (ROWS - OFF) * SUB
-THIN = LEVS * OFF * SUB
+BIG = 112
+THIN = 48
 LOWS = 256
 HIGHS = -(-POS // LOWS)
 
@@ -59,44 +59,73 @@
     return lax.dot_general(left, right, (((0,), (0,)), ((), ())), preferred_element_type=F32)
 
 
+def over(values, size):
+    return ((values.astype(F32) + 0.5) * (1.0 / size)).astype(jnp.int32)
+
+
+def in_piece(at, count):
+    lev = jnp.where(at >= count * HALF, 1, 0)
+    rest = at - lev * (count * HALF)
+    row = over(rest, HALF)
+    return lev, row, rest - row * HALF, (at >= 0) & (at < LEVS * count * HALF)
+
+
+def frame_place(at):
+    place = jnp.full(at.shape, -1, jnp.int32)
+    first = 0
+    for size, count, half in ((BIG, ROWS - OFF, 1), (THIN, OFF, 1), (BIG, ROWS - OFF, 0), (THIN, OFF, 0)):
+        lev, row, sub, used = in_piece(at - first, count)
+        skip = ROWS - count if count != OFF else 0
+        token = (lev * ROWS + row + skip) * COLS + half * HALF + sub
+        place = jnp.where(used, token, place)
+        first += size
+    return place
+
+
+def one_hot(match):
+    return match.astype(F32).astype(BF16)
+
+
 def pack_kernel(tok_ref, cot_ref, own_ref, side_ref, low_ref, corner_ref):
     both = jnp.concatenate(
         [ref[...].astype(F32).reshape(LEVS * ROWS * COLS, C) for ref in (tok_ref, cot_ref)], axis=-1
     ).astype(BF16)
 
-    def pick(first, count, col):
-        shape = (LEVS * count * SUB, LEVS * ROWS * COLS)
-        to = iota(shape, 0)
-        lev = jnp.where(to >= count * SUB, 1, 0)
-        row = (to >> 3) - lev * count + first
-        sub = jnp.bitwise_and(to, SUB - 1)
-        hot = (iota(shape, 1) == (row * COLS + col + sub) * 2 + lev) & (sub < HALF)
-        return product(hot.astype(F32).astype(BF16), both).astype(BF16)
-
-    own_ref[...] = pick(0, ROWS - OFF, 0)
-    side_ref[...] = pick(0, ROWS - OFF, HALF)
-    low_ref[...] = pick(ROWS - OFF, OFF, 0)
-    corner_ref[...] = pick(ROWS - OFF, OFF, HALF)
-
-
-def weight_kernel(
-    bits_ref, scale_ref, cq_ref, cp_ref, cu_ref, cd_ref, wq_ref, wp_ref, wu_ref, wd_ref
-):
-    def dequant(codes, layer, fan_in):
-        limit = jnp.left_shift(1, bits_ref[layer] - 1) - 1
-        clipped = jnp.minimum(jnp.maximum(codes, -limit), limit).astype(F32)
-        whole = jnp.full((1, 128), scale_ref[layer], jnp.int32).astype(F32)
-        return clipped * (math.sqrt(C / fan_in) / whole)[:, :1]
-
-    full = dequant(cq_ref[...], 0, C)
+    def pick(first, count, col, size):
+        shape = (size, LEVS * ROWS * COLS)
+        lev, row, sub, used = in_piece(iota(shape, 0), count)
+        token = ((row + first) * COLS + col + sub) * 2 + lev
+        return product(one_hot((iota(shape, 1) == token) & used), both).astype(BF16)
+
+    own_ref[...] = pick(0, ROWS - OFF, 0, BIG)
+    side_ref[...] = pick(0, ROWS - OFF, HALF, BIG)
+    low_ref[...] = pick(ROWS - OFF, OFF, 0, THIN)
+    corner_ref[...] = pick(ROWS - OFF, OFF, HALF, THIN)
+
+
+def weight_kernel(quant_ref, cq_ref, cp_ref, cu_ref, cd_ref, wq_ref, wp_ref, wu_ref, wd_ref):
+    def dequant(codes, layer):
+        limit = quant_ref[layer : layer + 1, 0:1]
+        factor = quant_ref[layer + 4 : layer + 5, 0:1]
+        return jnp.minimum(jnp.maximum(codes.astype(F32), -limit), limit) * factor
+
+    full = dequant(cq_ref[...], 0)
     for part in range(3):
         wq_ref[part] = full[:, part * C : (part + 1) * C].astype(BF16)
-    wp_ref[...] = dequant(cp_ref[...], 1, C).astype(BF16)
-    wu_ref[...] = dequant(cu_ref[...], 2, C).astype(BF16)
-    wd_ref[...] = dequant(cd_ref[...], 3, FF).astype(BF16)
-
-
-def bias_kernel(idx_ref, tab_ref, bias_ref, rows, places, found):
+    wp_ref[...] = dequant(cp_ref[...], 1).astype(BF16)
+    wu_ref[...] = dequant(cu_ref[...], 2).astype(BF16)
+    wd_ref[...] = dequant(cd_ref[...], 3).astype(BF16)
+
+
+def bias_kernel(
+    bits_ref, scale_ref, idx_ref, tab_ref, bias_ref, quant_ref, rows, places, found
+):
+    for layer, fan_in in enumerate((C, C, C, FF)):
+        limit = jnp.left_shift(1, bits_ref[layer] - 1) - 1
+        quant_ref[layer : layer + 1, :] = jnp.full((1, 128), limit, jnp.int32).astype(F32)
+        scale = jnp.full((1, 128), scale_ref[layer], jnp.int32).astype(F32)
+        quant_ref[layer + 4 : layer + 5, :] = math.sqrt(C / fan_in) / scale
+
     rows[...] = jnp.zeros_like(rows)
     for head in range(HEADS):
         table = tab_ref[head].astype(F32)
@@ -108,23 +137,13 @@
     table = rows[...].astype(BF16)
 
     index = idx_ref[...]
-    parts = [
-        lax.shift_right_logical(index, 8).astype(F32).astype(BF16),
-        jnp.bitwise_and(index, LOWS - 1).astype(F32).astype(BF16),
-    ]
-
-    def token(where):
-        sub = jnp.bitwise_and(where, SUB - 1)
-        inside = (where >> 4) * WLON + jnp.bitwise_and(where >> 3, 1) * HALF + sub
-        return jnp.where((sub < HALF) & (where < BLOCK), inside, -1000)
-
+    places[...] = jnp.zeros_like(places)
     for lev in range(LEVS):
-        base = (1 - lev) * (WTOK // 2)
-        pick_q = (iota((BLOCK, WTOK), 1) == token(iota((BLOCK, WTOK), 0)) + base).astype(F32)
-        pick_k = (iota((WTOK, 128), 0) == token(iota((WTOK, 128), 1)) + base).astype(F32)
-        for i, part in enumerate(parts):
-            moved = product(product(pick_q.astype(BF16), part).astype(BF16), pick_k.astype(BF16))
-            places[i, lev * BLOCK : (lev + 1) * BLOCK, :] = moved
+        base = (1 - lev) * BLOCK
+        inside = index[base : base + BLOCK, base : base + BLOCK]
+        at = slice(lev * BLOCK, (lev + 1) * BLOCK)
+        places[0, at, 0:BLOCK] = lax.shift_right_logical(inside, 8).astype(F32)
+        places[1, at, 0:BLOCK] = jnp.bitwise_and(inside, LOWS - 1).astype(F32)
 
     entry = iota((LOWS, 128), 0).astype(F32)
 
@@ -132,31 +151,27 @@
         at = pl.multiple_of(group * SUB, SUB)
         high = places[0, pl.ds(at, SUB), :]
         low = places[1, pl.ds(at, SUB), :]
-        hot = [(entry == low[s : s + 1]).astype(F32).astype(BF16) for s in range(HALF)]
+        hot = [one_hot(entry == low[s : s + 1]) for s in range(SUB)]
         values = product(table, jnp.concatenate(hot, axis=1))
-        for s in range(HALF):
+        for s in range(SUB):
             chosen = jnp.zeros((16, 128), F32)
             here = jnp.broadcast_to(high[s : s + 1], (16, 128))
             for i in range(HIGHS):
                 candidate = values[i * 16 : (i + 1) * 16, s * 128 : (s + 1) * 128]
                 chosen = jnp.where(here == float(i), candidate, chosen)
             found[at + s] = chosen
-        found[at + HALF] = jnp.zeros((16, 128), F32)
-        found[at + HALF + 1] = jnp.zeros((16, 128), F32)
         return carry
 
-    lax.fori_loop(0, LEVS * BLOCK // SUB, eight, 0, unroll=24)
+    lax.fori_loop(0, LEVS * BLOCK // SUB, eight, 0, unroll=18)
 
     key = iota((BLOCK, 128), 1)
     for win in range(2):
-        row = lax.axis_index(LAT) * ROWS - OFF + win * WLAT + (key >> 4)
-        usable = (row >= 0) & (row < lax.axis_size(LAT) * ROWS - LAT_PAD)
-        usable = usable & (jnp.bitwise_and(key, SUB - 1) < HALF) & (key < BLOCK)
+        row = lax.axis_index(LAT) * ROWS - OFF + win * WLAT + over(key, WLON)
+        usable = (row >= 0) & (row < lax.axis_size(LAT) * ROWS - LAT_PAD) & (key < BLOCK)
         for lev in range(LEVS):
             for head in range(HEADS):
                 values = found[lev * BLOCK : (lev + 1) * BLOCK, head * 2 + win, :]
-                values = jnp.where(usable, values, MASKED)
-                bias_ref[lev * 2 + win, head * BLOCK : (head + 1) * BLOCK, :] = values.astype(BF16)
+                bias_ref[lev * 2 + win, head] = jnp.where(usable, values, MASKED)
 
 
 def unit(values):
@@ -187,40 +202,33 @@
     side_out,
     keep_ref,
     give_ref,
-    frame,
 ):
-    below = ROWS - OFF
-
-    def piece(ref, rows):
-        return ref[...].astype(F32).reshape(LEVS, rows, SUB, 2 * C)
-
-    frame[:, OFF:, 1] = piece(own_ref, below)
-    frame[:, OFF:, 0] = piece(side_ref, below)
-    frame[:, :OFF, 1] = piece(low_ref, OFF)
-    frame[:, :OFF, 0] = piece(corner_ref, OFF)
-    both = frame[...].reshape(FRAME, 2 * C)
+    total = 2 * (BIG + THIN)
+    pieces = [ref[...] for ref in (own_ref, low_ref, side_ref, corner_ref)]
+    shape = (FRAME, total)
+    order = one_hot(iota(shape, 0) == frame_place(iota(shape, 1)))
+    both = product(order, jnp.concatenate(pieces, axis=0))
 
     place = iota((FRAME, C), 0)
-    row = lax.axis_index(LAT) * ROWS - OFF + (place >> 4) - jnp.where(place >= FRAME // 2, ROWS, 0)
+    row = lax.axis_index(LAT) * ROWS - OFF + over(place, COLS)
+    row = row - jnp.where(place >= FRAME // 2, ROWS, 0)
     valid = (row >= 0) & (row < lax.axis_size(LAT) * ROWS - LAT_PAD)
-    valid = valid & (jnp.bitwise_and(place, SUB - 1) < HALF)
     start = jnp.where(valid, both[:, :C], 0.0)
     d_out = jnp.where(valid, both[:, C:], 0.0)
     d_out_low = d_out.astype(BF16)
 
     normal, scale = unit(start)
     normed = normal.astype(BF16)
-    query = product(normed, wq_ref[0]).astype(BF16)
-    key = product(normed, wq_ref[1]).astype(BF16)
-    value = product(normed, wq_ref[2]).astype(BF16)
+    query = product(normed, wq_ref[0]).astype(BF16).astype(F32)
+    key = product(normed, wq_ref[1]).astype(BF16).astype(F32)
+    value = product(normed, wq_ref[2]).astype(BF16).astype(F32)
 
     lane_head = iota((HEADS, 1, C), 2) >> 5
     head_mask = lane_head == iota((HEADS, 1, C), 0)
-    mask_low = head_mask.astype(F32).astype(BF16)
     mask_full = head_mask.astype(F32)
 
     def spread_heads(block):
-        return (block[None] * mask_low).reshape(STACK, C)
+        return (block[None] * mask_full).reshape(STACK, C).astype(BF16)
 
     def join_heads(stacked):
         return jnp.sum(stacked.reshape(HEADS, BLOCK, C) * mask_full, axis=0)
@@ -230,12 +238,12 @@
     for block in range(4):
         at = slice(block * BLOCK, (block + 1) * BLOCK)
         q_stack = spread_heads(query[at])
-        scores = across(q_stack, key[at]) * HEAD_DIM ** (-0.5)
-        scores = scores + bias_ref[block][:, :BLOCK].astype(F32)
+        scores = across(q_stack, key[at].astype(BF16)) * HEAD_DIM ** (-0.5)
+        scores = scores + bias_ref[block].reshape(STACK, 128)[:, :BLOCK]
         weights = jnp.exp(scores - jnp.max(scores, axis=-1, keepdims=True))
         weights = weights / jnp.sum(weights, axis=-1, keepdims=True)
         weights_low = weights.astype(BF16)
-        heads_parts.append(join_heads(product(weights_low, value[at])))
+        heads_parts.append(join_heads(product(weights_low, value[at].astype(BF16))))
         saved.append((q_stack, weights, weights_low))
     heads = jnp.concatenate(heads_parts, axis=0).astype(BF16)
 
@@ -257,7 +265,7 @@
     d_pre = (slope * d_hidden).astype(BF16)
     d_normed_two = across(d_pre, wu_ref[...]).astype(BF16).astype(F32)
     d_resid = (d_out + unit_back(normal_two, scale_two, d_normed_two)).astype(BF16)
-    d_heads = across(d_resid, wp_ref[...]).astype(BF16)
+    d_heads = across(d_resid, wp_ref[...]).astype(BF16).astype(F32)
 
     dq_parts = []
     dk_parts = []
@@ -266,11 +274,11 @@
         at = slice(block * BLOCK, (block + 1) * BLOCK)
         q_stack, weights, weights_low = saved[block]
         d_stack = spread_heads(d_heads[at])
-        d_weights = across(d_stack, value[at]).astype(BF16).astype(F32)
+        d_weights = across(d_stack, value[at].astype(BF16)).astype(BF16).astype(F32)
         dv_parts.append(crossed(weights_low, d_stack))
         inside = jnp.sum(weights * d_weights, axis=-1, keepdims=True)
         d_scores = (weights * (d_weights - inside) * HEAD_DIM ** (-0.5)).astype(BF16)
-        dq_parts.append(join_heads(product(d_scores, key[at])))
+        dq_parts.append(join_heads(product(d_scores, key[at].astype(BF16))))
         dk_parts.append(crossed(d_scores, q_stack))
     d_query = jnp.concatenate(dq_parts, axis=0).astype(BF16)
     d_key = jnp.concatenate(dk_parts, axis=0).astype(BF16)
@@ -280,15 +288,13 @@
     d_normed = d_normed.astype(BF16).astype(F32)
     grad = jnp.where(valid, d_resid.astype(F32) + unit_back(normal, scale, d_normed), 0.0)
 
-    result = jnp.concatenate([final, grad], axis=-1).reshape(LEVS, ROWS, 2, SUB, 2 * C)
-
-    def flat(part):
-        return part.reshape(-1, 2 * C).astype(BF16)
-
-    own_out[...] = flat(result[:, OFF:, 1])
-    low_out[...] = flat(result[:, :OFF, 1])
-    side_out[0:BIG, :] = flat(result[:, OFF:, 0])
-    side_out[BIG:, :] = flat(result[:, :OFF, 0])
+    result = jnp.concatenate([final, grad], axis=-1).astype(BF16)
+    shape = (total, FRAME)
+    order = one_hot(iota(shape, 1) == frame_place(iota(shape, 0)))
+    parted = product(order, result).astype(BF16)
+    own_out[...] = parted[0:BIG]
+    low_out[...] = parted[BIG : BIG + THIN]
+    side_out[...] = parted[BIG + THIN :]
 
     small = [
         crossed(normed, d_query),
@@ -339,40 +345,38 @@
         down_ref[:, i * 128 : (i + 1) * 128] = tile(12 + i).astype(BF16)
 
 
-def finish_kernel(own_ref, side_ref, edge_ref, weight_ref, merged_ref, grad_ref, frame):
+def finish_kernel(own_ref, side_ref, edge_ref, weight_ref, merged_ref, grad_ref):
+    both = jnp.concatenate([own_ref[...], edge_ref[...], side_ref[0:BIG, :]], axis=0)
+    final = both[:, :C]
+    grad = both[:, C:]
+    total = 2 * (BIG + THIN)
     above = ROWS - OFF
 
-    def piece(block, rows):
-        return block.astype(F32).reshape(LEVS, rows, SUB, 2 * C)
-
-    frame[:, :above, 0] = piece(own_ref[...], above)
-    frame[:, above:, 0] = piece(edge_ref[0:THIN, :], OFF)
-    frame[:, :above, 1] = piece(side_ref[0:BIG, :], above)
-    frame[:, above:, 1] = piece(edge_ref[THIN:, :], OFF)
-    both = frame[...].reshape(FRAME, 2 * C)
-    final = both[:, :C].astype(BF16)
-    grad = both[:, C:].astype(BF16)
-
-    def source(col):
-        return jnp.where(col >= HALF, col + (SUB - HALF), col)
-
-    to = iota((FRAME, FRAME), 0)
+    def source(lev, row, col):
+        right = col >= HALF
+        below = row >= above
+        thin = (lev * OFF + row - above) * HALF + jnp.where(right, BIG + THIN, BIG)
+        big = (lev * above + row) * HALF + jnp.where(right, BIG + 2 * THIN, 0)
+        return jnp.where(below, thin, big) + col - jnp.where(right, HALF, 0)
+
+    count = LEVS * ROWS * 16
+    to = iota((count, total), 0)
+    lev = jnp.where(to >= count // 2, 1, 0)
     col = jnp.bitwise_and(to, 15)
-    pick = (iota((FRAME, FRAME), 1) == to - col + source(col)) & (col < COLS)
-    moved = product(pick.astype(F32).astype(BF16), grad).reshape(LEVS, ROWS, 16, C)
+    pick = (iota((count, total), 1) == source(lev, (to >> 4) - lev * ROWS, col)) & (col < COLS)
+    moved = product(one_hot(pick), grad).reshape(LEVS, ROWS, 16, C)
     grad_ref[...] = moved[:, :, :COLS, :].astype(BF16)
 
     count = LEVS * (ROWS // 2) * SUB
-    to = iota((count, FRAME), 0)
+    to = iota((count, total), 0)
     lev = jnp.where(to >= count // 2, 1, 0)
     pair = (to >> 3) - lev * (ROWS // 2)
     parts = []
     for down in range(2):
         for right in range(2):
             col = 2 * jnp.bitwise_and(to, SUB - 1) + right
-            wanted = lev * (FRAME // 2) + (2 * pair + down) * 16 + source(col)
-            pick = (iota((count, FRAME), 1) == wanted) & (col < COLS)
-            parts.append(product(pick.astype(F32).astype(BF16), final))
+            pick = (iota((count, total), 1) == source(lev, 2 * pair + down, col)) & (col < COLS)
+            parts.append(product(one_hot(pick), final))
     width = 4 * C
     mean = sum(jnp.sum(part, axis=-1, keepdims=True) for part in parts) / width
     centers = [part - mean for part in parts]
@@ -467,10 +471,12 @@
         (tokens.transpose(1, 2, 0, 3), cotangent.transpose(1, 2, 0, 3)),
     )
     side, low, corner = shifted(side, 0, 1), shifted(low, 1, 0), shifted(corner, 1, 1)
-    (bias,) = call(
+    bias, quant = call(
         bias_kernel,
-        [((4, STACK, 128), BF16)],
+        [((4, HEADS, BLOCK, 128), F32), ((8, 128), F32)],
         (
+            bit_widths,
+            quant_scales,
             bias_index.reshape(WTOK, WTOK),
             bias_table.transpose(1, 2, 0, 3).reshape(HEADS, 2, POS),
         ),
@@ -479,13 +485,13 @@
             pltpu.VMEM((2, LEVS * BLOCK, 128), F32),
             pltpu.VMEM((LEVS * BLOCK, 16, 128), F32),
         ],
+        scalars=2,
         flops=2_000_000_000,
     )
     weights = call(
         weight_kernel,
         [((3, C, C), BF16), ((C, C), BF16), ((C, FF), BF16), ((C, FF), BF16)],
-        (bit_widths, quant_scales, qkv_codes, proj_codes, up_codes, down_codes.T),
-        scalars=2,
+        (quant, qkv_codes, proj_codes, up_codes, down_codes.T),
         flops=1_000_000_000,
     )
     own, low, side, keep, give = call(
@@ -498,7 +504,6 @@
             ((9 * C, 128), BF16),
         ],
         (own, side, low, corner, *weights, bias),
-        [pltpu.VMEM((LEVS, ROWS, 2, SUB, 2 * C), F32)],
         flops=2_000_000_000,
         mib=32,
     )
@@ -526,7 +531,6 @@
         finish_kernel,
         [((LEVS, ROWS // 2, COLS // 2, 2 * C), BF16), ((LEVS, ROWS, COLS, C), BF16)],
         (own, side, edge, merge_weight),
-        [pltpu.VMEM((LEVS, ROWS, 2, SUB, 2 * C), F32)],
         flops=400_000_000,
     )
     half, merged, grad_tokens = lax.optimization_barrier((half, merged, grad_tokens))

time: 109 us -> 108 us (level)
  no operation moved by 1% of the time
where the time goes in v7:
time: 108 us
  blocking collectives  39.4 us (36%)
  starting transfers between devices  33.4 us (31%)
  waiting for transfers between devices  15 us (14%)
  Pallas kernels  14 us (13%)
  local copies, waits for them, and re-layouts  4.09 us (4%)
    all_to_all x2, blocking collectives, exchange(): return lax.all_to_all(parts, axes, 0, 0)  39.4 us
    pallas_call x9, Pallas kernels, call(): pl.pallas_call(kernel, out_shape=[jax.ShapeDtypeStruct(s, t) for s, t in...  14 us
    ppermute x2, starting transfers between devices, swapped(): return lax.ppermute(block, 'c', [(0, 1), (1, 0)])  10.2 us
    ppermute x2, waiting for transfers between devices, shifted(): lax.ppermute(block, LON, [(c, (c + lon_step) % cols) for c in range(cols)])  7.86 us
    all_to_all x2, starting transfers between devices, exchange(): return lax.all_to_all(parts, axes, 0, 0)  7.42 us
    ppermute x2, waiting for transfers between devices, shifted(): return lax.ppermute(block, LAT, route)  5.73 us
    ppermute x1, starting transfers between devices, shifted(): return lax.ppermute(block, LON + LAT, route)  5.58 us
    ppermute x2, starting transfers between devices, shifted(): return lax.ppermute(block, LAT, route)  5.23 us
  transfers between devices with their start and end apart: 9, of which 3 were waited for; matrix products, arithmetic and copies ran while one was open for 1% of the time, Pallas kernels for 5%

profile of v7, /device:TPU:1, one launch (start us, length us, event | category | flops | bytes accessed | tf_op | source)
XLA Modules:
  0.0 107.6 jit_solution(12174610010963192809)
XLA Ops:
  0.6 0.0 copy-start
  0.6 0.9 copy-done
  1.5 0.9 copy-done.1
  2.5 0.5 shard_map.154
  2.9 4.0 %collective-permute-start.1 = (bf16[48,384]{1,0:T(8,128)(2,1)S(1)}, bf16[48,384]{1,0:T(8,128)(2,1)S(1)}, u32[]{:S(2)}, u32[]{:S(2)}) collective-permute-start(bf16[48,384]{1,0:T(8,128)(2,1)S(1)} %get-tuple-element.36), channel_id=1, source_target_pairs={{0,1},{1,2},{2,3},{3,4},{4,5},{5,6},{6,7},{7,8},{8,9},{9,10},{10,1... | collective-permute-start | bytes 110600 | tf_op jit(solution)/shard_map/ppermute | solution.py:420
  6.9 5.6 %collective-permute-start.2 = (bf16[48,384]{1,0:T(8,128)(2,1)S(1)}, bf16[48,384]{1,0:T(8,128)(2,1)S(1)}, u32[]{:S(2)}, u32[]{:S(2)}) collective-permute-start(bf16[48,384]{1,0:T(8,128)(2,1)S(1)} %get-tuple-element.37), channel_id=1, source_target_pairs={{0,17},{1,18},{2,19},{3,20},{4,21},{5,22},{6,23},{7,24},{8,25},{9,... | collective-permute-start | bytes 110600 | tf_op jit(solution)/shard_map/ppermute | solution.py:417
  12.5 0.0 copy-start.7
  12.5 2.7 %collective-permute-start = (bf16[112,384]{1,0:T(8,128)(2,1)S(1)}, bf16[112,384]{1,0:T(8,128)(2,1)S(1)}, u32[]{:S(2)}, u32[]{:S(2)}) collective-permute-start(bf16[112,384]{1,0:T(8,128)(2,1)S(1)} %get-tuple-element.35), channel_id=1, source_target_pairs={{0,16},{16,32},{32,48},{48,64},{64,80},{80,96},{96,112},{112,128},... | collective-permute-start | bytes 258056 | tf_op jit(solution)/shard_map/ppermute | solution.py:421
  15.1 0.0 copy-done.10
  15.2 0.1 reshape.30.idx_ref
  15.3 0.0 copy-start.8
  15.3 0.0 copy-start.9
  15.3 0.0 copy-done.7
  15.3 0.6 copy-done.8
  15.9 0.0 copy-done.9
  16.0 3.4 %shard_map.155 = (f32[4,6,72,128]{3,2,1,0:T(8,128)S(1)}, f32[8,128]{1,0:T(8,128)S(1)}) custom-call(s32[4]{0:T(128)S(1)} %copy-done.8, s32[4]{0:T(128)S(1)} %copy-done.9, s32[144,144]{1,0:T(8,128)S(1)} %reshape.30.idx_ref, bf16[6,2,3312]{2,1,0:T(2,128)(2,1)S(1)} %bitcast.18), custom_call_target="tpu_custom_call" | custom-call | flops 2000000000 | bytes 1051296 | tf_op jit(solution)/shard_map/pallas_call | solution.py:396
  19.4 0.0 copy-done.2
  19.4 0.0 copy-done.3
  19.4 0.0 copy-done.5
  19.4 0.0 copy-done.6
  19.4 0.5 shard_map.156
  19.9 0.0 collective-permute-done.1.low_ref
  19.9 0.0 collective-permute-done.2.corner_ref
  20.0 0.0 collective-permute-done.side_ref
  20.0 6.5 %shard_map.157 = (bf16[112,384]{1,0:T(8,128)(2,1)S(1)}, bf16[48,384]{1,0:T(8,128)(2,1)S(1)}, bf16[160,384]{1,0:T(8,128)(2,1)S(1)}, bf16[1728,128]{1,0:T(8,128)(2,1)S(1)}, bf16[1728,128]{1,0:T(8,128)(2,1)S(1)}) custom-call(bf16[112,384]{1,0:T(8,128)(2,1)S(1)} %get-tuple-element.34.own_ref, bf16[112,384]{1,0:T(8,128)(2,1)S(1)} %collective-permute-done.side_ref, ...), custom_call_target="tpu_custom_call" | custom-call | flops 2000000000 | bytes 3145728 | tf_op jit(solution)/shard_map/pallas_call | solution.py:396
  26.4 5.7 %collective-permute-start.3 = (bf16[1728,128]{1,0:T(8,128)(2,1)S(1)}, bf16[1728,128]{1,0:T(8,128)(2,1)S(1)}, u32[]{:S(2)}, u32[]{:S(2)}) collective-permute-start(bf16[1728,128]{1,0:T(8,128)(2,1)S(1)} %get-tuple-element.45), channel_id=1, source_target_pairs={{0,16},{16,0},{1,17},{17,1},{2,18},{18,2},{3,19},{19,3},{4,20},{20... | collective-permute-start | bytes 1327112 | tf_op jit(solution)/shard_map/ppermute | solution.py:429
  32.1 1.4 %collective-permute-done.3 = bf16[1728,128]{1,0:T(8,128)(2,1)S(1)} collective-permute-done((bf16[1728,128]{1,0:T(8,128)(2,1)S(1)}, bf16[1728,128]{1,0:T(8,128)(2,1)S(1)}, u32[]{:S(2)}, u32[]{:S(2)}) %collective-permute-start.3) | collective-permute-done | bytes 442400 | tf_op jit(solution)/shard_map/ppermute | solution.py:429
  33.5 0.9 add_convert_fusion
  34.4 3.5 %all-to-all-start = ((bf16[4,432,128]{2,1,0:T(8,128)(2,1)}), bf16[4,432,128]{2,1,0:T(8,128)(2,1)S(1)}, u32[]{:S(2)}, u32[]{:S(2)}) async-start(bf16[4,432,128]{2,1,0:T(8,128)(2,1)} %bitcast.5), calls=%async_computation | async-start | bytes 884736 | tf_op jit(solution)/shard_map/all_to_all | solution.py:425
  37.9 2.3 %collective-permute-start.4 = (bf16[160,384]{1,0:T(8,128)(2,1)S(1)}, bf16[160,384]{1,0:T(8,128)(2,1)S(1)}, u32[]{:S(2)}, u32[]{:S(2)}) collective-permute-start(bf16[160,384]{1,0:T(8,128)(2,1)S(1)} %get-tuple-element.47), channel_id=1, source_target_pairs={{0,496},{16,0},{32,16},{48,32},{64,48},{80,64},{96,80},{112,96},{1... | collective-permute-start | bytes 368648 | tf_op jit(solution)/shard_map/ppermute | solution.py:421
  40.2 7.9 %collective-permute-done.4.side_ref = bf16[160,384]{1,0:T(8,128)(2,1)S(1)} collective-permute-done((bf16[160,384]{1,0:T(8,128)(2,1)S(1)}, bf16[160,384]{1,0:T(8,128)(2,1)S(1)}, u32[]{:S(2)}, u32[]{:S(2)}) %collective-permute-start.4) | collective-permute-done | bytes 122912 | tf_op jit(solution)/shard_map/ppermute | solution.py:421
  48.0 0.0 all-to-all-done.parts_ref
  48.0 0.1 shard_map.158
  48.1 24.0 %all_to_all.20.parts_ref = bf16[64,8,128]{2,1,0:T(8,128)(2,1)S(1)} all-to-all(bf16[64,8,128]{2,1,0:T(8,128)(2,1)S(1)} %bitcast.16), channel_id=1, replica_groups=mesh['z'=8,'xh'=2,'c'=2,'y'=8,'xl'=2] {'y','z'}, dimensions={0} | all-to-all | bytes 262144 | tf_op jit(solution)/shard_map/all_to_all | solution.py:425
  72.1 0.1 shard_map.159
  72.2 15.4 %all_to_all.21 = bf16[64,8,128]{2,1,0:T(8,128)(2,1)S(1)} all-to-all(bf16[64,8,128]{2,1,0:T(8,128)(2,1)S(1)} %shard_map.159), channel_id=1, replica_groups=mesh['z'=8,'xh'=2,'c'=2,'y'=8,'xl'=2] {'y','z'}, dimensions={0} | all-to-all | bytes 262144 | tf_op jit(solution)/shard_map/all_to_all | solution.py:425
  87.5 0.8 shard_map.160
  88.4 4.0 %all-to-all-start.3 = ((bf16[4,432,128]{2,1,0:T(8,128)(2,1)}), bf16[4,432,128]{2,1,0:T(8,128)(2,1)S(1)}, u32[]{:S(2)}, u32[]{:S(2)}) async-start(bf16[4,432,128]{2,1,0:T(8,128)(2,1)} %shard_map.160), calls=%async_computation.3 | async-start | bytes 884736 | tf_op jit(solution)/shard_map/all_to_all | solution.py:425
  92.3 1.3 %collective-permute-start.5 = (bf16[96,384]{1,0:T(8,128)(2,1)S(1)}, bf16[96,384]{1,0:T(8,128)(2,1)S(1)}, u32[]{:S(2)}, u32[]{:S(2)}) collective-permute-start(bf16[96,384]{1,0:T(8,128)(2,1)S(1)} %get-tuple-element.52), channel_id=1, source_target_pairs={{1,0},{2,1},{3,2},{4,3},{5,4},{6,5},{7,6},{8,7},{9,8},{10,9},{11,1... | collective-permute-start | bytes 221192 | tf_op jit(solution)/shard_map/ppermute | solution.py:420
  93.6 5.7 %collective-permute-done.5.edge_ref = bf16[96,384]{1,0:T(8,128)(2,1)S(1)} collective-permute-done((bf16[96,384]{1,0:T(8,128)(2,1)S(1)}, bf16[96,384]{1,0:T(8,128)(2,1)S(1)}, u32[]{:S(2)}, u32[]{:S(2)}) %collective-permute-start.5) | collective-permute-done | bytes 73760 | tf_op jit(solution)/shard_map/ppermute | solution.py:420
  99.4 0.0 copy-done.4
  99.4 1.1 %shard_map.161 = (bf16[2,6,6,384]{3,2,1,0:T(8,128)(2,1)S(1)}, bf16[2,12,12,192]{3,2,1,0:T(8,128)(2,1)S(1)}) custom-call(bf16[112,384]{1,0:T(8,128)(2,1)S(1)} %get-tuple-element.51.own_ref, bf16[160,384]{1,0:T(8,128)(2,1)S(1)} %collective-permute-done.4.side_ref, bf16[96,384]{1,0:T(8,128)(2,1)S(1)} %collective-permute-done.5.edge_ref, ...), custom_call_target="tpu_custom_call" | custom-call | flops 400000000 | bytes 1038336 | tf_op jit(solution)/shard_map/pallas_call | solution.py:396
  100.5 0.0 all-to-all-done.3
  100.5 4.6 %collective-permute-start.6 = (bf16[1728,128]{1,0:T(8,128)(2,1)S(1)}, bf16[1728,128]{1,0:T(8,128)(2,1)S(1)}, u32[]{:S(2)}, u32[]{:S(2)}) collective-permute-start(bf16[1728,128]{1,0:T(8,128)(2,1)S(1)} %bitcast.11), channel_id=1, source_target_pairs={{0,16},{16,0},{1,17},{17,1},{2,18},{18,2},{3,19},{19,3},{4,20},{20... | collective-permute-start | bytes 1327112 | tf_op jit(solution)/shard_map/ppermute | solution.py:429
  105.0 0.7 copy.17
  105.7 0.8 copy.18
  106.5 0.0 collective-permute-done.6.other_ref
  106.5 1.1 shard_map.162
  (7 shorter events, 0.0 us)
Async XLA Ops:
  0.6 0.9 copy-start
  1.5 0.9 copy-start.1
  2.5 12.7 %copy-start.10 = (s32[20736]{0:T(1024)S(1)}, s32[20736]{0:T(1024)}, u32[]{:S(2)}) copy-start(s32[20736]{0:T(1024)} %param.20) | copy-start | bytes 248836
  2.9 17.0 %collective-permute-start.1 = (bf16[48,384]{1,0:T(8,128)(2,1)S(1)}, bf16[48,384]{1,0:T(8,128)(2,1)S(1)}, u32[]{:S(2)}, u32[]{:S(2)}) collective-permute-start(bf16[48,384]{1,0:T(8,128)(2,1)S(1)} %get-tuple-element.36), channel_id=1, source_target_pairs={{0,1},{1,2},{2,3},{3,4},{4,5},{5,6},{6,7},{7,8},{8,9},{9,10},{10,1... | collective-permute-start | bytes 110600 | tf_op jit(solution)/shard_map/ppermute | solution.py:420
  6.9 13.1 %collective-permute-start.2 = (bf16[48,384]{1,0:T(8,128)(2,1)S(1)}, bf16[48,384]{1,0:T(8,128)(2,1)S(1)}, u32[]{:S(2)}, u32[]{:S(2)}) collective-permute-start(bf16[48,384]{1,0:T(8,128)(2,1)S(1)} %get-tuple-element.37), channel_id=1, source_target_pairs={{0,17},{1,18},{2,19},{3,20},{4,21},{5,22},{6,23},{7,24},{8,25},{9,... | collective-permute-start | bytes 110600 | tf_op jit(solution)/shard_map/ppermute | solution.py:417
  12.5 2.8 %copy-start.7 = (bf16[2,1,6,3312]{3,0,2,1:T(2,128)(2,1)S(1)}, bf16[2,1,6,3312]{3,0,2,1:T(2,128)(2,1)}, u32[]{:S(2)}) copy-start(bf16[2,1,6,3312]{3,0,2,1:T(2,128)(2,1)} %param.19) | copy-start | bytes 238468
  12.5 7.5 %collective-permute-start = (bf16[112,384]{1,0:T(8,128)(2,1)S(1)}, bf16[112,384]{1,0:T(8,128)(2,1)S(1)}, u32[]{:S(2)}, u32[]{:S(2)}) collective-permute-start(bf16[112,384]{1,0:T(8,128)(2,1)S(1)} %get-tuple-element.35), channel_id=1, source_target_pairs={{0,16},{16,32},{32,48},{48,64},{64,80},{80,96},{96,112},{112,128},... | collective-permute-start | bytes 258056 | tf_op jit(solution)/shard_map/ppermute | solution.py:421
  15.3 0.7 copy-start.8
  15.3 0.7 copy-start.9
  16.0 3.4 %copy-start.2 = (s32[192,768]{1,0:T(8,128)S(1)}, s32[192,768]{1,0:T(8,128)}, u32[]{:S(2)}) copy-start(s32[192,768]{1,0:T(8,128)} %cu_ref.1) | copy-start | bytes 1769476
  16.0 3.4 %copy-start.3 = (s32[768,192]{0,1:T(8,128)S(1)}, s32[768,192]{0,1:T(8,128)}, u32[]{:S(2)}) copy-start(s32[768,192]{0,1:T(8,128)} %param.16) | copy-start | bytes 1769476
  16.0 3.4 %copy-start.5 = (s32[192,576]{1,0:T(8,128)S(1)}, s32[192,576]{1,0:T(8,128)}, u32[]{:S(2)}) copy-start(s32[192,576]{1,0:T(8,128)} %cq_ref.1) | copy-start | bytes 1327108
  16.0 3.4 %copy-start.6 = (s32[192,192]{1,0:T(8,128)S(1)}, s32[192,192]{1,0:T(8,128)}, u32[]{:S(2)}) copy-start(s32[192,192]{1,0:T(8,128)} %cp_ref.1) | copy-start | bytes 442372
  26.4 7.1 %collective-permute-start.3 = (bf16[1728,128]{1,0:T(8,128)(2,1)S(1)}, bf16[1728,128]{1,0:T(8,128)(2,1)S(1)}, u32[]{:S(2)}, u32[]{:S(2)}) collective-permute-start(bf16[1728,128]{1,0:T(8,128)(2,1)S(1)} %get-tuple-element.45), channel_id=1, source_target_pairs={{0,16},{16,0},{1,17},{17,1},{2,18},{18,2},{3,19},{19,3},{4,20},{20... | collective-permute-start | bytes 1327112 | tf_op jit(solution)/shard_map/ppermute | solution.py:429
  34.4 13.6 %all-to-all-start = ((bf16[4,432,128]{2,1,0:T(8,128)(2,1)}), bf16[4,432,128]{2,1,0:T(8,128)(2,1)S(1)}, u32[]{:S(2)}, u32[]{:S(2)}) async-start(bf16[4,432,128]{2,1,0:T(8,128)(2,1)} %bitcast.5), calls=%async_computation | async-start | bytes 884736 | tf_op jit(solution)/shard_map/all_to_all | solution.py:425
  37.9 10.1 %collective-permute-start.4 = (bf16[160,384]{1,0:T(8,128)(2,1)S(1)}, bf16[160,384]{1,0:T(8,128)(2,1)S(1)}, u32[]{:S(2)}, u32[]{:S(2)}) collective-permute-start(bf16[160,384]{1,0:T(8,128)(2,1)S(1)} %get-tuple-element.47), channel_id=1, source_target_pairs={{0,496},{16,0},{32,16},{48,32},{64,48},{80,64},{96,80},{112,96},{1... | collective-permute-start | bytes 368648 | tf_op jit(solution)/shard_map/ppermute | solution.py:421
  87.5 11.8 %copy-start.4 = (bf16[768,384]{1,0:T(8,128)(2,1)S(1)}, bf16[768,384]{1,0:T(8,128)(2,1)}, u32[]{:S(2)}) copy-start(bf16[768,384]{1,0:T(8,128)(2,1)} %weight_ref.1) | copy-start | bytes 1769476
  88.4 12.1 %all-to-all-start.3 = ((bf16[4,432,128]{2,1,0:T(8,128)(2,1)}), bf16[4,432,128]{2,1,0:T(8,128)(2,1)S(1)}, u32[]{:S(2)}, u32[]{:S(2)}) async-start(bf16[4,432,128]{2,1,0:T(8,128)(2,1)} %shard_map.160), calls=%async_computation.3 | async-start | bytes 884736 | tf_op jit(solution)/shard_map/all_to_all | solution.py:425
  92.3 7.0 %collective-permute-start.5 = (bf16[96,384]{1,0:T(8,128)(2,1)S(1)}, bf16[96,384]{1,0:T(8,128)(2,1)S(1)}, u32[]{:S(2)}, u32[]{:S(2)}) collective-permute-start(bf16[96,384]{1,0:T(8,128)(2,1)S(1)} %get-tuple-element.52), channel_id=1, source_target_pairs={{1,0},{2,1},{3,2},{4,3},{5,4},{6,5},{7,6},{8,7},{9,8},{10,9},{11,1... | collective-permute-start | bytes 221192 | tf_op jit(solution)/shard_map/ppermute | solution.py:420
  100.5 6.1 %collective-permute-start.6 = (bf16[1728,128]{1,0:T(8,128)(2,1)S(1)}, bf16[1728,128]{1,0:T(8,128)(2,1)S(1)}, u32[]{:S(2)}, u32[]{:S(2)}) collective-permute-start(bf16[1728,128]{1,0:T(8,128)(2,1)S(1)} %bitcast.11), channel_id=1, source_target_pairs={{0,16},{16,0},{1,17},{17,1},{2,18},{18,2},{3,19},{19,3},{4,20},{20... | collective-permute-start | bytes 1327112 | tf_op jit(solution)/shard_map/ppermute | solution.py:429

commit v8 on v7

--- a/solution.py
+++ b/solution.py
@@ -359,23 +359,23 @@
         big = (lev * above + row) * HALF + jnp.where(right, BIG + 2 * THIN, 0)
         return jnp.where(below, thin, big) + col - jnp.where(right, HALF, 0)
 
-    count = LEVS * ROWS * 16
+    count = ROWS * COLS * LEVS
     to = iota((count, total), 0)
-    lev = jnp.where(to >= count // 2, 1, 0)
-    col = jnp.bitwise_and(to, 15)
-    pick = (iota((count, total), 1) == source(lev, (to >> 4) - lev * ROWS, col)) & (col < COLS)
-    moved = product(one_hot(pick), grad).reshape(LEVS, ROWS, 16, C)
-    grad_ref[...] = moved[:, :, :COLS, :].astype(BF16)
-
-    count = LEVS * (ROWS // 2) * SUB
+    lev = jnp.bitwise_and(to, 1)
+    row = over(to, COLS * LEVS)
+    col = (to >> 1) - row * COLS
+    pick = iota((count, total), 1) == source(lev, row, col)
+    grad_ref[...] = product(one_hot(pick), grad).reshape(ROWS, COLS, LEVS, C).astype(BF16)
+
+    count = (ROWS // 2) * (COLS // 2) * LEVS
     to = iota((count, total), 0)
-    lev = jnp.where(to >= count // 2, 1, 0)
-    pair = (to >> 3) - lev * (ROWS // 2)
+    lev = jnp.bitwise_and(to, 1)
+    pair = over(to, COLS // 2 * LEVS)
+    beside = (to >> 1) - pair * (COLS // 2)
     parts = []
     for down in range(2):
         for right in range(2):
-            col = 2 * jnp.bitwise_and(to, SUB - 1) + right
-            pick = (iota((count, total), 1) == source(lev, 2 * pair + down, col)) & (col < COLS)
+            pick = iota((count, total), 1) == source(lev, 2 * pair + down, 2 * beside + right)
             parts.append(product(one_hot(pick), final))
     width = 4 * C
     mean = sum(jnp.sum(part, axis=-1, keepdims=True) for part in parts) / width
@@ -385,7 +385,7 @@
     total = jnp.zeros((count, 2 * C), F32)
     for i, part in enumerate(centers):
         total = total + product((part * scale).astype(BF16), weight_ref[i * C : (i + 1) * C, :])
-    merged_ref[...] = total.reshape(LEVS, ROWS // 2, SUB, 2 * C)[:, :, :HALF, :].astype(BF16)
+    merged_ref[...] = total.reshape(ROWS // 2, COLS // 2, LEVS, 2 * C).astype(BF16)
 
 
 def call(kernel, outs, args, scratch=(), scalars=0, flops=0, mib=16):
@@ -527,13 +527,14 @@
     edge = shifted(edge, -1, 0)
     (spread,) = call(copies_kernel, [((near, rows, 128), BF16)], (part,))
     half = exchange(spread, NEAR)
+    half, edge = lax.optimization_barrier((half, edge))
     merged, grad_tokens = call(
         finish_kernel,
-        [((LEVS, ROWS // 2, COLS // 2, 2 * C), BF16), ((LEVS, ROWS, COLS, C), BF16)],
+        [((ROWS // 2, COLS // 2, LEVS, 2 * C), BF16), ((ROWS, COLS, LEVS, C), BF16)],
         (own, side, edge, merge_weight),
         flops=400_000_000,
     )
-    half, merged, grad_tokens = lax.optimization_barrier((half, merged, grad_tokens))
+    merged, grad_tokens = merged.transpose(2, 0, 1, 3), grad_tokens.transpose(2, 0, 1, 3)
     half = half.reshape(near * rows, 128)
     qkv, proj, up, down = call(
         spread_kernel,

time: 108 us -> 108 us (level)
  local copies, waits for them, and re-layouts: 4.09 us -> 2.61 us
    unnamed x24 -> x22, local copies, waits for them, and re-layouts: 3.97 us -> 2.49 us
  transfers between devices with their start and end apart: 9 -> 9, of which waited for: 3 -> 3; matrix products, arithmetic and copies ran while one was open for 1% -> 0% of each run, Pallas kernels for 5% -> 5%
where the time goes in v8:
time: 108 us; the launch traced here: 107 us
  blocking collectives  39.4 us (36%)
  starting transfers between devices  34.1 us (32%)
  waiting for transfers between devices  15 us (14%)
  Pallas kernels  14.6 us (14%)
  local copies, waits for them, and re-layouts  2.61 us (2%)
    all_to_all x2, blocking collectives, exchange(): return lax.all_to_all(parts, axes, 0, 0)  39.4 us
    pallas_call x9, Pallas kernels, call(): pl.pallas_call(kernel, out_shape=[jax.ShapeDtypeStruct(s, t) for s, t in...  14.6 us
    ppermute x2, starting transfers between devices, swapped(): return lax.ppermute(block, 'c', [(0, 1), (1, 0)])  10.9 us
    ppermute x2, waiting for transfers between devices, shifted(): lax.ppermute(block, LON, [(c, (c + lon_step) % cols) for c in range(cols)])  7.86 us
    all_to_all x2, starting transfers between devices, exchange(): return lax.all_to_all(parts, axes, 0, 0)  7.42 us
    ppermute x2, waiting for transfers between devices, shifted(): return lax.ppermute(block, LAT, route)  5.73 us
    ppermute x1, starting transfers between devices, shifted(): return lax.ppermute(block, LON + LAT, route)  5.58 us
    ppermute x2, starting transfers between devices, shifted(): return lax.ppermute(block, LAT, route)  5.23 us
  transfers between devices with their start and end apart: 9, of which 3 were waited for; matrix products, arithmetic and copies ran while one was open for 0% of the time, Pallas kernels for 5%

profile of v8, /device:TPU:1, one launch (start us, length us, event | category | flops | bytes accessed | tf_op | source)
XLA Modules:
  0.0 107.4 jit_solution(12011652526266351390)
XLA Ops:
  0.6 0.0 copy-start
  0.6 0.9 copy-done
  1.5 0.0 copy-start.1
  1.5 0.9 copy-done.1
  2.5 0.0 copy-start.10
  2.5 0.5 shard_map.154
  2.9 4.0 %collective-permute-start.1 = (bf16[48,384]{1,0:T(8,128)(2,1)S(1)}, bf16[48,384]{1,0:T(8,128)(2,1)S(1)}, u32[]{:S(2)}, u32[]{:S(2)}) collective-permute-start(bf16[48,384]{1,0:T(8,128)(2,1)S(1)} %get-tuple-element.35), channel_id=1, source_target_pairs={{0,1},{1,2},{2,3},{3,4},{4,5},{5,6},{6,7},{7,8},{8,9},{9,10},{10,1... | collective-permute-start | bytes 110600 | tf_op jit(solution)/shard_map/ppermute | solution.py:420
  6.9 5.6 %collective-permute-start.2 = (bf16[48,384]{1,0:T(8,128)(2,1)S(1)}, bf16[48,384]{1,0:T(8,128)(2,1)S(1)}, u32[]{:S(2)}, u32[]{:S(2)}) collective-permute-start(bf16[48,384]{1,0:T(8,128)(2,1)S(1)} %get-tuple-element.36), channel_id=1, source_target_pairs={{0,17},{1,18},{2,19},{3,20},{4,21},{5,22},{6,23},{7,24},{8,25},{9,... | collective-permute-start | bytes 110600 | tf_op jit(solution)/shard_map/ppermute | solution.py:417
  12.5 0.0 copy-start.7
  12.5 2.7 %collective-permute-start = (bf16[112,384]{1,0:T(8,128)(2,1)S(1)}, bf16[112,384]{1,0:T(8,128)(2,1)S(1)}, u32[]{:S(2)}, u32[]{:S(2)}) collective-permute-start(bf16[112,384]{1,0:T(8,128)(2,1)S(1)} %get-tuple-element.34), channel_id=1, source_target_pairs={{0,16},{16,32},{32,48},{48,64},{64,80},{80,96},{96,112},{112,128},... | collective-permute-start | bytes 258056 | tf_op jit(solution)/shard_map/ppermute | solution.py:421
  15.1 0.0 copy-done.10
  15.2 0.1 reshape.30.idx_ref
  15.3 0.0 copy-start.8
  15.3 0.0 copy-start.9
  15.3 0.0 copy-done.7
  15.3 0.6 copy-done.8
  15.9 0.0 copy-done.9
  16.0 3.4 %shard_map.155 = (f32[4,6,72,128]{3,2,1,0:T(8,128)S(1)}, f32[8,128]{1,0:T(8,128)S(1)}) custom-call(s32[4]{0:T(128)S(1)} %copy-done.8, s32[4]{0:T(128)S(1)} %copy-done.9, s32[144,144]{1,0:T(8,128)S(1)} %reshape.30.idx_ref, bf16[6,2,3312]{2,1,0:T(2,128)(2,1)S(1)} %bitcast.20), custom_call_target="tpu_custom_call" | custom-call | flops 2000000000 | bytes 1051296 | tf_op jit(solution)/shard_map/pallas_call | solution.py:396
  19.4 0.0 copy-done.2
  19.4 0.0 copy-done.3
  19.4 0.0 copy-done.5
  19.4 0.0 copy-done.6
  19.4 0.5 shard_map.156
  19.9 0.0 collective-permute-done.1.low_ref
  19.9 0.0 collective-permute-done.2.corner_ref
  20.0 0.0 collective-permute-done.side_ref
  20.0 6.5 %shard_map.157 = (bf16[112,384]{1,0:T(8,128)(2,1)S(1)}, bf16[48,384]{1,0:T(8,128)(2,1)S(1)}, bf16[160,384]{1,0:T(8,128)(2,1)S(1)}, bf16[1728,128]{1,0:T(8,128)(2,1)S(1)}, bf16[1728,128]{1,0:T(8,128)(2,1)S(1)}) custom-call(bf16[112,384]{1,0:T(8,128)(2,1)S(1)} %get-tuple-element.33.own_ref, bf16[112,384]{1,0:T(8,128)(2,1)S(1)} %collective-permute-done.side_ref, ...), custom_call_target="tpu_custom_call" | custom-call | flops 2000000000 | bytes 3145728 | tf_op jit(solution)/shard_map/pallas_call | solution.py:396
  26.4 5.7 %collective-permute-start.4 = (bf16[1728,128]{1,0:T(8,128)(2,1)S(1)}, bf16[1728,128]{1,0:T(8,128)(2,1)S(1)}, u32[]{:S(2)}, u32[]{:S(2)}) collective-permute-start(bf16[1728,128]{1,0:T(8,128)(2,1)S(1)} %get-tuple-element.46), channel_id=1, source_target_pairs={{0,16},{16,0},{1,17},{17,1},{2,18},{18,2},{3,19},{19,3},{4,20},{20... | collective-permute-start | bytes 1327112 | tf_op jit(solution)/shard_map/ppermute | solution.py:429
  32.1 1.4 %collective-permute-done.4 = bf16[1728,128]{1,0:T(8,128)(2,1)S(1)} collective-permute-done((bf16[1728,128]{1,0:T(8,128)(2,1)S(1)}, bf16[1728,128]{1,0:T(8,128)(2,1)S(1)}, u32[]{:S(2)}, u32[]{:S(2)}) %collective-permute-start.4) | collective-permute-done | bytes 442400 | tf_op jit(solution)/shard_map/ppermute | solution.py:429
  33.5 0.9 add_convert_fusion
  34.4 3.5 %all-to-all-start = ((bf16[4,432,128]{2,1,0:T(8,128)(2,1)}), bf16[4,432,128]{2,1,0:T(8,128)(2,1)S(1)}, u32[]{:S(2)}, u32[]{:S(2)}) async-start(bf16[4,432,128]{2,1,0:T(8,128)(2,1)} %bitcast.5), calls=%async_computation | async-start | bytes 884736 | tf_op jit(solution)/shard_map/all_to_all | solution.py:425
  37.9 2.3 %collective-permute-start.3 = (bf16[160,384]{1,0:T(8,128)(2,1)S(1)}, bf16[160,384]{1,0:T(8,128)(2,1)S(1)}, u32[]{:S(2)}, u32[]{:S(2)}) collective-permute-start(bf16[160,384]{1,0:T(8,128)(2,1)S(1)} %get-tuple-element.44), channel_id=1, source_target_pairs={{0,496},{16,0},{32,16},{48,32},{64,48},{80,64},{96,80},{112,96},{1... | collective-permute-start | bytes 368648 | tf_op jit(solution)/shard_map/ppermute | solution.py:421
  40.2 7.9 %collective-permute-done.3.side_ref = bf16[160,384]{1,0:T(8,128)(2,1)S(1)} collective-permute-done((bf16[160,384]{1,0:T(8,128)(2,1)S(1)}, bf16[160,384]{1,0:T(8,128)(2,1)S(1)}, u32[]{:S(2)}, u32[]{:S(2)}) %collective-permute-start.3) | collective-permute-done | bytes 122912 | tf_op jit(solution)/shard_map/ppermute | solution.py:421
  48.0 0.0 all-to-all-done.parts_ref
  48.0 0.1 shard_map.158
  48.1 24.0 %all_to_all.20.parts_ref = bf16[64,8,128]{2,1,0:T(8,128)(2,1)S(1)} all-to-all(bf16[64,8,128]{2,1,0:T(8,128)(2,1)S(1)} %bitcast.18), channel_id=1, replica_groups=mesh['z'=8,'xh'=2,'c'=2,'y'=8,'xl'=2] {'y','z'}, dimensions={0} | all-to-all | bytes 262144 | tf_op jit(solution)/shard_map/all_to_all | solution.py:425
  72.1 0.1 shard_map.159
  72.2 15.4 %all_to_all.21 = bf16[64,8,128]{2,1,0:T(8,128)(2,1)S(1)} all-to-all(bf16[64,8,128]{2,1,0:T(8,128)(2,1)S(1)} %shard_map.159), channel_id=1, replica_groups=mesh['z'=8,'xh'=2,'c'=2,'y'=8,'xl'=2] {'y','z'}, dimensions={0} | all-to-all | bytes 262144 | tf_op jit(solution)/shard_map/all_to_all | solution.py:425
  87.5 0.8 shard_map.160
  88.4 4.0 %all-to-all-start.3 = ((bf16[4,432,128]{2,1,0:T(8,128)(2,1)}), bf16[4,432,128]{2,1,0:T(8,128)(2,1)S(1)}, u32[]{:S(2)}, u32[]{:S(2)}) async-start(bf16[4,432,128]{2,1,0:T(8,128)(2,1)} %shard_map.160), calls=%async_computation.3 | async-start | bytes 884736 | tf_op jit(solution)/shard_map/all_to_all | solution.py:425
  92.3 1.3 %collective-permute-start.5 = (bf16[96,384]{1,0:T(8,128)(2,1)S(1)}, bf16[96,384]{1,0:T(8,128)(2,1)S(1)}, u32[]{:S(2)}, u32[]{:S(2)}) collective-permute-start(bf16[96,384]{1,0:T(8,128)(2,1)S(1)} %get-tuple-element.51), channel_id=1, source_target_pairs={{1,0},{2,1},{3,2},{4,3},{5,4},{6,5},{7,6},{8,7},{9,8},{10,9},{11,1... | collective-permute-start | bytes 221192 | tf_op jit(solution)/shard_map/ppermute | solution.py:420
  93.6 5.7 %collective-permute-done.5.edge_ref = bf16[96,384]{1,0:T(8,128)(2,1)S(1)} collective-permute-done((bf16[96,384]{1,0:T(8,128)(2,1)S(1)}, bf16[96,384]{1,0:T(8,128)(2,1)S(1)}, u32[]{:S(2)}, u32[]{:S(2)}) %collective-permute-start.5) | collective-permute-done | bytes 73760 | tf_op jit(solution)/shard_map/ppermute | solution.py:420
  99.4 0.0 all-to-all-done.3
  99.4 5.2 %collective-permute-start.6 = (bf16[1728,128]{1,0:T(8,128)(2,1)S(1)}, bf16[1728,128]{1,0:T(8,128)(2,1)S(1)}, u32[]{:S(2)}, u32[]{:S(2)}) collective-permute-start(bf16[1728,128]{1,0:T(8,128)(2,1)S(1)} %bitcast.13), channel_id=1, source_target_pairs={{0,16},{16,0},{1,17},{17,1},{2,18},{18,2},{3,19},{19,3},{4,20},{20... | collective-permute-start | bytes 1327112 | tf_op jit(solution)/shard_map/ppermute | solution.py:429
  104.6 0.0 copy-done.4
  104.6 1.7 %shard_map.161 = (bf16[6,6,2,384]{3,2,1,0:T(2,128)(2,1)}, bf16[12,12,2,192]{3,2,1,0:T(2,128)(2,1)}) custom-call(bf16[112,384]{1,0:T(8,128)(2,1)S(1)} %get-tuple-element.43.own_ref, bf16[160,384]{1,0:T(8,128)(2,1)S(1)} %collective-permute-done.3.side_ref, bf16[96,384]{1,0:T(8,128)(2,1)S(1)} %collective-permute-done.5.edge_ref, bf16[768,384]{1,0:T(8,128)(2,1)S(1)} %copy-done.4), custom_call_target="tpu_custom_call" | custom-call | flops 400000000 | bytes 1038336 | tf_op jit(solution)/shard_map/pallas_call | solution.py:396
  106.3 0.0 collective-permute-done.6.other_ref
  106.3 1.1 %shard_map.162 = (bf16[192,576]{1,0:T(8,128)(2,1)}, bf16[192,192]{1,0:T(8,128)(2,1)}, bf16[192,768]{1,0:T(8,128)(2,1)}, bf16[192,768]{1,0:T(8,128)(2,1)}) custom-call(bf16[1728,128]{1,0:T(8,128)(2,1)S(1)} %bitcast.14, bf16[1728,128]{1,0:T(8,128)(2,1)S(1)} %collective-permute-done.6.other_ref), custom_call_target="tpu_custom_call" | custom-call | bytes 1769472 | tf_op jit(solution)/shard_map/pallas_call | solution.py:396
  (5 shorter events, 0.0 us)
Async XLA Ops:
  0.6 0.9 copy-start
  1.5 0.9 copy-start.1
  2.5 12.7 %copy-start.10 = (s32[20736]{0:T(1024)S(1)}, s32[20736]{0:T(1024)}, u32[]{:S(2)}) copy-start(s32[20736]{0:T(1024)} %param.20) | copy-start | bytes 248836
  2.9 17.0 %collective-permute-start.1 = (bf16[48,384]{1,0:T(8,128)(2,1)S(1)}, bf16[48,384]{1,0:T(8,128)(2,1)S(1)}, u32[]{:S(2)}, u32[]{:S(2)}) collective-permute-start(bf16[48,384]{1,0:T(8,128)(2,1)S(1)} %get-tuple-element.35), channel_id=1, source_target_pairs={{0,1},{1,2},{2,3},{3,4},{4,5},{5,6},{6,7},{7,8},{8,9},{9,10},{10,1... | collective-permute-start | bytes 110600 | tf_op jit(solution)/shard_map/ppermute | solution.py:420
  6.9 13.1 %collective-permute-start.2 = (bf16[48,384]{1,0:T(8,128)(2,1)S(1)}, bf16[48,384]{1,0:T(8,128)(2,1)S(1)}, u32[]{:S(2)}, u32[]{:S(2)}) collective-permute-start(bf16[48,384]{1,0:T(8,128)(2,1)S(1)} %get-tuple-element.36), channel_id=1, source_target_pairs={{0,17},{1,18},{2,19},{3,20},{4,21},{5,22},{6,23},{7,24},{8,25},{9,... | collective-permute-start | bytes 110600 | tf_op jit(solution)/shard_map/ppermute | solution.py:417
  12.5 2.8 %copy-start.7 = (bf16[2,1,6,3312]{3,0,2,1:T(2,128)(2,1)S(1)}, bf16[2,1,6,3312]{3,0,2,1:T(2,128)(2,1)}, u32[]{:S(2)}) copy-start(bf16[2,1,6,3312]{3,0,2,1:T(2,128)(2,1)} %param.19) | copy-start | bytes 238468
  12.5 7.5 %collective-permute-start = (bf16[112,384]{1,0:T(8,128)(2,1)S(1)}, bf16[112,384]{1,0:T(8,128)(2,1)S(1)}, u32[]{:S(2)}, u32[]{:S(2)}) collective-permute-start(bf16[112,384]{1,0:T(8,128)(2,1)S(1)} %get-tuple-element.34), channel_id=1, source_target_pairs={{0,16},{16,32},{32,48},{48,64},{64,80},{80,96},{96,112},{112,128},... | collective-permute-start | bytes 258056 | tf_op jit(solution)/shard_map/ppermute | solution.py:421
  15.3 0.7 copy-start.8
  15.3 0.7 copy-start.9
  16.0 3.4 %copy-start.2 = (s32[192,768]{1,0:T(8,128)S(1)}, s32[192,768]{1,0:T(8,128)}, u32[]{:S(2)}) copy-start(s32[192,768]{1,0:T(8,128)} %cu_ref.1) | copy-start | bytes 1769476
  16.0 3.4 %copy-start.3 = (s32[768,192]{0,1:T(8,128)S(1)}, s32[768,192]{0,1:T(8,128)}, u32[]{:S(2)}) copy-start(s32[768,192]{0,1:T(8,128)} %param.16) | copy-start | bytes 1769476
  16.0 3.4 %copy-start.5 = (s32[192,576]{1,0:T(8,128)S(1)}, s32[192,576]{1,0:T(8,128)}, u32[]{:S(2)}) copy-start(s32[192,576]{1,0:T(8,128)} %cq_ref.1) | copy-start | bytes 1327108
  16.0 3.4 %copy-start.6 = (s32[192,192]{1,0:T(8,128)S(1)}, s32[192,192]{1,0:T(8,128)}, u32[]{:S(2)}) copy-start(s32[192,192]{1,0:T(8,128)} %cp_ref.1) | copy-start | bytes 442372
  26.4 7.1 %collective-permute-start.4 = (bf16[1728,128]{1,0:T(8,128)(2,1)S(1)}, bf16[1728,128]{1,0:T(8,128)(2,1)S(1)}, u32[]{:S(2)}, u32[]{:S(2)}) collective-permute-start(bf16[1728,128]{1,0:T(8,128)(2,1)S(1)} %get-tuple-element.46), channel_id=1, source_target_pairs={{0,16},{16,0},{1,17},{17,1},{2,18},{18,2},{3,19},{19,3},{4,20},{20... | collective-permute-start | bytes 1327112 | tf_op jit(solution)/shard_map/ppermute | solution.py:429
  34.4 13.6 %all-to-all-start = ((bf16[4,432,128]{2,1,0:T(8,128)(2,1)}), bf16[4,432,128]{2,1,0:T(8,128)(2,1)S(1)}, u32[]{:S(2)}, u32[]{:S(2)}) async-start(bf16[4,432,128]{2,1,0:T(8,128)(2,1)} %bitcast.5), calls=%async_computation | async-start | bytes 884736 | tf_op jit(solution)/shard_map/all_to_all | solution.py:425
  37.9 10.1 %collective-permute-start.3 = (bf16[160,384]{1,0:T(8,128)(2,1)S(1)}, bf16[160,384]{1,0:T(8,128)(2,1)S(1)}, u32[]{:S(2)}, u32[]{:S(2)}) collective-permute-start(bf16[160,384]{1,0:T(8,128)(2,1)S(1)} %get-tuple-element.44), channel_id=1, source_target_pairs={{0,496},{16,0},{32,16},{48,32},{64,48},{80,64},{96,80},{112,96},{1... | collective-permute-start | bytes 368648 | tf_op jit(solution)/shard_map/ppermute | solution.py:421
  87.5 17.1 %copy-start.4 = (bf16[768,384]{1,0:T(8,128)(2,1)S(1)}, bf16[768,384]{1,0:T(8,128)(2,1)}, u32[]{:S(2)}) copy-start(bf16[768,384]{1,0:T(8,128)(2,1)} %weight_ref.1) | copy-start | bytes 1769476
  88.4 11.0 %all-to-all-start.3 = ((bf16[4,432,128]{2,1,0:T(8,128)(2,1)}), bf16[4,432,128]{2,1,0:T(8,128)(2,1)S(1)}, u32[]{:S(2)}, u32[]{:S(2)}) async-start(bf16[4,432,128]{2,1,0:T(8,128)(2,1)} %shard_map.160), calls=%async_computation.3 | async-start | bytes 884736 | tf_op jit(solution)/shard_map/all_to_all | solution.py:425
  92.3 7.0 %collective-permute-start.5 = (bf16[96,384]{1,0:T(8,128)(2,1)S(1)}, bf16[96,384]{1,0:T(8,128)(2,1)S(1)}, u32[]{:S(2)}, u32[]{:S(2)}) collective-permute-start(bf16[96,384]{1,0:T(8,128)(2,1)S(1)} %get-tuple-element.51), channel_id=1, source_target_pairs={{1,0},{2,1},{3,2},{4,3},{5,4},{6,5},{7,6},{8,7},{9,8},{10,9},{11,1... | collective-permute-start | bytes 221192 | tf_op jit(solution)/shard_map/ppermute | solution.py:420
  99.4 6.9 %collective-permute-start.6 = (bf16[1728,128]{1,0:T(8,128)(2,1)S(1)}, bf16[1728,128]{1,0:T(8,128)(2,1)S(1)}, u32[]{:S(2)}, u32[]{:S(2)}) collective-permute-start(bf16[1728,128]{1,0:T(8,128)(2,1)S(1)} %bitcast.13), channel_id=1, source_target_pairs={{0,16},{16,0},{1,17},{17,1},{2,18},{18,2},{3,19},{19,3},{4,20},{20... | collective-permute-start | bytes 1327112 | tf_op jit(solution)/shard_map/ppermute | solution.py:429

commit v9 on v8

--- a/solution.py
+++ b/solution.py
@@ -241,7 +241,7 @@
         scores = across(q_stack, key[at].astype(BF16)) * HEAD_DIM ** (-0.5)
         scores = scores + bias_ref[block].reshape(STACK, 128)[:, :BLOCK]
         weights = jnp.exp(scores - jnp.max(scores, axis=-1, keepdims=True))
-        weights = weights / jnp.sum(weights, axis=-1, keepdims=True)
+        weights = weights * (1.0 / jnp.sum(weights, axis=-1, keepdims=True))
         weights_low = weights.astype(BF16)
         heads_parts.append(join_heads(product(weights_low, value[at].astype(BF16))))
         saved.append((q_stack, weights, weights_low))
@@ -446,6 +446,13 @@
     out_ref[...] = jnp.broadcast_to(total[None], out_ref.shape)
 
 
+def add_kernel(one_ref, two_ref, out_ref):
+    count, rows, _ = out_ref.shape
+    for i in range(count):
+        at = slice(i * rows, (i + 1) * rows)
+        out_ref[i] = (one_ref[at, :].astype(F32) + two_ref[at, :].astype(F32)).astype(BF16)
+
+
 def copies_kernel(part_ref, out_ref):
     count, rows, _ = out_ref.shape
     for i in range(count):
@@ -512,8 +519,8 @@
     far = lax.axis_size(FAR)
     rows = 9 * C // near
     padded = -(-rows // (8 * far)) * (8 * far)
-    part = (keep.astype(F32) + swapped(give).astype(F32)).astype(BF16)
-    part = exchange(part.reshape(near, rows, 128), NEAR)
+    (part,) = call(add_kernel, [((near, rows, 128), BF16)], (keep, swapped(give)))
+    part = exchange(part, NEAR)
     side = shifted(side, 0, -1)
     part, edge = call(
         sum_kernel,

time: 108 us -> 108 us (level)
    pallas_call x9 -> x10, Pallas kernels: 14.6 us -> 15.5 us  [call(): pl.pallas_call(kernel, out_shape=[jax.ShapeDtypeStruct(s, t) for s, t in...]
where the time goes in v9:
time: 108 us; the launch traced here: 107 us
  blocking collectives  39.4 us (36%)
  starting transfers between devices  34.1 us (32%)
  Pallas kernels  15.5 us (14%)
  waiting for transfers between devices  15 us (14%)
  local copies, waits for them, and re-layouts  2.61 us (2%)
    all_to_all x2, blocking collectives, exchange(): return lax.all_to_all(parts, axes, 0, 0)  39.4 us
    pallas_call x10, Pallas kernels, call(): pl.pallas_call(kernel, out_shape=[jax.ShapeDtypeStruct(s, t) for s, t in...  15.5 us
    ppermute x2, starting transfers between devices, swapped(): return lax.ppermute(block, 'c', [(0, 1), (1, 0)])  10.9 us
    ppermute x2, waiting for transfers between devices, shifted(): lax.ppermute(block, LON, [(c, (c + lon_step) % cols) for c in range(cols)])  7.86 us
    all_to_all x2, starting transfers between devices, exchange(): return lax.all_to_all(parts, axes, 0, 0)  7.42 us
    ppermute x2, waiting for transfers between devices, shifted(): return lax.ppermute(block, LAT, route)  5.73 us
    ppermute x1, starting transfers between devices, shifted(): return lax.ppermute(block, LON + LAT, route)  5.58 us
    ppermute x2, starting transfers between devices, shifted(): return lax.ppermute(block, LAT, route)  5.23 us
  transfers between devices with their start and end apart: 9, of which 3 were waited for; matrix products, arithmetic and copies ran while one was open for 0% of the time, Pallas kernels for 5%

profile of v9, /device:TPU:1, one launch (start us, length us, event | category | flops | bytes accessed | tf_op | source)
XLA Modules:
  0.0 107.4 jit_solution(4957782570778873545)
XLA Ops:
  0.6 0.0 copy-start
  0.6 0.9 copy-done
  1.5 0.0 copy-start.1
  1.5 0.9 copy-done.1
  2.5 0.0 copy-start.10
  2.5 0.5 shard_map.154
  2.9 4.0 %collective-permute-start.1 = (bf16[48,384]{1,0:T(8,128)(2,1)S(1)}, bf16[48,384]{1,0:T(8,128)(2,1)S(1)}, u32[]{:S(2)}, u32[]{:S(2)}) collective-permute-start(bf16[48,384]{1,0:T(8,128)(2,1)S(1)} %get-tuple-element.35), channel_id=1, source_target_pairs={{0,1},{1,2},{2,3},{3,4},{4,5},{5,6},{6,7},{7,8},{8,9},{9,10},{10,1... | collective-permute-start | bytes 110600 | tf_op jit(solution)/shard_map/ppermute | solution.py:420
  6.9 5.6 %collective-permute-start.2 = (bf16[48,384]{1,0:T(8,128)(2,1)S(1)}, bf16[48,384]{1,0:T(8,128)(2,1)S(1)}, u32[]{:S(2)}, u32[]{:S(2)}) collective-permute-start(bf16[48,384]{1,0:T(8,128)(2,1)S(1)} %get-tuple-element.36), channel_id=1, source_target_pairs={{0,17},{1,18},{2,19},{3,20},{4,21},{5,22},{6,23},{7,24},{8,25},{9,... | collective-permute-start | bytes 110600 | tf_op jit(solution)/shard_map/ppermute | solution.py:417
  12.5 0.0 copy-start.7
  12.5 2.7 %collective-permute-start = (bf16[112,384]{1,0:T(8,128)(2,1)S(1)}, bf16[112,384]{1,0:T(8,128)(2,1)S(1)}, u32[]{:S(2)}, u32[]{:S(2)}) collective-permute-start(bf16[112,384]{1,0:T(8,128)(2,1)S(1)} %get-tuple-element.34), channel_id=1, source_target_pairs={{0,16},{16,32},{32,48},{48,64},{64,80},{80,96},{96,112},{112,128},... | collective-permute-start | bytes 258056 | tf_op jit(solution)/shard_map/ppermute | solution.py:421
  15.1 0.0 copy-done.10
  15.2 0.1 reshape.27.idx_ref
  15.3 0.0 copy-start.8
  15.3 0.0 copy-start.9
  15.3 0.0 copy-done.7
  15.3 0.6 copy-done.8
  15.9 0.0 copy-done.9
  16.0 3.4 %shard_map.155 = (f32[4,6,72,128]{3,2,1,0:T(8,128)S(1)}, f32[8,128]{1,0:T(8,128)S(1)}) custom-call(s32[4]{0:T(128)S(1)} %copy-done.8, s32[4]{0:T(128)S(1)} %copy-done.9, s32[144,144]{1,0:T(8,128)S(1)} %reshape.27.idx_ref, bf16[6,2,3312]{2,1,0:T(2,128)(2,1)S(1)} %bitcast.19), custom_call_target="tpu_custom_call" | custom-call | flops 2000000000 | bytes 1051296 | tf_op jit(solution)/shard_map/pallas_call | solution.py:396
  19.4 0.0 copy-done.2
  19.4 0.0 copy-done.3
  19.4 0.0 copy-done.5
  19.4 0.0 copy-done.6
  19.4 0.5 shard_map.156
  19.9 0.0 collective-permute-done.1.low_ref
  19.9 0.0 collective-permute-done.2.corner_ref
  20.0 0.0 collective-permute-done.side_ref
  20.0 6.5 %shard_map.157 = (bf16[112,384]{1,0:T(8,128)(2,1)S(1)}, bf16[48,384]{1,0:T(8,128)(2,1)S(1)}, bf16[160,384]{1,0:T(8,128)(2,1)S(1)}, bf16[1728,128]{1,0:T(8,128)(2,1)S(1)}, bf16[1728,128]{1,0:T(8,128)(2,1)S(1)}) custom-call(bf16[112,384]{1,0:T(8,128)(2,1)S(1)} %get-tuple-element.33.own_ref, bf16[112,384]{1,0:T(8,128)(2,1)S(1)} %collective-permute-done.side_ref, ...), custom_call_target="tpu_custom_call" | custom-call | flops 2000000000 | bytes 3145728 | tf_op jit(solution)/shard_map/pallas_call | solution.py:396
  26.4 5.7 %collective-permute-start.4 = (bf16[1728,128]{1,0:T(8,128)(2,1)S(1)}, bf16[1728,128]{1,0:T(8,128)(2,1)S(1)}, u32[]{:S(2)}, u32[]{:S(2)}) collective-permute-start(bf16[1728,128]{1,0:T(8,128)(2,1)S(1)} %get-tuple-element.46), channel_id=1, source_target_pairs={{0,16},{16,0},{1,17},{17,1},{2,18},{18,2},{3,19},{19,3},{4,20},{20... | collective-permute-start | bytes 1327112 | tf_op jit(solution)/shard_map/ppermute | solution.py:429
  32.1 1.4 %collective-permute-done.4.two_ref = bf16[1728,128]{1,0:T(8,128)(2,1)S(1)} collective-permute-done((bf16[1728,128]{1,0:T(8,128)(2,1)S(1)}, bf16[1728,128]{1,0:T(8,128)(2,1)S(1)}, u32[]{:S(2)}, u32[]{:S(2)}) %collective-permute-start.4) | collective-permute-done | bytes 442400 | tf_op jit(solution)/shard_map/ppermute | solution.py:429
  33.5 0.9 shard_map.158
  34.4 3.5 %all-to-all-start = ((bf16[4,432,128]{2,1,0:T(8,128)(2,1)}), bf16[4,432,128]{2,1,0:T(8,128)(2,1)S(1)}, u32[]{:S(2)}, u32[]{:S(2)}) async-start(bf16[4,432,128]{2,1,0:T(8,128)(2,1)} %shard_map.158), calls=%async_computation | async-start | bytes 884736 | tf_op jit(solution)/shard_map/all_to_all | solution.py:425
  37.9 2.3 %collective-permute-start.3 = (bf16[160,384]{1,0:T(8,128)(2,1)S(1)}, bf16[160,384]{1,0:T(8,128)(2,1)S(1)}, u32[]{:S(2)}, u32[]{:S(2)}) collective-permute-start(bf16[160,384]{1,0:T(8,128)(2,1)S(1)} %get-tuple-element.44), channel_id=1, source_target_pairs={{0,496},{16,0},{32,16},{48,32},{64,48},{80,64},{96,80},{112,96},{1... | collective-permute-start | bytes 368648 | tf_op jit(solution)/shard_map/ppermute | solution.py:421
  40.1 7.9 %collective-permute-done.3.side_ref = bf16[160,384]{1,0:T(8,128)(2,1)S(1)} collective-permute-done((bf16[160,384]{1,0:T(8,128)(2,1)S(1)}, bf16[160,384]{1,0:T(8,128)(2,1)S(1)}, u32[]{:S(2)}, u32[]{:S(2)}) %collective-permute-start.3) | collective-permute-done | bytes 122912 | tf_op jit(solution)/shard_map/ppermute | solution.py:421
  48.0 0.0 all-to-all-done.parts_ref
  48.0 0.1 shard_map.159
  48.1 24.0 %all_to_all.20.parts_ref = bf16[64,8,128]{2,1,0:T(8,128)(2,1)S(1)} all-to-all(bf16[64,8,128]{2,1,0:T(8,128)(2,1)S(1)} %bitcast.17), channel_id=1, replica_groups=mesh['z'=8,'xh'=2,'c'=2,'y'=8,'xl'=2] {'y','z'}, dimensions={0} | all-to-all | bytes 262144 | tf_op jit(solution)/shard_map/all_to_all | solution.py:425
  72.1 0.1 shard_map.160
  72.1 15.4 %all_to_all.21 = bf16[64,8,128]{2,1,0:T(8,128)(2,1)S(1)} all-to-all(bf16[64,8,128]{2,1,0:T(8,128)(2,1)S(1)} %shard_map.160), channel_id=1, replica_groups=mesh['z'=8,'xh'=2,'c'=2,'y'=8,'xl'=2] {'y','z'}, dimensions={0} | all-to-all | bytes 262144 | tf_op jit(solution)/shard_map/all_to_all | solution.py:425
  87.5 0.8 shard_map.161
  88.4 4.0 %all-to-all-start.3 = ((bf16[4,432,128]{2,1,0:T(8,128)(2,1)}), bf16[4,432,128]{2,1,0:T(8,128)(2,1)S(1)}, u32[]{:S(2)}, u32[]{:S(2)}) async-start(bf16[4,432,128]{2,1,0:T(8,128)(2,1)} %shard_map.161), calls=%async_computation.3 | async-start | bytes 884736 | tf_op jit(solution)/shard_map/all_to_all | solution.py:425
  92.3 1.3 %collective-permute-start.5 = (bf16[96,384]{1,0:T(8,128)(2,1)S(1)}, bf16[96,384]{1,0:T(8,128)(2,1)S(1)}, u32[]{:S(2)}, u32[]{:S(2)}) collective-permute-start(bf16[96,384]{1,0:T(8,128)(2,1)S(1)} %get-tuple-element.51), channel_id=1, source_target_pairs={{1,0},{2,1},{3,2},{4,3},{5,4},{6,5},{7,6},{8,7},{9,8},{10,9},{11,1... | collective-permute-start | bytes 221192 | tf_op jit(solution)/shard_map/ppermute | solution.py:420
  93.6 5.7 %collective-permute-done.5.edge_ref = bf16[96,384]{1,0:T(8,128)(2,1)S(1)} collective-permute-done((bf16[96,384]{1,0:T(8,128)(2,1)S(1)}, bf16[96,384]{1,0:T(8,128)(2,1)S(1)}, u32[]{:S(2)}, u32[]{:S(2)}) %collective-permute-start.5) | collective-permute-done | bytes 73760 | tf_op jit(solution)/shard_map/ppermute | solution.py:420
  99.4 0.0 all-to-all-done.3
  99.4 5.2 %collective-permute-start.6 = (bf16[1728,128]{1,0:T(8,128)(2,1)S(1)}, bf16[1728,128]{1,0:T(8,128)(2,1)S(1)}, u32[]{:S(2)}, u32[]{:S(2)}) collective-permute-start(bf16[1728,128]{1,0:T(8,128)(2,1)S(1)} %bitcast.12), channel_id=1, source_target_pairs={{0,16},{16,0},{1,17},{17,1},{2,18},{18,2},{3,19},{19,3},{4,20},{20... | collective-permute-start | bytes 1327112 | tf_op jit(solution)/shard_map/ppermute | solution.py:429
  104.6 0.0 copy-done.4
  104.6 1.7 %shard_map.162 = (bf16[6,6,2,384]{3,2,1,0:T(2,128)(2,1)}, bf16[12,12,2,192]{3,2,1,0:T(2,128)(2,1)}) custom-call(bf16[112,384]{1,0:T(8,128)(2,1)S(1)} %get-tuple-element.43.own_ref, bf16[160,384]{1,0:T(8,128)(2,1)S(1)} %collective-permute-done.3.side_ref, bf16[96,384]{1,0:T(8,128)(2,1)S(1)} %collective-permute-done.5.edge_ref, bf16[768,384]{1,0:T(8,128)(2,1)S(1)} %copy-done.4), custom_call_target="tpu_custom_call" | custom-call | flops 400000000 | bytes 1038336 | tf_op jit(solution)/shard_map/pallas_call | solution.py:396
  106.3 0.0 collective-permute-done.6.other_ref
  106.3 1.1 %shard_map.163 = (bf16[192,576]{1,0:T(8,128)(2,1)}, bf16[192,192]{1,0:T(8,128)(2,1)}, bf16[192,768]{1,0:T(8,128)(2,1)}, bf16[192,768]{1,0:T(8,128)(2,1)}) custom-call(bf16[1728,128]{1,0:T(8,128)(2,1)S(1)} %bitcast.13, bf16[1728,128]{1,0:T(8,128)(2,1)S(1)} %collective-permute-done.6.other_ref), custom_call_target="tpu_custom_call" | custom-call | bytes 1769472 | tf_op jit(solution)/shard_map/pallas_call | solution.py:396
  (5 shorter events, 0.0 us)
Async XLA Ops:
  0.6 0.9 copy-start
  1.5 0.9 copy-start.1
  2.5 12.7 %copy-start.10 = (s32[20736]{0:T(1024)S(1)}, s32[20736]{0:T(1024)}, u32[]{:S(2)}) copy-start(s32[20736]{0:T(1024)} %param.20) | copy-start | bytes 248836
  2.9 17.0 %collective-permute-start.1 = (bf16[48,384]{1,0:T(8,128)(2,1)S(1)}, bf16[48,384]{1,0:T(8,128)(2,1)S(1)}, u32[]{:S(2)}, u32[]{:S(2)}) collective-permute-start(bf16[48,384]{1,0:T(8,128)(2,1)S(1)} %get-tuple-element.35), channel_id=1, source_target_pairs={{0,1},{1,2},{2,3},{3,4},{4,5},{5,6},{6,7},{7,8},{8,9},{9,10},{10,1... | collective-permute-start | bytes 110600 | tf_op jit(solution)/shard_map/ppermute | solution.py:420
  6.9 13.1 %collective-permute-start.2 = (bf16[48,384]{1,0:T(8,128)(2,1)S(1)}, bf16[48,384]{1,0:T(8,128)(2,1)S(1)}, u32[]{:S(2)}, u32[]{:S(2)}) collective-permute-start(bf16[48,384]{1,0:T(8,128)(2,1)S(1)} %get-tuple-element.36), channel_id=1, source_target_pairs={{0,17},{1,18},{2,19},{3,20},{4,21},{5,22},{6,23},{7,24},{8,25},{9,... | collective-permute-start | bytes 110600 | tf_op jit(solution)/shard_map/ppermute | solution.py:417
  12.5 2.8 %copy-start.7 = (bf16[2,1,6,3312]{3,0,2,1:T(2,128)(2,1)S(1)}, bf16[2,1,6,3312]{3,0,2,1:T(2,128)(2,1)}, u32[]{:S(2)}) copy-start(bf16[2,1,6,3312]{3,0,2,1:T(2,128)(2,1)} %param.19) | copy-start | bytes 238468
  12.5 7.5 %collective-permute-start = (bf16[112,384]{1,0:T(8,128)(2,1)S(1)}, bf16[112,384]{1,0:T(8,128)(2,1)S(1)}, u32[]{:S(2)}, u32[]{:S(2)}) collective-permute-start(bf16[112,384]{1,0:T(8,128)(2,1)S(1)} %get-tuple-element.34), channel_id=1, source_target_pairs={{0,16},{16,32},{32,48},{48,64},{64,80},{80,96},{96,112},{112,128},... | collective-permute-start | bytes 258056 | tf_op jit(solution)/shard_map/ppermute | solution.py:421
  15.3 0.7 copy-start.8
  15.3 0.7 copy-start.9
  16.0 3.4 %copy-start.2 = (s32[192,768]{1,0:T(8,128)S(1)}, s32[192,768]{1,0:T(8,128)}, u32[]{:S(2)}) copy-start(s32[192,768]{1,0:T(8,128)} %cu_ref.1) | copy-start | bytes 1769476
  16.0 3.4 %copy-start.3 = (s32[768,192]{0,1:T(8,128)S(1)}, s32[768,192]{0,1:T(8,128)}, u32[]{:S(2)}) copy-start(s32[768,192]{0,1:T(8,128)} %param.16) | copy-start | bytes 1769476
  16.0 3.4 %copy-start.5 = (s32[192,576]{1,0:T(8,128)S(1)}, s32[192,576]{1,0:T(8,128)}, u32[]{:S(2)}) copy-start(s32[192,576]{1,0:T(8,128)} %cq_ref.1) | copy-start | bytes 1327108
  16.0 3.4 %copy-start.6 = (s32[192,192]{1,0:T(8,128)S(1)}, s32[192,192]{1,0:T(8,128)}, u32[]{:S(2)}) copy-start(s32[192,192]{1,0:T(8,128)} %cp_ref.1) | copy-start | bytes 442372
  26.4 7.1 %collective-permute-start.4 = (bf16[1728,128]{1,0:T(8,128)(2,1)S(1)}, bf16[1728,128]{1,0:T(8,128)(2,1)S(1)}, u32[]{:S(2)}, u32[]{:S(2)}) collective-permute-start(bf16[1728,128]{1,0:T(8,128)(2,1)S(1)} %get-tuple-element.46), channel_id=1, source_target_pairs={{0,16},{16,0},{1,17},{17,1},{2,18},{18,2},{3,19},{19,3},{4,20},{20... | collective-permute-start | bytes 1327112 | tf_op jit(solution)/shard_map/ppermute | solution.py:429
  34.4 13.6 %all-to-all-start = ((bf16[4,432,128]{2,1,0:T(8,128)(2,1)}), bf16[4,432,128]{2,1,0:T(8,128)(2,1)S(1)}, u32[]{:S(2)}, u32[]{:S(2)}) async-start(bf16[4,432,128]{2,1,0:T(8,128)(2,1)} %shard_map.158), calls=%async_computation | async-start | bytes 884736 | tf_op jit(solution)/shard_map/all_to_all | solution.py:425
  37.9 10.1 %collective-permute-start.3 = (bf16[160,384]{1,0:T(8,128)(2,1)S(1)}, bf16[160,384]{1,0:T(8,128)(2,1)S(1)}, u32[]{:S(2)}, u32[]{:S(2)}) collective-permute-start(bf16[160,384]{1,0:T(8,128)(2,1)S(1)} %get-tuple-element.44), channel_id=1, source_target_pairs={{0,496},{16,0},{32,16},{48,32},{64,48},{80,64},{96,80},{112,96},{1... | collective-permute-start | bytes 368648 | tf_op jit(solution)/shard_map/ppermute | solution.py:421
  87.5 17.1 %copy-start.4 = (bf16[768,384]{1,0:T(8,128)(2,1)S(1)}, bf16[768,384]{1,0:T(8,128)(2,1)}, u32[]{:S(2)}) copy-start(bf16[768,384]{1,0:T(8,128)(2,1)} %weight_ref.1) | copy-start | bytes 1769476
  88.4 11.0 %all-to-all-start.3 = ((bf16[4,432,128]{2,1,0:T(8,128)(2,1)}), bf16[4,432,128]{2,1,0:T(8,128)(2,1)S(1)}, u32[]{:S(2)}, u32[]{:S(2)}) async-start(bf16[4,432,128]{2,1,0:T(8,128)(2,1)} %shard_map.161), calls=%async_computation.3 | async-start | bytes 884736 | tf_op jit(solution)/shard_map/all_to_all | solution.py:425
  92.3 7.0 %collective-permute-start.5 = (bf16[96,384]{1,0:T(8,128)(2,1)S(1)}, bf16[96,384]{1,0:T(8,128)(2,1)S(1)}, u32[]{:S(2)}, u32[]{:S(2)}) collective-permute-start(bf16[96,384]{1,0:T(8,128)(2,1)S(1)} %get-tuple-element.51), channel_id=1, source_target_pairs={{1,0},{2,1},{3,2},{4,3},{5,4},{6,5},{7,6},{8,7},{9,8},{10,9},{11,1... | collective-permute-start | bytes 221192 | tf_op jit(solution)/shard_map/ppermute | solution.py:420
  99.4 6.9 %collective-permute-start.6 = (bf16[1728,128]{1,0:T(8,128)(2,1)S(1)}, bf16[1728,128]{1,0:T(8,128)(2,1)S(1)}, u32[]{:S(2)}, u32[]{:S(2)}) collective-permute-start(bf16[1728,128]{1,0:T(8,128)(2,1)S(1)} %bitcast.12), channel_id=1, source_target_pairs={{0,16},{16,0},{1,17},{17,1},{2,18},{18,2},{3,19},{19,3},{4,20},{20... | collective-permute-start | bytes 1327112 | tf_op jit(solution)/shard_map/ppermute | solution.py:429
